TPU v7x, 256 devices: a whole 4x4x8 slice. The times are simulated.
256 devices in a mesh: blk: 16 (over x, y_lo, core), uly: 16 (over z, y_hi).
Axes of the slice: x: 4, y: 4 (y_hi: 2, y_lo: 2; y = y_hi * 2 + y_lo), z: 8, core: 2. Of those that a mesh axis runs over, the one named last changes fastest.
Arguments:
- queries: bfloat16 [32768, 4096], P(('blk', 'uly')), may hold values from -128 to 128
- keys: bfloat16 [32768, 1024], P(('blk', 'uly')), may hold values from -7 to 7
- values: bfloat16 [32768, 1024], P(('blk', 'uly')), may hold values from -6 to 6
- doc_ids: int32 [32768], P(('blk', 'uly')), may hold values from 0 to 63, never falling along the last dimension, each value on 1 to 2048 neighbouring positions
- out_weight: bfloat16 [4096, 4096], P('uly'), may hold values from -0.09375 to 0.09375
Outputs:
- mixed: bfloat16 [32768, 4096], P(('blk', 'uly'))
Inputs may be any that keep to these rules, and one draw needn't show every extreme that they name: `doc_ids`: document numbers never fall along the pack; each document holds 1 to 2048 consecutive tokens, and some document holds exactly 2048.
All inputs are finite; a program needn't handle non-finite values.
Results may differ from a plain program's by a relative error of at most 0.017.
Values may be sent and summed in bfloat16 or wider, within the bound.
No kernel may reach another device: no remote copies, remote signals or barrier semaphores. Data moves between devices by JAX's collectives and lax.ppermute only.
A program may use at most 64 MiB of HBM per device.

v0:
```python
import math

import jax
import jax.numpy as jnp
from jax import lax
from jax.sharding import Mesh
from jax.sharding import PartitionSpec as P

HEAD_DIM = 128
ULY = ("uly_0", "uly_1")
BLK_ULY = ("blk", "uly_0", "uly_1")


def in_order(blocks, dim):
    dims = list(blocks.shape[1:])
    dims[dim] *= blocks.shape[0]
    return jnp.moveaxis(blocks, 0, dim).reshape(dims)


def sent_to_all(shard, axis):
    size = lax.axis_size(axis)
    return lax.all_to_all(
        jnp.broadcast_to(shard[None], (size, *shard.shape)), axis, 0, 0, tiled=True
    )


def gather_directly(shard, axis, dim):
    return in_order(sent_to_all(shard, axis), dim)


def in_one_piece(arrays, axis, split_dim, concat_dim, along):
    ends, at = ([], 0)
    for a in arrays[:-1]:
        at += a.shape[along]
        ends.append(at)
    both = jnp.concatenate(arrays, axis=along)
    return tuple(
        jnp.split(
            lax.all_to_all(both, axis, split_axis=split_dim, concat_axis=concat_dim, tiled=True),
            ends,
            axis=along,
        )
    )


def shifted(value, axis, steps):
    count = lax.axis_size(axis)
    first, last = (max(0, -steps), min(count, count - steps))
    return lax.ppermute(value, axis, [(source, source + steps) for source in range(first, last)])


def sum_by_axis(terms, axes):
    running = terms.astype(jnp.bfloat16)
    for axis in axes:
        running = lax.psum_scatter(running, axis, scatter_dimension=0, tiled=True)
    return running.astype(jnp.float32)


def body(queries, keys, values, doc_ids, out_weight):
    n_uly = lax.axis_size(ULY)
    blk_index = lax.axis_index("blk")
    rows = queries.shape[0]
    head_dim = HEAD_DIM
    heads = queries.shape[1] // head_dim
    kv_heads = keys.shape[1] // head_dim
    repeat = max(1, n_uly // kv_heads)
    kv_local = max(n_uly, kv_heads) // n_uly
    local_heads = heads // n_uly
    grouped = local_heads // kv_local
    block = rows * n_uly
    sub_rows = math.gcd(block, 512)
    n_sub = block // sub_rows
    scale = 1.0 / math.sqrt(head_dim)
    query_ids = gather_directly(doc_ids, ULY, 0)
    query_split = queries.reshape(rows, heads, head_dim)
    key_wide = jnp.repeat(keys.reshape(rows, kv_heads, head_dim), repeat, axis=1)
    value_wide = jnp.repeat(values.reshape(rows, kv_heads, head_dim), repeat, axis=1)
    key_wide, value_wide = (key_wide, value_wide)
    query_local, key_local, value_local = (
        lax.all_to_all(query_split, ULY, split_axis=1, concat_axis=0, tiled=True),
        *in_one_piece((key_wide, value_wide), ULY, 1, 0, 2),
    )
    carried = (key_local, value_local)
    query_grouped = query_local.reshape(n_sub, sub_rows, kv_local, grouped, head_dim)
    query_start = blk_index * block
    query_pos = query_start + jnp.arange(block, dtype=jnp.int32)
    first_id = query_ids[0]
    offsets = jnp.arange(block, dtype=jnp.int32)
    ids_sub = query_ids.reshape(n_sub, sub_rows)
    pos_sub = query_pos.reshape(n_sub, sub_rows)

    def attend(state, pair, key_ids, source):
        key_block, value_block = pair
        key_start = jnp.maximum(source, 0) * block
        key_pos = key_start + offsets
        needed = (source >= 0) & (
            (source == blk_index) | (source < blk_index) & (key_ids[block - 1] == first_id)
        )

        def compute(state_in):

            def one(item):
                query_part, pos_part, ids_part, accum, peak, total = item
                scores = (
                    jnp.einsum(
                        "qkgd,pkd->kgqp", query_part, key_block, preferred_element_type=jnp.float32
                    )
                    * scale
                )
                allowed = (key_pos[None, :] <= pos_part[:, None]) & (
                    key_ids[None, :] == ids_part[:, None]
                )
                scores = jnp.where(allowed, scores, -1e30)
                peak_new = jnp.maximum(peak, jnp.max(scores, axis=-1))
                expo = jnp.where(allowed, jnp.exp(scores - peak_new[..., None]), 0.0)
                factor = jnp.exp(peak - peak_new)
                total_new = total * factor + jnp.sum(expo, axis=-1)
                update = jnp.einsum(
                    "kgqp,pkd->kgqd",
                    expo.astype(jnp.bfloat16),
                    value_block,
                    preferred_element_type=jnp.float32,
                )
                return (accum * factor[..., None] + update, peak_new, total_new)

            return lax.map(
                one, (query_grouped, pos_sub, ids_sub, state_in[0], state_in[1], state_in[2])
            )

        def keep(state_in):
            return state_in

        return lax.cond(needed, compute, keep, state)

    start_state = (
        jnp.zeros((n_sub, kv_local, grouped, sub_rows, head_dim), jnp.float32),
        jnp.full((n_sub, kv_local, grouped, sub_rows), -1e30, jnp.float32),
        jnp.zeros((n_sub, kv_local, grouped, sub_rows), jnp.float32),
    )
    state = attend(start_state, carried, query_ids, blk_index)
    earlier_key, earlier_value, earlier_marks = shifted(
        (carried[0], carried[1], query_ids.astype(jnp.bfloat16)), "blk", 1
    )
    earlier_ids = earlier_marks.astype(jnp.int32)
    state = attend(state, (earlier_key, earlier_value), earlier_ids, blk_index - 1)
    accum, peak, total = state
    attn = (
        (accum / total[..., None])
        .transpose(0, 3, 1, 2, 4)
        .reshape(block, local_heads * head_dim)
        .astype(jnp.bfloat16)
    )
    mixed = sum_by_axis(jnp.dot(attn, out_weight, preferred_element_type=jnp.float32), ULY)
    return mixed.astype(jnp.bfloat16)


def solution(mesh):
    torus = Mesh(mesh.devices.reshape(mesh.shape["blk"], 8, 2), ("blk", "uly_0", "uly_1"))
    in_specs = (P(BLK_ULY, None), P(BLK_ULY, None), P(BLK_ULY, None), P(BLK_ULY), P(ULY, None))
    out_specs = P(BLK_ULY, None)
    return jax.shard_map(body, mesh=torus, in_specs=in_specs, out_specs=out_specs, check_vma=False)
```

profile of v0, /device:TPU:1, one launch (start us, length us, event | category | flops | bytes accessed | tf_op | source)
XLA Modules:
  0.0 437.3 jit_solution(12410283171894998707)
XLA Ops:
  6.5 1.4 broadcast_in_dim.61
  7.9 11.7 %all-to-all-start = ((s32[16,1,128]{2,1,0:T(1,128)}), s32[16,1,128]{2,1,0:T(1,128)S(1)}, u32[]{:S(2)}, u32[]{:S(2)}) async-start(s32[16,1,128]{2,1,0:T(1,128)} %broadcast_in_dim.61), calls=%async_computation | async-start | bytes 16384 | tf_op jit(solution)/shard_map/all_to_all | solution.py:22
  19.7 1.0 copy_bitcast_fusion.1
  20.7 1.0 copy_bitcast_fusion
  21.9 1.1 pad_maximum_fusion
  23.0 5.5 %all-to-all-done = s32[16,1,128]{2,1,0:T(1,128)S(1)} async-done(((s32[16,1,128]{2,1,0:T(1,128)}), s32[16,1,128]{2,1,0:T(1,128)S(1)}, u32[]{:S(2)}, u32[]{:S(2)}) %all-to-all-start) | async-done | bytes 8224 | tf_op jit(solution)/shard_map/all_to_all | solution.py:22
  28.5 3.7 all-to-all-start.2
  32.1 2.3 copy.27
  34.4 23.6 %all-to-all-done.2 = bf16[128,16,256]{2,0,1:T(8,128)(2,1)S(1)} async-done(((bf16[128,16,256]{2,0,1:T(8,128)(2,1)}), bf16[128,16,256]{2,0,1:T(8,128)(2,1)S(1)}, u32[]{:S(2)}, u32[]{:S(2)}) %all-to-all-start.2) | async-done | bytes 1048608 | tf_op jit(solution)/shard_map/all_to_all | solution.py:39
  58.0 1.0 copy-done.1
  59.0 7.3 %all-to-all-start.1 = ((bf16[128,32,128]{0,2,1:T(8,128)(2,1)}), bf16[128,32,128]{0,2,1:T(8,128)(2,1)S(1)}, u32[]{:S(2)}, u32[]{:S(2)}) async-start(bf16[128,32,128]{0,2,1:T(8,128)(2,1)} %bitcast.35), calls=%async_computation.1 | async-start | bytes 2097152 | tf_op jit(solution)/shard_map/all_to_all | solution.py:80
  66.3 2.3 fusion.61
  68.6 3.0 collective-permute-start.2
  71.6 1.9 collective-permute-start.1
  73.5 4.3 collective-permute-start
  79.6 13.8 %collective-permute-done = bf16[2048]{0:T(1024)(128)(2,1)S(1)} collective-permute-done((bf16[2048]{0:T(1024)(128)(2,1)S(1)}, bf16[2048]{0:T(1024)(128)(2,1)S(1)}, u32[]{:S(2)}, u32[]{:S(2)}) %collective-permute-start) | collective-permute-done | bytes 4128 | tf_op jit(solution)/shard_map/ppermute | solution.py:49
  95.3 1.3 copy.29
  96.6 49.1 %conditional.2 = (f32[4,1,2,512,128]{4,3,2,1,0:T(8,128)}, f32[4,1,2,512]{3,2,1,0:T(2,128)}, f32[4,1,2,512]{3,2,1,0:T(2,128)}) conditional(s32[]{:T(128)} %convert_element_type.35, () %tuple.28, (s32[]{:T(128)}, s32[2048]{0:T(1024)S(1)}, s32[16,1,128]{2,1,0:T(1,128)S(1)}, s32[4,512]{1,0:T(4,128)S(1)}, s32[4,512]{1,0:T(4,128)S(1)}, ...), branch_computations={%region_0.0_spmd, %region_1.6_spmd} | conditional | flops 1104288768 | bytes 31289640 | solution.py:133
  96.7 49.1 %while.24 = (s32[]{:T(128)}, f32[4,1,2,512,128]{4,3,2,1,0:T(8,128)}, f32[4,1,2,512]{3,2,1,0:T(2,128)}, f32[4,1,2,512]{3,2,1,0:T(2,128)}, s32[2048]{0:T(1024)S(1)...) while((s32[]{:T(128)}, ...), condition=%wide.region_5.5_spmd, body=%wide.region_2.4_spmd.sunk | while | flops 1104286720 | bytes 31273100 | solution.py:126
  96.7 0.9 compare_and_fusion.5
  97.6 3.2 fusion.87
  100.8 2.9 fusion.89
  103.7 4.7 %fusion.88 = f32[4,1,2,512,128]{4,3,2,1,0:T(8,128)} fusion(f32[4,1,2,512,128]{4,3,2,1,0:T(8,128)} %get-tuple-element.585, s32[]{:T(128)S(6)} %copy.66, f32[512,2,2048]{2,0,1:T(8,128)S(1)} %get-tuple-element.524, f32[2,512]{1,0:T(2,128)S(1)} %get-tuple-element.526, pred[512,2048]{1,0:T(8,128)(4,1)S(1)} %compare_and_fusion.5, ...), kind=kOutput, calls=%fused_computation.11.clone.1 | convolution fusion | flops 547487744 | bytes 10493956 | tf_op jit(solution)/shard_map/cond/branch_1_fun/while/body/eval_jaxpr/kgqp,pkd->kgqd/dot_general | solution.py:118
  109.0 0.9 compare_and_fusion.5
  109.9 3.2 fusion.87
  113.0 2.9 fusion.89
  115.9 4.7 %fusion.88 = f32[4,1,2,512,128]{4,3,2,1,0:T(8,128)} fusion(f32[4,1,2,512,128]{4,3,2,1,0:T(8,128)} %get-tuple-element.585, s32[]{:T(128)S(6)} %copy.66, f32[512,2,2048]{2,0,1:T(8,128)S(1)} %get-tuple-element.524, f32[2,512]{1,0:T(2,128)S(1)} %get-tuple-element.526, pred[512,2048]{1,0:T(8,128)(4,1)S(1)} %compare_and_fusion.5, ...), kind=kOutput, calls=%fused_computation.11.clone.1 | convolution fusion | flops 547487744 | bytes 10493956 | tf_op jit(solution)/shard_map/cond/branch_1_fun/while/body/eval_jaxpr/kgqp,pkd->kgqd/dot_general | solution.py:118
  121.2 0.9 compare_and_fusion.5
  122.1 3.1 fusion.87
  125.3 2.9 fusion.89
  128.2 4.7 %fusion.88 = f32[4,1,2,512,128]{4,3,2,1,0:T(8,128)} fusion(f32[4,1,2,512,128]{4,3,2,1,0:T(8,128)} %get-tuple-element.585, s32[]{:T(128)S(6)} %copy.66, f32[512,2,2048]{2,0,1:T(8,128)S(1)} %get-tuple-element.524, f32[2,512]{1,0:T(2,128)S(1)} %get-tuple-element.526, pred[512,2048]{1,0:T(8,128)(4,1)S(1)} %compare_and_fusion.5, ...), kind=kOutput, calls=%fused_computation.11.clone.1 | convolution fusion | flops 547487744 | bytes 10493956 | tf_op jit(solution)/shard_map/cond/branch_1_fun/while/body/eval_jaxpr/kgqp,pkd->kgqd/dot_general | solution.py:118
  133.5 0.9 compare_and_fusion.5
  134.4 3.2 fusion.87
  137.6 2.9 fusion.89
  140.5 4.7 %fusion.88 = f32[4,1,2,512,128]{4,3,2,1,0:T(8,128)} fusion(f32[4,1,2,512,128]{4,3,2,1,0:T(8,128)} %get-tuple-element.585, s32[]{:T(128)S(6)} %copy.66, f32[512,2,2048]{2,0,1:T(8,128)S(1)} %get-tuple-element.524, f32[2,512]{1,0:T(2,128)S(1)} %get-tuple-element.526, pred[512,2048]{1,0:T(8,128)(4,1)S(1)} %compare_and_fusion.5, ...), kind=kOutput, calls=%fused_computation.11.clone.1 | convolution fusion | flops 547487744 | bytes 10493956 | tf_op jit(solution)/shard_map/cond/branch_1_fun/while/body/eval_jaxpr/kgqp,pkd->kgqd/dot_general | solution.py:118
  145.8 56.5 %conditional.3 = ((f32[4,1,2,512,128]{4,3,2,1,0:T(8,128)}, f32[4,1,2,512]{3,2,1,0:T(2,128)})) conditional(s32[]{:T(128)} %convert_element_type.34, (f32[4,1,2,512,128]{4,3,2,1,0:T(8,128)}, f32[4,1,2,512]{3,2,1,0:T(2,128)}) %tuple.30, (s32[]{:T(128)}, s32[2048]{0:T(1024)S(1)}, f32[4,1,2,512,128]{4,3,2,1,0:T(8,128)}, f32[4,1,2,512]{3,2,1,0:T(2,128)}, ...), branch_computations={%region_6.7_spmd, %region_7.12_spmd} | conditional | flops 1104418816 | bytes 36049228 | solution.py:133
  146.0 52.6 %while.25 = (s32[]{:T(128)}, f32[4,1,2,512,128]{4,3,2,1,0:T(8,128)}, f32[4,1,2,512]{3,2,1,0:T(2,128)S(1)}, f32[4,1,2,512,128]{4,3,2,1,0:T(8,128)}, f32[4,1,2,512...) while((s32[]{:T(128)}, ...), condition=%wide.region_11.11_spmd, body=%wide.region_8.10_spmd.sunk | while | flops 1104416768 | bytes 31805600 | solution.py:126
  146.0 0.9 compare_and_fusion.4
  147.0 3.1 fusion.80
  150.1 0.7 fusion.81
  150.8 2.9 fusion.83
  153.7 4.8 %fusion.82 = f32[4,1,2,512,128]{4,3,2,1,0:T(8,128)} fusion(f32[4,1,2,512,128]{4,3,2,1,0:T(8,128)} %get-tuple-element.545, s32[]{:T(128)S(6)} %copy.53, f32[512,2,2048]{2,0,1:T(8,128)S(1)} %get-tuple-element.507, f32[2,512]{1,0:T(2,128)S(1)} %get-tuple-element.509, pred[512,2048]{1,0:T(8,128)(4,1)S(1)} %compare_and_fusion.4, ...), kind=kOutput, calls=%fused_computation.43.clone.1 | convolution fusion | flops 547618816 | bytes 11018244 | tf_op jit(solution)/shard_map/cond/branch_1_fun/while/body/eval_jaxpr/kgqp,pkd->kgqd/dot_general | solution.py:118
  158.5 0.7 fusion.84
  159.2 0.9 compare_and_fusion.4
  160.1 3.1 fusion.80
  164.0 2.9 fusion.83
  166.8 4.8 %fusion.82 = f32[4,1,2,512,128]{4,3,2,1,0:T(8,128)} fusion(f32[4,1,2,512,128]{4,3,2,1,0:T(8,128)} %get-tuple-element.545, s32[]{:T(128)S(6)} %copy.53, f32[512,2,2048]{2,0,1:T(8,128)S(1)} %get-tuple-element.507, f32[2,512]{1,0:T(2,128)S(1)} %get-tuple-element.509, pred[512,2048]{1,0:T(8,128)(4,1)S(1)} %compare_and_fusion.4, ...), kind=kOutput, calls=%fused_computation.43.clone.1 | convolution fusion | flops 547618816 | bytes 11018244 | tf_op jit(solution)/shard_map/cond/branch_1_fun/while/body/eval_jaxpr/kgqp,pkd->kgqd/dot_general | solution.py:118
  171.6 0.7 fusion.84
  172.3 0.9 compare_and_fusion.4
  173.3 3.2 fusion.80
  177.1 2.9 fusion.83
  180.0 4.8 %fusion.82 = f32[4,1,2,512,128]{4,3,2,1,0:T(8,128)} fusion(f32[4,1,2,512,128]{4,3,2,1,0:T(8,128)} %get-tuple-element.545, s32[]{:T(128)S(6)} %copy.53, f32[512,2,2048]{2,0,1:T(8,128)S(1)} %get-tuple-element.507, f32[2,512]{1,0:T(2,128)S(1)} %get-tuple-element.509, pred[512,2048]{1,0:T(8,128)(4,1)S(1)} %compare_and_fusion.4, ...), kind=kOutput, calls=%fused_computation.43.clone.1 | convolution fusion | flops 547618816 | bytes 11018244 | tf_op jit(solution)/shard_map/cond/branch_1_fun/while/body/eval_jaxpr/kgqp,pkd->kgqd/dot_general | solution.py:118
  184.8 0.7 fusion.84
  185.5 0.9 compare_and_fusion.4
  186.4 3.1 fusion.80
  190.3 2.9 fusion.83
  193.2 4.8 %fusion.82 = f32[4,1,2,512,128]{4,3,2,1,0:T(8,128)} fusion(f32[4,1,2,512,128]{4,3,2,1,0:T(8,128)} %get-tuple-element.545, s32[]{:T(128)S(6)} %copy.53, f32[512,2,2048]{2,0,1:T(8,128)S(1)} %get-tuple-element.507, f32[2,512]{1,0:T(2,128)S(1)} %get-tuple-element.509, pred[512,2048]{1,0:T(8,128)(4,1)S(1)} %compare_and_fusion.4, ...), kind=kOutput, calls=%fused_computation.43.clone.1 | convolution fusion | flops 547618816 | bytes 11018244 | tf_op jit(solution)/shard_map/cond/branch_1_fun/while/body/eval_jaxpr/kgqp,pkd->kgqd/dot_general | solution.py:118
  197.9 0.7 fusion.84
  199.2 3.1 copy.82
  202.3 2.0 fusion.60
  204.3 1.1 copy.35
  205.4 8.1 %convolution_convert_fusion = bf16[2048,4096]{1,0:T(8,128)(2,1)} fusion(bf16[256,4096]{1,0:T(8,128)(2,1)S(1)} %copy-done, bf16[256,8,2,128]{3,2,1,0:T(2,128)(2,1)S(1)} %bitcast.228), kind=kOutput, calls=%fused_computation.66 | convolution fusion | flops 4303355904 | bytes 19922944 | tf_op jit(solution)/shard_map/dot_general | solution.py:153
  213.5 177.3 %reduce-scatter.3.cloned.1.call-done = bf16[256,4096]{1,0:T(8,128)(2,1)} async-done(((bf16[2048,4096]{1,0:T(8,128)(2,1)}), bf16[256,4096]{1,0:T(8,128)(2,1)}) %reduce-scatter.3.cloned.1.call-update) | async-done | bytes 2097168 | tf_op jit(solution)/shard_map/reduce_scatter | solution.py:55
  390.9 39.5 %reduce-scatter.5.cloned.1.call-done = bf16[128,4096]{1,0:T(8,128)(2,1)} async-done(((bf16[256,4096]{1,0:T(8,128)(2,1)}), bf16[128,4096]{1,0:T(8,128)(2,1)}) %reduce-scatter.5.cloned.1.call-update) | async-done | bytes 1048592 | tf_op jit(solution)/shard_map/reduce_scatter | solution.py:55
  (49 shorter events, 8.0 us)
Async XLA Ops:
  6.5 198.8 %copy-start = (bf16[256,4096]{1,0:T(8,128)(2,1)S(1)}, bf16[256,4096]{1,0:T(8,128)(2,1)}, u32[]{:S(2)}) copy-start(bf16[256,4096]{1,0:T(8,128)(2,1)} %param.17) | copy-start | bytes 6291460
  7.9 20.5 %all-to-all-start = ((s32[16,1,128]{2,1,0:T(1,128)}), s32[16,1,128]{2,1,0:T(1,128)S(1)}, u32[]{:S(2)}, u32[]{:S(2)}) async-start(s32[16,1,128]{2,1,0:T(1,128)} %broadcast_in_dim.61), calls=%async_computation | async-start | bytes 16384 | tf_op jit(solution)/shard_map/all_to_all | solution.py:22
  28.5 29.5 %all-to-all-start.2 = ((bf16[128,16,256]{2,0,1:T(8,128)(2,1)}), bf16[128,16,256]{2,0,1:T(8,128)(2,1)S(1)}, u32[]{:S(2)}, u32[]{:S(2)}) async-start(bf16[128,16,256]{2,0,1:T(8,128)(2,1)} %pad_maximum_fusion), calls=%async_computation.2 | async-start | bytes 2097152 | tf_op jit(solution)/shard_map/all_to_all | solution.py:39
  58.0 1.0 copy-start.1
  59.0 36.3 %all-to-all-start.1 = ((bf16[128,32,128]{0,2,1:T(8,128)(2,1)}), bf16[128,32,128]{0,2,1:T(8,128)(2,1)S(1)}, u32[]{:S(2)}, u32[]{:S(2)}) async-start(bf16[128,32,128]{0,2,1:T(8,128)(2,1)} %bitcast.35), calls=%async_computation.1 | async-start | bytes 2097152 | tf_op jit(solution)/shard_map/all_to_all | solution.py:80
  66.2 324.6 %reduce-scatter.3.cloned.1.call-start = ((), (), s32[]{:S(2)}) async-start(), calls=%async_computation.5 | async-start | bytes 18874368 | tf_op jit(solution)/shard_map/reduce_scatter | solution.py:55
  68.6 77.2 %collective-permute-start.2 = (bf16[2048,1,128]{2,0,1:T(8,128)(2,1)}, bf16[2048,1,128]{2,0,1:T(8,128)(2,1)}, u32[]{:S(2)}, u32[]{:S(2)}) collective-permute-start(bf16[2048,1,128]{2,0,1:T(8,128)(2,1)} %get-tuple-element.354), channel_id=1, source_target_pairs={{0,16},{16,32},{32,48},{48,64},{64,80},{80,96},{96,112},{112,128},... | collective-permute-start | bytes 1572872 | tf_op jit(solution)/shard_map/ppermute | solution.py:49
  71.6 74.2 %collective-permute-start.1 = (bf16[2048,1,128]{2,0,1:T(8,128)(2,1)}, bf16[2048,1,128]{2,0,1:T(8,128)(2,1)}, u32[]{:S(2)}, u32[]{:S(2)}) collective-permute-start(bf16[2048,1,128]{2,0,1:T(8,128)(2,1)} %get-tuple-element.355), channel_id=1, source_target_pairs={{0,16},{16,32},{32,48},{48,64},{64,80},{80,96},{96,112},{112,128},... | collective-permute-start | bytes 1572872 | tf_op jit(solution)/shard_map/ppermute | solution.py:49
  73.5 19.9 %collective-permute-start = (bf16[2048]{0:T(1024)(128)(2,1)S(1)}, bf16[2048]{0:T(1024)(128)(2,1)S(1)}, u32[]{:S(2)}, u32[]{:S(2)}) collective-permute-start(bf16[2048]{0:T(1024)(128)(2,1)S(1)} %convert_element_type.32), channel_id=1, source_target_pairs={{0,16},{16,32},{32,48},{48,64},{64,80},{80,96},{96,112},{112,128},... | collective-permute-start | bytes 12296 | tf_op jit(solution)/shard_map/ppermute | solution.py:49
  213.5 216.9 %reduce-scatter.5.cloned.1.call-start = ((), (), s32[]{:S(2)}) async-start(), calls=%async_computation.6 | async-start | bytes 3145728 | tf_op jit(solution)/shard_map/reduce_scatter | solution.py:55
Sparse Core Ops, SparseCore 0:
  213.6 177.1 reduce-scatter.2
  393.3 37.0 reduce-scatter.4
where the time goes:
time: 439 us; the launch traced here: 437 us
  waiting for transfers between devices  260 us (59%)
  matrix products  71.1 us (16%)
  other arithmetic  42.2 us (10%)
  starting transfers between devices  32 us (7%)
  local copies, waits for them, and re-layouts  17 us (4%)
  between operations  14.9 us (3%)
    reduce_scatter x2, waiting for transfers between devices, sum_by_axis(): running = lax.psum_scatter(running, axis, scatter_dimension=0, tiled=True)  217 us
    dot_general x8, matrix products, one(): jnp.einsum('kgqp,pkd->kgqd', expo.astype(jnp.bfloat16), value_block, pref...  37.8 us
    dot_general x8, matrix products, one(): jnp.einsum('qkgd,pkd->kgqp', query_part, key_block, preferred_element_typ...  25.2 us
    all_to_all x1, waiting for transfers between devices, in_one_piece(): lax.all_to_all(both, axis, split_axis=split_dim, concat_axis=concat_dim,...  23.6 us
    reduce_sum x8, other arithmetic, one(): total_new = total * factor + jnp.sum(expo, axis=-1)  23 us
    ppermute x3, waiting for transfers between devices, shifted(): lax.ppermute(value, axis, [(source, source + steps) for source in range(f...  13.8 us
    all_to_all x1, starting transfers between devices, sent_to_all(): lax.all_to_all(jnp.broadcast_to(shard[None], (size, *shard.shape)), axis,...  11.7 us
    ppermute x3, starting transfers between devices, shifted(): lax.ppermute(value, axis, [(source, source + steps) for source in range(f...  9.23 us
  transfers between devices with their start and end apart: 8, of which 5 were waited for; matrix products, arithmetic and copies ran while one was open for 14% of the time, Pallas kernels for 0%

commit v1 on v0

v1 whole, which is shorter than its diff:
```python
import functools
import math

import jax
import jax.numpy as jnp
from jax import lax
from jax.experimental import pallas as pl
from jax.experimental.pallas import tpu as pltpu
from jax.sharding import Mesh
from jax.sharding import PartitionSpec as P

HEAD_DIM = 128
ROWS = 128
Z = 8
GROUP = 4
PAIRS = 16
EXP2_SCALE = math.log2(math.e) / math.sqrt(HEAD_DIM)
MASKED = -1e30
VMEM_LIMIT = 48 * 1024 * 1024

AXES = ("x", "yl", "core", "zh", "zl", "yh")
BLK = ("x", "yl", "core")


def pack_kernel(k_ref, v_ref, id_ref, o_ref):
    ids = jnp.broadcast_to((id_ref[...] + 1).astype(jnp.float32), (16, ROWS)).astype(jnp.bfloat16)
    for g in range(Z):
        cols = slice(g * HEAD_DIM, (g + 1) * HEAD_DIM)
        o_ref[g, 0:ROWS, 0:HEAD_DIM] = k_ref[:, cols]
        o_ref[g, 0:ROWS, HEAD_DIM : 2 * HEAD_DIM] = v_ref[:, cols]
        o_ref[g, ROWS : ROWS + 16, 0:HEAD_DIM] = ids
        o_ref[g, ROWS : ROWS + 16, HEAD_DIM : 2 * HEAD_DIM] = ids


def attention_kernel(
    q_ref, own_ref, oth_ref, pown_ref, poth_ref, o_ref,
    k_buf, v_buf, ids_own, ids_oth, last_ref, lo_ref, s_ref, m_ref, acc_ref,
):
    odd = lax.axis_index("yh") == 1
    ones = jnp.ones((2 * ROWS, HEAD_DIM), jnp.bfloat16)
    for side, (a, b) in enumerate(((pown_ref, poth_ref), (own_ref, oth_ref))):
        for g in range(Z):
            p = side * Z + g
            for half, src in enumerate((a, b)):
                rows = slice(half * ROWS, (half + 1) * ROWS)
                k_buf[p, rows, :] = src[g, 0:ROWS, 0:HEAD_DIM]
                v_buf[p, rows, 0:HEAD_DIM] = src[g, 0:ROWS, HEAD_DIM : 2 * HEAD_DIM]
                ids = src[g, ROWS : ROWS + 16, 0:HEAD_DIM].astype(jnp.float32)[0:1, :]
                (ids_own if half == 0 else ids_oth)[p : p + 1, :] = ids
            v_buf[p, :, HEAD_DIM : 2 * HEAD_DIM] = ones
    last_ref[...] = jnp.broadcast_to(
        jnp.max(jnp.maximum(ids_own[...], ids_oth[...]), axis=1, keepdims=True), (PAIRS, ROWS)
    )
    for z in range(Z):
        first = jnp.min(ids_own[Z + z : Z + z + 1, :], axis=1, keepdims=True)
        before = jnp.where(last_ref[...] < first, 1.0 / ROWS, 0.0)
        lo_ref[z] = jnp.sum(before).astype(jnp.int32)

    def scores(q4, p):
        return lax.dot_general(
            q4, k_buf[p], (((1,), (1,)), ((), ())), preferred_element_type=jnp.float32
        )

    def weigh(slot, p):
        part = s_ref[slot]
        peak = jnp.concatenate([m_ref[...]] * 2, axis=1)
        weights = jnp.exp2((part - peak) * EXP2_SCALE).astype(jnp.bfloat16)
        return jnp.dot(weights, v_buf[p], preferred_element_type=jnp.float32)

    @pl.loop(0, Z)
    def _(z):
        q = q_ref[z]
        q4 = jnp.concatenate([q[:, g * HEAD_DIM : (g + 1) * HEAD_DIM] for g in range(GROUP)], axis=0)
        diag = Z + z
        count = jnp.clip(diag - lo_ref[z], 0, Z)
        steps = (count + 1) // 2
        qid = jnp.transpose(jnp.broadcast_to(ids_own[pl.ds(diag, 1), :], (ROWS, ROWS)))

        def put(slot, part, keep_own, keep_oth, start):
            for g in range(GROUP):
                rows = slice(g * ROWS, (g + 1) * ROWS)
                left = jnp.where(keep_own, part[rows, 0:ROWS], MASKED)
                right = jnp.where(keep_oth, part[rows, ROWS : 2 * ROWS], MASKED)
                s_ref[slot, rows, 0:ROWS] = left
                s_ref[slot, rows, ROWS : 2 * ROWS] = right
                most = jnp.maximum(left, right)
                m_ref[rows, :] = most if start else jnp.maximum(m_ref[rows, :], most)

        at_row = lax.broadcasted_iota(jnp.int32, (ROWS, ROWS), 0)
        at_col = lax.broadcasted_iota(jnp.int32, (ROWS, ROWS), 1)
        same_own = ids_own[pl.ds(diag, 1), :] == qid
        same_oth = ids_oth[pl.ds(diag, 1), :] == qid
        put(Z, scores(q4, diag), same_own & (at_col <= at_row), same_oth & odd, True)

        @pl.loop(0, steps)
        def _(k):
            for u in range(2):
                slot = 2 * k + u
                p = jnp.maximum(diag - 1 - slot, 0)
                put(
                    slot,
                    scores(q4, p),
                    ids_own[pl.ds(p, 1), :] == qid,
                    ids_oth[pl.ds(p, 1), :] == qid,
                    False,
                )

        m_ref[...] = jnp.broadcast_to(
            jnp.max(m_ref[...], axis=1, keepdims=True), (GROUP * ROWS, ROWS)
        )
        acc_ref[...] = weigh(Z, diag)

        @pl.loop(0, steps)
        def _(k):
            total = None
            for u in range(2):
                slot = 2 * k + u
                p = jnp.maximum(diag - 1 - slot, 0)
                term = weigh(slot, p)
                total = term if total is None else total + term
            acc_ref[...] += total

        zh, zl = z // 2, z % 2
        for g in range(GROUP):
            rows = slice(g * ROWS, (g + 1) * ROWS)
            out = acc_ref[rows, 0:HEAD_DIM] / acc_ref[rows, HEAD_DIM : 2 * HEAD_DIM]
            half = g // 2
            o_ref[
                2 * zh + g % 2, pl.ds(zl * ROWS, ROWS), half * HEAD_DIM : (half + 1) * HEAD_DIM
            ] = out.astype(jnp.bfloat16)


def projection_kernel(a_ref, w_ref, mine_ref, other_ref, a_buf):
    @pl.when(pl.program_id(0) == 0)
    def _():
        core = lax.axis_index("core")
        zl = lax.axis_index("zl")
        for zh in range(4):
            for t in range(2):
                source = 2 * zh + (core if t == 0 else 1 - core)
                for u in range(2):
                    row = (zl if u == 0 else 1 - zl) * ROWS
                    at = (2 * t + u) * ROWS
                    a_buf[at : at + ROWS, zh * 256 : (zh + 1) * 256] = a_ref[
                        source, pl.ds(row, ROWS), :
                    ]

    cols = w_ref.shape[-1]
    w = w_ref[0].reshape(8 * ROWS, cols)
    y = jnp.dot(a_buf[...], w, preferred_element_type=jnp.float32).astype(jnp.bfloat16)
    for u in range(2):
        mine_ref[u] = y[u * ROWS : (u + 1) * ROWS]
        other_ref[u] = y[(2 + u) * ROWS : (3 + u) * ROWS]


def body(queries, keys, values, doc_ids, out_weight):
    bf16 = jnp.bfloat16
    params = pltpu.CompilerParams(vmem_limit_bytes=VMEM_LIMIT)
    core = lax.axis_index("core")
    out_cols = out_weight.shape[1]
    piece = out_cols // 4

    own_part = lax.dynamic_slice(
        out_weight, (core * ROWS, lax.axis_index("x") * piece), (ROWS, piece)
    )
    weight = lax.all_gather(own_part, ("zh", "yh"), axis=0, tiled=False)
    weight = lax.all_gather(weight, "x", axis=0, tiled=False)

    packed = pl.pallas_call(
        pack_kernel,
        out_shape=jax.ShapeDtypeStruct((Z, ROWS + 16, 2 * HEAD_DIM), bf16),
        compiler_params=params,
        name="pack_kv",
    )(keys, values, doc_ids.reshape(1, ROWS))
    own = lax.all_to_all(packed, ("zh", "zl"), 0, 0, tiled=True)
    swap = [(0, 1), (1, 0)]
    ahead = [(i, i + 1) for i in range(15)]
    other = lax.ppermute(own, "yh", swap)
    prev_own = lax.ppermute(own, BLK, ahead)
    prev_other = lax.ppermute(other, BLK, ahead)

    split = queries.reshape(ROWS, Z, GROUP * HEAD_DIM).transpose(1, 0, 2)
    query = lax.all_to_all(split, ("zh", "zl"), 0, 0, tiled=True)

    attn = pl.pallas_call(
        attention_kernel,
        out_shape=jax.ShapeDtypeStruct((8, 2 * ROWS, 2 * HEAD_DIM), bf16),
        scratch_shapes=[
            pltpu.VMEM((PAIRS, 2 * ROWS, HEAD_DIM), bf16),
            pltpu.VMEM((PAIRS, 2 * ROWS, 2 * HEAD_DIM), bf16),
            pltpu.VMEM((PAIRS, ROWS), jnp.float32),
            pltpu.VMEM((PAIRS, ROWS), jnp.float32),
            pltpu.VMEM((PAIRS, ROWS), jnp.float32),
            pltpu.SMEM((Z,), jnp.int32),
            pltpu.VMEM((Z + 1, GROUP * ROWS, 2 * ROWS), jnp.float32),
            pltpu.VMEM((GROUP * ROWS, ROWS), jnp.float32),
            pltpu.VMEM((GROUP * ROWS, 2 * HEAD_DIM), jnp.float32),
        ],
        compiler_params=params,
        name="attention",
    )(query, own, other, prev_own, prev_other)

    spread = lax.all_to_all(attn, ("zh", "core"), 0, 0, tiled=True)
    half = jax.ShapeDtypeStruct((2, ROWS, out_cols), bf16)
    mine, theirs = pl.pallas_call(
        projection_kernel,
        grid=(4,),
        in_specs=[
            pl.BlockSpec((8, 2 * ROWS, 2 * HEAD_DIM), lambda i: (0, 0, 0)),
            pl.BlockSpec((1, 8, ROWS, piece), lambda i: (i, 0, 0, 0)),
        ],
        out_specs=[
            pl.BlockSpec((2, ROWS, piece), lambda i: (0, 0, i)),
            pl.BlockSpec((2, ROWS, piece), lambda i: (0, 0, i)),
        ],
        out_shape=[half, half],
        scratch_shapes=[pltpu.VMEM((4 * ROWS, 8 * ROWS), bf16)],
        compiler_params=params,
        name="projection",
    )(spread, weight)
    arrived = lax.ppermute(theirs, "core", swap)
    summed = mine.astype(jnp.float32) + arrived.astype(jnp.float32)
    last = lax.ppermute(summed[1].astype(bf16), "zl", swap)
    return (summed[0] + last.astype(jnp.float32)).astype(bf16)


def solution(mesh):
    torus = Mesh(mesh.devices.reshape(4, 2, 2, 4, 2, 2), AXES)
    uly = ("zh", "zl", "yh")
    rows = P(BLK + uly, None)
    in_specs = (rows, rows, rows, P(BLK + uly), P(uly, None))
    return jax.shard_map(body, mesh=torus, in_specs=in_specs, out_specs=rows, check_vma=False)
```

time: 439 us -> 245 us (0.56)
  the two profiles are of different devices: /device:TPU:1 before, /device:TPU:6 now
where the time goes in v1:
time: 245 us; the launch traced here: 241 us
  waiting for transfers between devices  152 us (62%)
  blocking collectives  35.8 us (15%)
  Pallas kernels  19.5 us (8%)
  starting transfers between devices  14.5 us (6%)
  between operations  13.5 us (6%)
  local copies, waits for them, and re-layouts  3.85 us (2%)
    all_gather x1, waiting for transfers between devices, body(): weight = lax.all_gather(own_part, ('zh', 'yh'), axis=0, tiled=False)  67.5 us
    all_to_all x1, blocking collectives, body(): spread = lax.all_to_all(attn, ('zh', 'core'), 0, 0, tiled=True)  35.8 us
    ppermute x1, waiting for transfers between devices, body(): last = lax.ppermute(summed[1].astype(bf16), 'zl', swap)  24 us
    all_to_all x1, waiting for transfers between devices, body(): own = lax.all_to_all(packed, ('zh', 'zl'), 0, 0, tiled=True)  16.8 us
    ppermute x1, waiting for transfers between devices, body(): other = lax.ppermute(own, 'yh', swap)  15.4 us
    ppermute x1, waiting for transfers between devices, body(): prev_other = lax.ppermute(other, BLK, ahead)  14.9 us
    pallas_call x1, Pallas kernels, body(): pl.pallas_call(attention_kernel, out_shape=jax.ShapeDtypeStruct((8, 2 * R...  11.3 us
    pallas_call x1, Pallas kernels, body(): pl.pallas_call(projection_kernel, grid=(4,), in_specs=[pl.BlockSpec((8, 2...  7.35 us
  transfers between devices with their start and end apart: 9, of which 8 were waited for; matrix products, arithmetic and copies ran while one was open for 1% of the time, Pallas kernels for 5%

profile of v1, /device:TPU:6, one launch (start us, length us, event | category | flops | bytes accessed | tf_op | source)
XLA Modules:
  0.0 241.4 jit_solution(14564382346800008707)
XLA Ops:
  6.5 0.0 copy-start.2
  6.5 0.0 copy-start.1
  6.5 0.0 copy-start
  6.5 0.0 all-gather.5.cloned.1.call-start
  6.5 1.7 dynamic_slice.3
  8.3 0.0 all-gather.5.cloned.1.call-update
  8.3 0.0 all-gather.7.cloned.1.call-start
  8.3 67.5 %all-gather.5.cloned.1.call-done = bf16[1024,1024]{1,0:T(8,128)(2,1)} async-done(((bf16[128,1024]{1,0:T(8,128)(2,1)}), bf16[1024,1024]{1,0:T(8,128)(2,1)}) %all-gather.5.cloned.1.call-update) | async-done | bytes 2097168 | tf_op jit(solution)/shard_map/all_gather | solution.py:166
  75.9 0.0 copy-start.3
  75.9 0.0 all-gather.7.cloned.1.call-update
  75.9 0.0 copy-done.2
  75.9 0.0 copy-done.1
  75.9 0.0 copy-done
  75.9 0.9 pack_kv.1
  76.9 5.2 %all-to-all-start.1 = ((bf16[8,144,256]{2,1,0:T(8,128)(2,1)}), bf16[8,144,256]{2,1,0:T(8,128)(2,1)S(1)}, u32[]{:S(2)}, u32[]{:S(2)}) async-start(bf16[8,144,256]{2,1,0:T(8,128)(2,1)} %pack_kv.1), calls=%async_computation.1 | async-start | bytes 1179648 | tf_op jit(solution)/shard_map/all_to_all | solution.py:175
  82.1 0.0 copy-done.3
  82.1 0.7 copy.8
  82.7 1.3 copy.9
  84.0 16.8 %all-to-all-done.1.own_ref = bf16[8,144,256]{2,1,0:T(8,128)(2,1)S(1)} async-done(((bf16[8,144,256]{2,1,0:T(8,128)(2,1)}), bf16[8,144,256]{2,1,0:T(8,128)(2,1)S(1)}, u32[]{:S(2)}, u32[]{:S(2)}) %all-to-all-start.1) | async-done | bytes 589856 | tf_op jit(solution)/shard_map/all_to_all | solution.py:175
  100.9 3.6 %all-to-all-start = ((bf16[8,128,512]{2,1,0:T(8,128)(2,1)}), bf16[8,128,512]{2,1,0:T(8,128)(2,1)S(1)}, u32[]{:S(2)}, u32[]{:S(2)}) async-start(bf16[8,128,512]{2,1,0:T(8,128)(2,1)} %bitcast.1), calls=%async_computation | async-start | bytes 2097152 | tf_op jit(solution)/shard_map/all_to_all | solution.py:183
  104.5 0.4 collective-permute-start
  104.9 1.9 collective-permute-start.1
  106.8 15.4 %collective-permute-done.oth_ref = bf16[8,144,256]{2,1,0:T(8,128)(2,1)S(1)} collective-permute-done((bf16[8,144,256]{2,1,0:T(8,128)(2,1)S(1)}, bf16[8,144,256]{2,1,0:T(8,128)(2,1)S(1)}, u32[]{:S(2)}, u32[]{:S(2)}) %collective-permute-start) | collective-permute-done | bytes 589856 | tf_op jit(solution)/shard_map/ppermute | solution.py:178
  122.2 1.9 collective-permute-start.2
  124.2 5.4 %collective-permute-done.1.pown_ref = bf16[8,144,256]{2,1,0:T(8,128)(2,1)S(1)} collective-permute-done((bf16[8,144,256]{2,1,0:T(8,128)(2,1)S(1)}, bf16[8,144,256]{2,1,0:T(8,128)(2,1)S(1)}, u32[]{:S(2)}, u32[]{:S(2)}) %collective-permute-start.1) | collective-permute-done | bytes 589856 | tf_op jit(solution)/shard_map/ppermute | solution.py:179
  129.6 4.0 %all-to-all-done.q_ref = bf16[8,128,512]{2,1,0:T(8,128)(2,1)S(1)} async-done(((bf16[8,128,512]{2,1,0:T(8,128)(2,1)}), bf16[8,128,512]{2,1,0:T(8,128)(2,1)S(1)}, u32[]{:S(2)}, u32[]{:S(2)}) %all-to-all-start) | async-done | bytes 1048608 | tf_op jit(solution)/shard_map/all_to_all | solution.py:183
  133.6 14.9 %collective-permute-done.2.poth_ref = bf16[8,144,256]{2,1,0:T(8,128)(2,1)S(1)} collective-permute-done((bf16[8,144,256]{2,1,0:T(8,128)(2,1)S(1)}, bf16[8,144,256]{2,1,0:T(8,128)(2,1)S(1)}, u32[]{:S(2)}, u32[]{:S(2)}) %collective-permute-start.2) | collective-permute-done | bytes 589856 | tf_op jit(solution)/shard_map/ppermute | solution.py:180
  148.5 11.3 %attention.1 = bf16[8,256,256]{2,1,0:T(8,128)(2,1)S(1)} custom-call(bf16[8,128,512]{2,1,0:T(8,128)(2,1)S(1)} %all-to-all-done.q_ref, bf16[8,144,256]{2,1,0:T(8,128)(2,1)S(1)} %all-to-all-done.1.own_ref, bf16[8,144,256]{2,1,0:T(8,128)(2,1)S(1)} %collective-permute-done.oth_ref, bf16[8,144,256]{2,1,0:T(8,128)(2,1)S(1)} %collective-permute-done.1.pown_ref, ...), custom_call_target="tpu_custom_call" | custom-call | tf_op jit(solution)/shard_map/attention/pallas_call | solution.py:185
  159.8 35.8 %all_to_all.15.a_ref = bf16[8,256,256]{2,1,0:T(8,128)(2,1)S(1)} all-to-all(bf16[8,256,256]{2,1,0:T(8,128)(2,1)S(1)} %attention.1), channel_id=1, replica_groups=mesh['x'=4,'yl'=2,'core'=2,'zh'=4,'zl'=2,'yh'=2] {'zh','core'}, dimensions={0} | all-to-all | bytes 2097152 | tf_op jit(solution)/shard_map/all_to_all | solution.py:203
  195.6 0.0 all-gather.7.cloned.1.call-done
  195.6 7.3 %projection.1 = (bf16[2,128,4096]{2,1,0:T(8,128)(2,1)S(1)}, bf16[2,128,4096]{2,1,0:T(8,128)(2,1)S(1)}) custom-call(bf16[8,256,256]{2,1,0:T(8,128)(2,1)S(1)} %all_to_all.15.a_ref, bf16[4,8,128,1024]{3,2,1,0:T(8,128)(2,1)} %bitcast.14), custom_call_target="tpu_custom_call" | custom-call | tf_op jit(solution)/shard_map/projection/pallas_call | solution.py:205
  202.9 0.1 collective-permute-start.3
  203.0 4.1 %collective-permute-done.3 = bf16[2,128,4096]{2,1,0:T(8,128)(2,1)S(1)} collective-permute-done((bf16[2,128,4096]{2,1,0:T(8,128)(2,1)S(1)}, bf16[2,128,4096]{2,1,0:T(8,128)(2,1)S(1)}, u32[]{:S(2)}, u32[]{:S(2)}) %collective-permute-start.3) | collective-permute-done | bytes 2097184 | tf_op jit(solution)/shard_map/ppermute | solution.py:221
  207.2 0.7 convert_add_fusion
  207.9 0.1 fusion.2
  208.0 1.3 collective-permute-start.4
  209.3 24.0 %collective-permute-done.4 = bf16[128,4096]{1,0:T(8,128)(2,1)S(1)} collective-permute-done((bf16[128,4096]{1,0:T(8,128)(2,1)S(1)}, bf16[128,4096]{1,0:T(8,128)(2,1)S(1)}, u32[]{:S(2)}, u32[]{:S(2)}) %collective-permute-start.4) | collective-permute-done | bytes 1048608 | tf_op jit(solution)/shard_map/ppermute | solution.py:223
  233.3 1.2 fusion.1
Async XLA Ops:
  6.5 69.4 %copy-start.2 = (s32[128]{0:T(128)S(1)}, s32[128]{0:T(128)}, u32[]{:S(2)}) copy-start(s32[128]{0:T(128)} %param.8) | copy-start | bytes 1540
  6.5 69.4 %copy-start.1 = (bf16[128,1024]{1,0:T(8,128)(2,1)S(1)}, bf16[128,1024]{1,0:T(8,128)(2,1)}, u32[]{:S(2)}) copy-start(bf16[128,1024]{1,0:T(8,128)(2,1)} %v_ref.1) | copy-start | bytes 786436
  6.5 69.4 %copy-start = (bf16[128,1024]{1,0:T(8,128)(2,1)S(1)}, bf16[128,1024]{1,0:T(8,128)(2,1)}, u32[]{:S(2)}) copy-start(bf16[128,1024]{1,0:T(8,128)(2,1)} %k_ref.1) | copy-start | bytes 786436
  6.5 69.3 %all-gather.5.cloned.1.call-start = ((), (), s32[]{:S(2)}) async-start(), calls=%async_computation.3 | async-start | bytes 2359296 | tf_op jit(solution)/shard_map/all_gather | solution.py:166
  8.3 187.3 %all-gather.7.cloned.1.call-start = ((), (), s32[]{:S(2)}) async-start(), calls=%async_computation.4 | async-start | bytes 10485760 | tf_op jit(solution)/shard_map/all_gather | solution.py:167
  75.9 6.2 %copy-start.3 = (bf16[128,4096]{1,0:T(8,128)(2,1)S(1)}, bf16[128,4096]{1,0:T(8,128)(2,1)}, u32[]{:S(2)}) copy-start(bf16[128,4096]{1,0:T(8,128)(2,1)} %param.5) | copy-start | bytes 3145732
  76.9 24.0 %all-to-all-start.1 = ((bf16[8,144,256]{2,1,0:T(8,128)(2,1)}), bf16[8,144,256]{2,1,0:T(8,128)(2,1)S(1)}, u32[]{:S(2)}, u32[]{:S(2)}) async-start(bf16[8,144,256]{2,1,0:T(8,128)(2,1)} %pack_kv.1), calls=%async_computation.1 | async-start | bytes 1179648 | tf_op jit(solution)/shard_map/all_to_all | solution.py:175
  100.9 32.7 %all-to-all-start = ((bf16[8,128,512]{2,1,0:T(8,128)(2,1)}), bf16[8,128,512]{2,1,0:T(8,128)(2,1)S(1)}, u32[]{:S(2)}, u32[]{:S(2)}) async-start(bf16[8,128,512]{2,1,0:T(8,128)(2,1)} %bitcast.1), calls=%async_computation | async-start | bytes 2097152 | tf_op jit(solution)/shard_map/all_to_all | solution.py:183
  104.5 17.8 %collective-permute-start = (bf16[8,144,256]{2,1,0:T(8,128)(2,1)S(1)}, bf16[8,144,256]{2,1,0:T(8,128)(2,1)S(1)}, u32[]{:S(2)}, u32[]{:S(2)}) collective-permute-start(bf16[8,144,256]{2,1,0:T(8,128)(2,1)S(1)} %all-to-all-done.1.own_ref), channel_id=1, source_target_pairs={{0,1},{1,0},{2,3},{3,2},{4,5},{5,4},{6,7},{7,6},{8,9},{9,8},{10,11... | collective-permute-start | bytes 1769480 | tf_op jit(solution)/shard_map/ppermute | solution.py:178
  104.9 24.7 %collective-permute-start.1 = (bf16[8,144,256]{2,1,0:T(8,128)(2,1)S(1)}, bf16[8,144,256]{2,1,0:T(8,128)(2,1)S(1)}, u32[]{:S(2)}, u32[]{:S(2)}) collective-permute-start(bf16[8,144,256]{2,1,0:T(8,128)(2,1)S(1)} %all-to-all-done.1.own_ref), channel_id=1, source_target_pairs={{0,16},{16,32},{32,48},{48,64},{64,80},{80,96},{96,112},{112,128},... | collective-permute-start | bytes 1769480 | tf_op jit(solution)/shard_map/ppermute | solution.py:179
  122.2 26.3 %collective-permute-start.2 = (bf16[8,144,256]{2,1,0:T(8,128)(2,1)S(1)}, bf16[8,144,256]{2,1,0:T(8,128)(2,1)S(1)}, u32[]{:S(2)}, u32[]{:S(2)}) collective-permute-start(bf16[8,144,256]{2,1,0:T(8,128)(2,1)S(1)} %collective-permute-done.oth_ref), channel_id=1, source_target_pairs={{0,16},{16,32},{32,48},{48,64},{64,80},{80,96},{96,112},{112,128},... | collective-permute-start | bytes 1769480 | tf_op jit(solution)/shard_map/ppermute | solution.py:180
  202.9 4.2 %collective-permute-start.3 = (bf16[2,128,4096]{2,1,0:T(8,128)(2,1)S(1)}, bf16[2,128,4096]{2,1,0:T(8,128)(2,1)S(1)}, u32[]{:S(2)}, u32[]{:S(2)}) collective-permute-start(bf16[2,128,4096]{2,1,0:T(8,128)(2,1)S(1)} %get-tuple-element.8), channel_id=1, source_target_pairs={{0,16},{16,0},{1,17},{17,1},{2,18},{18,2},{3,19},{19,3},{4,20},{20... | collective-permute-start | bytes 6291464 | tf_op jit(solution)/shard_map/ppermute | solution.py:221
  208.0 25.3 %collective-permute-start.4 = (bf16[128,4096]{1,0:T(8,128)(2,1)S(1)}, bf16[128,4096]{1,0:T(8,128)(2,1)S(1)}, u32[]{:S(2)}, u32[]{:S(2)}) collective-permute-start(bf16[128,4096]{1,0:T(8,128)(2,1)S(1)} %fusion.2), channel_id=1, source_target_pairs={{0,2},{2,0},{1,3},{3,1},{4,6},{6,4},{5,7},{7,5},{8,10},{10,8},{9,1... | collective-permute-start | bytes 3145736 | tf_op jit(solution)/shard_map/ppermute | solution.py:223
Sparse Core Ops, SparseCore 0:
  10.0 65.8 all-gather.4
  77.7 82.0 all-gather.6

commit v2 on v1

--- a/solution.py
+++ b/solution.py
@@ -16,6 +16,7 @@
 PAIRS = 16
 EXP2_SCALE = math.log2(math.e) / math.sqrt(HEAD_DIM)
 MASKED = -1e30
+HALVES = 2
 VMEM_LIMIT = 48 * 1024 * 1024
 
 AXES = ("x", "yl", "core", "zh", "zl", "yh")
@@ -33,19 +34,20 @@
 
 
 def attention_kernel(
-    q_ref, own_ref, oth_ref, pown_ref, poth_ref, o_ref,
+    q_ref, own_ref, oth_ref, pown_ref, poth0_ref, poth1_ref, o_ref,
     k_buf, v_buf, ids_own, ids_oth, last_ref, lo_ref, s_ref, m_ref, acc_ref,
 ):
     odd = lax.axis_index("yh") == 1
     ones = jnp.ones((2 * ROWS, HEAD_DIM), jnp.bfloat16)
-    for side, (a, b) in enumerate(((pown_ref, poth_ref), (own_ref, oth_ref))):
+    for side, (a, b) in enumerate((((pown_ref,), (poth0_ref, poth1_ref)), ((own_ref,), (oth_ref,)))):
         for g in range(Z):
             p = side * Z + g
-            for half, src in enumerate((a, b)):
+            for half, parts in enumerate((a, b)):
+                block = parts[0][g] if len(parts) == 1 else parts[0][g] + parts[1][g]
                 rows = slice(half * ROWS, (half + 1) * ROWS)
-                k_buf[p, rows, :] = src[g, 0:ROWS, 0:HEAD_DIM]
-                v_buf[p, rows, 0:HEAD_DIM] = src[g, 0:ROWS, HEAD_DIM : 2 * HEAD_DIM]
-                ids = src[g, ROWS : ROWS + 16, 0:HEAD_DIM].astype(jnp.float32)[0:1, :]
+                k_buf[p, rows, :] = block[0:ROWS, 0:HEAD_DIM]
+                v_buf[p, rows, 0:HEAD_DIM] = block[0:ROWS, HEAD_DIM : 2 * HEAD_DIM]
+                ids = block[ROWS : ROWS + 16, 0:HEAD_DIM].astype(jnp.float32)[0:1, :]
                 (ids_own if half == 0 else ids_oth)[p : p + 1, :] = ids
             v_buf[p, :, HEAD_DIM : 2 * HEAD_DIM] = ones
     last_ref[...] = jnp.broadcast_to(
@@ -120,33 +122,25 @@
                 total = term if total is None else total + term
             acc_ref[...] += total
 
-        zh, zl = z // 2, z % 2
         for g in range(GROUP):
             rows = slice(g * ROWS, (g + 1) * ROWS)
             out = acc_ref[rows, 0:HEAD_DIM] / acc_ref[rows, HEAD_DIM : 2 * HEAD_DIM]
-            half = g // 2
-            o_ref[
-                2 * zh + g % 2, pl.ds(zl * ROWS, ROWS), half * HEAD_DIM : (half + 1) * HEAD_DIM
-            ] = out.astype(jnp.bfloat16)
+            o_ref[4 * z + 2 * (g % 2) + g // 2] = out.astype(jnp.bfloat16)
 
 
 def projection_kernel(a_ref, w_ref, mine_ref, other_ref, a_buf):
     @pl.when(pl.program_id(0) == 0)
     def _():
         core = lax.axis_index("core")
-        zl = lax.axis_index("zl")
-        for zh in range(4):
-            for t in range(2):
-                source = 2 * zh + (core if t == 0 else 1 - core)
-                for u in range(2):
-                    row = (zl if u == 0 else 1 - zl) * ROWS
-                    at = (2 * t + u) * ROWS
-                    a_buf[at : at + ROWS, zh * 256 : (zh + 1) * 256] = a_ref[
-                        source, pl.ds(row, ROWS), :
-                    ]
-
-    cols = w_ref.shape[-1]
-    w = w_ref[0].reshape(8 * ROWS, cols)
+        yl = lax.axis_index("yl")
+        for t in range(2):
+            for u in range(2):
+                source = 2 * (core if t == 0 else 1 - core) + (yl if u == 0 else 1 - yl)
+                at = (2 * t + u) * ROWS
+                for z in range(Z):
+                    a_buf[at : at + ROWS, z * ROWS : (z + 1) * ROWS] = a_ref[4 * z + source]
+
+    w = w_ref[0].reshape(Z * ROWS, w_ref.shape[-1])
     y = jnp.dot(a_buf[...], w, preferred_element_type=jnp.float32).astype(jnp.bfloat16)
     for u in range(2):
         mine_ref[u] = y[u * ROWS : (u + 1) * ROWS]
@@ -158,13 +152,9 @@
     params = pltpu.CompilerParams(vmem_limit_bytes=VMEM_LIMIT)
     core = lax.axis_index("core")
     out_cols = out_weight.shape[1]
-    piece = out_cols // 4
-
-    own_part = lax.dynamic_slice(
-        out_weight, (core * ROWS, lax.axis_index("x") * piece), (ROWS, piece)
-    )
-    weight = lax.all_gather(own_part, ("zh", "yh"), axis=0, tiled=False)
-    weight = lax.all_gather(weight, "x", axis=0, tiled=False)
+    cols = out_cols // HALVES
+    piece = cols // 4
+    swap = [(0, 1), (1, 0)]
 
     packed = pl.pallas_call(
         pack_kernel,
@@ -172,19 +162,32 @@
         compiler_params=params,
         name="pack_kv",
     )(keys, values, doc_ids.reshape(1, ROWS))
+    mine = [
+        lax.dynamic_slice(
+            out_weight, (core * ROWS, j * cols + lax.axis_index("x") * piece), (ROWS, piece)
+        )
+        for j in range(HALVES)
+    ]
+    mine, packed = lax.optimization_barrier((jnp.stack(mine), packed))
+    mine = lax.ppermute(mine, ("yl", "yh"), [(0, 0), (1, 2), (2, 1), (3, 3)])
+    weights = [lax.all_gather(mine[j], ("x", "zh", "zl"), axis=0, tiled=False) for j in range(HALVES)]
+
     own = lax.all_to_all(packed, ("zh", "zl"), 0, 0, tiled=True)
-    swap = [(0, 1), (1, 0)]
-    ahead = [(i, i + 1) for i in range(15)]
     other = lax.ppermute(own, "yh", swap)
-    prev_own = lax.ppermute(own, BLK, ahead)
-    prev_other = lax.ppermute(other, BLK, ahead)
+    prev_own = lax.ppermute(own, BLK, [(i, i + 1) for i in range(15)])
+    prev_other_0 = lax.ppermute(
+        own,
+        BLK + ("yh",),
+        [(2 * i + h, 2 * (i + 1) + 1 - h) for i in range(1, 15, 2) for h in range(2)],
+    )
+    prev_other_1 = lax.ppermute(other, "core", [(0, 1)])
 
     split = queries.reshape(ROWS, Z, GROUP * HEAD_DIM).transpose(1, 0, 2)
     query = lax.all_to_all(split, ("zh", "zl"), 0, 0, tiled=True)
 
     attn = pl.pallas_call(
         attention_kernel,
-        out_shape=jax.ShapeDtypeStruct((8, 2 * ROWS, 2 * HEAD_DIM), bf16),
+        out_shape=jax.ShapeDtypeStruct((4 * Z, ROWS, HEAD_DIM), bf16),
         scratch_shapes=[
             pltpu.VMEM((PAIRS, 2 * ROWS, HEAD_DIM), bf16),
             pltpu.VMEM((PAIRS, 2 * ROWS, 2 * HEAD_DIM), bf16),
@@ -197,31 +200,50 @@
             pltpu.VMEM((GROUP * ROWS, 2 * HEAD_DIM), jnp.float32),
         ],
         compiler_params=params,
+        cost_estimate=pl.CostEstimate(
+            flops=2_000_000_000, bytes_accessed=6_000_000, transcendentals=4_000_000
+        ),
         name="attention",
-    )(query, own, other, prev_own, prev_other)
-
-    spread = lax.all_to_all(attn, ("zh", "core"), 0, 0, tiled=True)
-    half = jax.ShapeDtypeStruct((2, ROWS, out_cols), bf16)
-    mine, theirs = pl.pallas_call(
-        projection_kernel,
-        grid=(4,),
-        in_specs=[
-            pl.BlockSpec((8, 2 * ROWS, 2 * HEAD_DIM), lambda i: (0, 0, 0)),
-            pl.BlockSpec((1, 8, ROWS, piece), lambda i: (i, 0, 0, 0)),
-        ],
-        out_specs=[
-            pl.BlockSpec((2, ROWS, piece), lambda i: (0, 0, i)),
-            pl.BlockSpec((2, ROWS, piece), lambda i: (0, 0, i)),
-        ],
-        out_shape=[half, half],
-        scratch_shapes=[pltpu.VMEM((4 * ROWS, 8 * ROWS), bf16)],
-        compiler_params=params,
-        name="projection",
-    )(spread, weight)
-    arrived = lax.ppermute(theirs, "core", swap)
-    summed = mine.astype(jnp.float32) + arrived.astype(jnp.float32)
-    last = lax.ppermute(summed[1].astype(bf16), "zl", swap)
-    return (summed[0] + last.astype(jnp.float32)).astype(bf16)
+    )(query, own, other, prev_own, prev_other_0, prev_other_1)
+
+    spread = lax.all_to_all(attn, ("zh", "zl", "core", "yl"), 0, 0, tiled=True)
+    half = jax.ShapeDtypeStruct((2, ROWS, cols), bf16)
+
+    def finish(summed):
+        last = lax.ppermute(summed[1].astype(bf16), "yl", swap)
+        return (summed[0] + last.astype(jnp.float32)).astype(bf16)
+
+    parts = []
+    for j in range(HALVES):
+        if parts:
+            spread, summed = lax.optimization_barrier((spread, summed))
+            parts[-1] = finish(summed)
+        own_sum, theirs = pl.pallas_call(
+            projection_kernel,
+            grid=(4,),
+            in_specs=[
+                pl.BlockSpec((4 * Z, ROWS, HEAD_DIM), lambda i: (0, 0, 0)),
+                pl.BlockSpec((1, Z, ROWS, piece), lambda i: (i, 0, 0, 0)),
+            ],
+            out_specs=[
+                pl.BlockSpec((2, ROWS, piece), lambda i: (0, 0, i)),
+                pl.BlockSpec((2, ROWS, piece), lambda i: (0, 0, i)),
+            ],
+            out_shape=[half, half],
+            scratch_shapes=[pltpu.VMEM((4 * ROWS, Z * ROWS), bf16)],
+            compiler_params=params,
+            cost_estimate=pl.CostEstimate(
+                flops=2 * 4 * ROWS * Z * ROWS * cols,
+                bytes_accessed=2 * Z * ROWS * cols + 8 * ROWS * cols,
+                transcendentals=0,
+            ),
+            name="projection",
+        )(spread, weights[j].reshape(4, Z, ROWS, piece))
+        arrived = lax.ppermute(theirs, "core", swap)
+        summed = own_sum.astype(jnp.float32) + arrived.astype(jnp.float32)
+        parts.append(None)
+    parts[-1] = finish(summed)
+    return jnp.concatenate(parts, axis=1)
 
 
 def solution(mesh):

time: 245 us -> 255 us (1.041)
  the two profiles are of different devices: /device:TPU:6 before, /device:TPU:1 now
where the time goes in v2:
time: 255 us
  waiting for transfers between devices  123 us (48%)
  blocking collectives  48 us (19%)
  starting transfers between devices  39.6 us (16%)
  Pallas kernels  22.2 us (9%)
  between operations  13.6 us (5%)
  local copies, waits for them, and re-layouts  6.45 us (3%)
    all_gather x2, waiting for transfers between devices, body(): lax.all_gather(mine[j], ('x', 'zh', 'zl'), axis=0, tiled=False)  69.4 us
    all_to_all x1, blocking collectives, body(): spread = lax.all_to_all(attn, ('zh', 'zl', 'core', 'yl'), 0, 0, tiled=True)  48 us
    ppermute x2, waiting for transfers between devices, finish(): last = lax.ppermute(summed[1].astype(bf16), 'yl', swap)  20.8 us
    all_to_all x1, waiting for transfers between devices, body(): own = lax.all_to_all(packed, ('zh', 'zl'), 0, 0, tiled=True)  17.4 us
    pallas_call x1, Pallas kernels, body(): pl.pallas_call(attention_kernel, out_shape=jax.ShapeDtypeStruct((4 * Z, R...  11.1 us
    ppermute x1, starting transfers between devices, body(): other = lax.ppermute(own, 'yh', swap)  10.1 us
    pallas_call x2, Pallas kernels, body(): pl.pallas_call(projection_kernel, grid=(4,), in_specs=[pl.BlockSpec((4 *...  10.1 us
    all_to_all x1, starting transfers between devices, body(): own = lax.all_to_all(packed, ('zh', 'zl'), 0, 0, tiled=True)  9.03 us
  transfers between devices with their start and end apart: 13, of which 10 were waited for; matrix products, arithmetic and copies ran while one was open for 1% of the time, Pallas kernels for 6%

profile of v2, /device:TPU:1, one launch (start us, length us, event | category | flops | bytes accessed | tf_op | source)
XLA Modules:
  0.0 254.6 jit_solution(5388307862285456831)
XLA Ops:
  6.5 0.0 copy-start.3
  6.5 0.0 all-gather.3.cloned.1.call-start
  6.5 1.1 dynamic-slice_bitcast_fusion.1
  7.7 0.0 copy-start
  7.7 0.9 copy-done
  8.6 0.0 copy-start.1
  8.6 0.9 copy-done.1
  9.6 0.0 copy-start.2
  9.6 0.7 copy-done.2
  10.2 1.0 pack_kv.1
  11.2 0.7 collective-permute-start.4
  11.9 0.0 collective-permute-done.4
  11.9 0.7 fusion.5
  12.6 0.0 all-gather.3.cloned.1.call-update
  12.7 0.0 all-gather.5.cloned.1.call-start
  12.7 0.7 all-gather.5.cloned.1.call-update
  13.4 9.0 %all-to-all-start.1 = ((bf16[8,144,256]{2,1,0:T(8,128)(2,1)}), bf16[8,144,256]{2,1,0:T(8,128)(2,1)S(1)}, u32[]{:S(2)}, u32[]{:S(2)}) async-start(bf16[8,144,256]{2,1,0:T(8,128)(2,1)} %pack_kv.1), calls=%async_computation.1 | async-start | bytes 1179648 | tf_op jit(solution)/shard_map/all_to_all | solution.py:175
  22.4 0.0 copy-done.3
  22.4 0.7 copy.8
  23.1 1.3 copy.9
  24.4 17.4 %all-to-all-done.1.own_ref = bf16[8,144,256]{2,1,0:T(8,128)(2,1)S(1)} async-done(((bf16[8,144,256]{2,1,0:T(8,128)(2,1)}), bf16[8,144,256]{2,1,0:T(8,128)(2,1)S(1)}, u32[]{:S(2)}, u32[]{:S(2)}) %all-to-all-start.1) | async-done | bytes 589856 | tf_op jit(solution)/shard_map/all_to_all | solution.py:175
  41.8 3.6 %all-to-all-start = ((bf16[8,128,512]{2,1,0:T(8,128)(2,1)}), bf16[8,128,512]{2,1,0:T(8,128)(2,1)S(1)}, u32[]{:S(2)}, u32[]{:S(2)}) async-start(bf16[8,128,512]{2,1,0:T(8,128)(2,1)} %bitcast.1), calls=%async_computation | async-start | bytes 2097152 | tf_op jit(solution)/shard_map/all_to_all | solution.py:186
  45.4 10.1 %collective-permute-start = (bf16[8,144,256]{2,1,0:T(8,128)(2,1)S(1)}, bf16[8,144,256]{2,1,0:T(8,128)(2,1)S(1)}, u32[]{:S(2)}, u32[]{:S(2)}) collective-permute-start(bf16[8,144,256]{2,1,0:T(8,128)(2,1)S(1)} %all-to-all-done.1.own_ref), channel_id=1, source_target_pairs={{0,1},{1,0},{2,3},{3,2},{4,5},{5,4},{6,7},{7,6},{8,9},{9,8},{10,11... | collective-permute-start | bytes 1769480 | tf_op jit(solution)/shard_map/ppermute | solution.py:176
  55.5 3.3 %collective-permute-start.1 = (bf16[8,144,256]{2,1,0:T(8,128)(2,1)S(1)}, bf16[8,144,256]{2,1,0:T(8,128)(2,1)S(1)}, u32[]{:S(2)}, u32[]{:S(2)}) collective-permute-start(bf16[8,144,256]{2,1,0:T(8,128)(2,1)S(1)} %all-to-all-done.1.own_ref), channel_id=1, source_target_pairs={{0,16},{16,32},{32,48},{48,64},{64,80},{80,96},{96,112},{112,128},... | collective-permute-start | bytes 1769480 | tf_op jit(solution)/shard_map/ppermute | solution.py:177
  58.8 4.6 %collective-permute-start.2 = (bf16[8,144,256]{2,1,0:T(8,128)(2,1)S(1)}, bf16[8,144,256]{2,1,0:T(8,128)(2,1)S(1)}, u32[]{:S(2)}, u32[]{:S(2)}) collective-permute-start(bf16[8,144,256]{2,1,0:T(8,128)(2,1)S(1)} %all-to-all-done.1.own_ref), channel_id=1, source_target_pairs={{16,33},{17,32},{48,65},{49,64},{80,97},{81,96},{112,129},{113,128... | collective-permute-start | bytes 1769480 | tf_op jit(solution)/shard_map/ppermute | solution.py:178
  63.4 2.7 %collective-permute-done.oth_ref = bf16[8,144,256]{2,1,0:T(8,128)(2,1)S(1)} collective-permute-done((bf16[8,144,256]{2,1,0:T(8,128)(2,1)S(1)}, bf16[8,144,256]{2,1,0:T(8,128)(2,1)S(1)}, u32[]{:S(2)}, u32[]{:S(2)}) %collective-permute-start) | collective-permute-done | bytes 589856 | tf_op jit(solution)/shard_map/ppermute | solution.py:176
  66.1 1.3 collective-permute-start.3
  67.4 7.5 %collective-permute-done.1.pown_ref = bf16[8,144,256]{2,1,0:T(8,128)(2,1)S(1)} collective-permute-done((bf16[8,144,256]{2,1,0:T(8,128)(2,1)S(1)}, bf16[8,144,256]{2,1,0:T(8,128)(2,1)S(1)}, u32[]{:S(2)}, u32[]{:S(2)}) %collective-permute-start.1) | collective-permute-done | bytes 589856 | tf_op jit(solution)/shard_map/ppermute | solution.py:177
  75.0 0.0 collective-permute-done.2.poth0_ref
  75.0 0.3 all-to-all-done.q_ref
  75.2 0.7 collective-permute-done.3.poth1_ref
  75.9 11.1 %attention.1 = bf16[32,128,128]{2,1,0:T(8,128)(2,1)S(1)} custom-call(bf16[8,128,512]{2,1,0:T(8,128)(2,1)S(1)} %all-to-all-done.q_ref, bf16[8,144,256]{2,1,0:T(8,128)(2,1)S(1)} %all-to-all-done.1.own_ref, bf16[8,144,256]{2,1,0:T(8,128)(2,1)S(1)} %collective-permute-done.oth_ref, bf16[8,144,256]{2,1,0:T(8,128)(2,1)S(1)} %collective-permute-done.1.pown_ref, ...), custom_call_target="tpu_custom_call" | custom-call | flops 2000000000 | bytes 6000000 | tf_op jit(solution)/shard_map/attention/pallas_call | solution.py:188
  87.1 48.0 %all_to_all.15.a_ref = bf16[32,128,128]{2,1,0:T(8,128)(2,1)S(1)} all-to-all(bf16[32,128,128]{2,1,0:T(8,128)(2,1)S(1)} %attention.1), channel_id=1, replica_groups=mesh['x'=4,'yl'=2,'core'=2,'zh'=4,'zl'=2,'yh'=2] {'zh','zl','core','yl'}, dimensions={0} | all-to-all | bytes 2097152 | tf_op jit(solution)/shard_map/all_to_all | solution.py:209
  135.1 0.0 all-gather.3.cloned.1.call-done
  135.1 5.0 %projection.2 = (bf16[2,128,2048]{2,1,0:T(8,128)(2,1)S(1)}, bf16[2,128,2048]{2,1,0:T(8,128)(2,1)S(1)}) custom-call(bf16[32,128,128]{2,1,0:T(8,128)(2,1)S(1)} %all_to_all.15.a_ref, bf16[4,8,128,512]{3,2,1,0:T(8,128)(2,1)} %bitcast.26), custom_call_target="tpu_custom_call" | custom-call | flops 2147483648 | bytes 6291456 | tf_op jit(solution)/shard_map/projection/pallas_call | solution.py:221
  140.1 1.0 collective-permute-start.5
  141.1 2.3 collective-permute-done.5
  143.4 0.4 convert_add_fusion.1
  143.8 69.4 %all-gather.5.cloned.1.call-done = bf16[32,128,512]{2,1,0:T(8,128)(2,1)} async-done(((bf16[1,128,512]{2,1,0:T(8,128)(2,1)}), bf16[32,128,512]{2,1,0:T(8,128)(2,1)}) %all-gather.5.cloned.1.call-update) | async-done | bytes 4194320 | tf_op jit(solution)/shard_map/all_gather | solution.py:173
  213.2 5.0 %projection.3 = (bf16[2,128,2048]{2,1,0:T(8,128)(2,1)S(1)}, bf16[2,128,2048]{2,1,0:T(8,128)(2,1)S(1)}) custom-call(bf16[32,128,128]{2,1,0:T(8,128)(2,1)S(1)} %all_to_all.15.a_ref, bf16[4,8,128,512]{3,2,1,0:T(8,128)(2,1)} %bitcast.25), custom_call_target="tpu_custom_call" | custom-call | flops 2147483648 | bytes 6291456 | tf_op jit(solution)/shard_map/projection/pallas_call | solution.py:221
  218.2 3.4 %collective-permute-start.7 = (bf16[2,128,2048]{2,1,0:T(8,128)(2,1)S(1)}, bf16[2,128,2048]{2,1,0:T(8,128)(2,1)S(1)}, u32[]{:S(2)}, u32[]{:S(2)}) collective-permute-start(bf16[2,128,2048]{2,1,0:T(8,128)(2,1)S(1)} %get-tuple-element.20), channel_id=1, source_target_pairs={{0,16},{16,0},{1,17},{17,1},{2,18},{18,2},{3,19},{19,3},{4,20},{20... | collective-permute-start | bytes 3145736 | tf_op jit(solution)/shard_map/ppermute | solution.py:242
  221.6 0.1 fusion.3
  221.7 1.3 collective-permute-start.6
  223.0 0.9 collective-permute-done.7
  223.9 0.4 convert_add_fusion
  224.3 0.1 fusion.4
  224.3 1.3 collective-permute-start.8
  225.6 9.7 %collective-permute-done.6 = bf16[128,2048]{1,0:T(8,128)(2,1)S(1)} collective-permute-done((bf16[128,2048]{1,0:T(8,128)(2,1)S(1)}, bf16[128,2048]{1,0:T(8,128)(2,1)S(1)}, u32[]{:S(2)}, u32[]{:S(2)}) %collective-permute-start.6) | collective-permute-done | bytes 524320 | tf_op jit(solution)/shard_map/ppermute | solution.py:213
  235.3 0.1 fusion.2
  235.4 11.1 %collective-permute-done.8 = bf16[128,2048]{1,0:T(8,128)(2,1)S(1)} collective-permute-done((bf16[128,2048]{1,0:T(8,128)(2,1)S(1)}, bf16[128,2048]{1,0:T(8,128)(2,1)S(1)}, u32[]{:S(2)}, u32[]{:S(2)}) %collective-permute-start.8) | collective-permute-done | bytes 524320 | tf_op jit(solution)/shard_map/ppermute | solution.py:213
  246.5 0.1 fusion.1
  246.7 1.1 pad_maximum_fusion
  (1 shorter events, 0.0 us)
Async XLA Ops:
  6.5 15.9 %copy-start.3 = (bf16[128,4096]{1,0:T(8,128)(2,1)S(1)}, bf16[128,4096]{1,0:T(8,128)(2,1)}, u32[]{:S(2)}) copy-start(bf16[128,4096]{1,0:T(8,128)(2,1)} %param.5) | copy-start | bytes 3145732
  6.5 128.5 %all-gather.3.cloned.1.call-start = ((), (), s32[]{:S(2)}) async-start(), calls=%async_computation.3 | async-start | bytes 4325376 | tf_op jit(solution)/shard_map/all_gather | solution.py:173
  7.7 1.0 copy-start
  8.6 0.9 copy-start.1
  9.6 0.7 copy-start.2
  11.2 0.7 collective-permute-start.4
  12.7 200.5 %all-gather.5.cloned.1.call-start = ((), (), s32[]{:S(2)}) async-start(), calls=%async_computation.4 | async-start | bytes 4325376 | tf_op jit(solution)/shard_map/all_gather | solution.py:173
  13.4 28.4 %all-to-all-start.1 = ((bf16[8,144,256]{2,1,0:T(8,128)(2,1)}), bf16[8,144,256]{2,1,0:T(8,128)(2,1)S(1)}, u32[]{:S(2)}, u32[]{:S(2)}) async-start(bf16[8,144,256]{2,1,0:T(8,128)(2,1)} %pack_kv.1), calls=%async_computation.1 | async-start | bytes 1179648 | tf_op jit(solution)/shard_map/all_to_all | solution.py:175
  41.8 33.4 %all-to-all-start = ((bf16[8,128,512]{2,1,0:T(8,128)(2,1)}), bf16[8,128,512]{2,1,0:T(8,128)(2,1)S(1)}, u32[]{:S(2)}, u32[]{:S(2)}) async-start(bf16[8,128,512]{2,1,0:T(8,128)(2,1)} %bitcast.1), calls=%async_computation | async-start | bytes 2097152 | tf_op jit(solution)/shard_map/all_to_all | solution.py:186
  45.4 20.8 %collective-permute-start = (bf16[8,144,256]{2,1,0:T(8,128)(2,1)S(1)}, bf16[8,144,256]{2,1,0:T(8,128)(2,1)S(1)}, u32[]{:S(2)}, u32[]{:S(2)}) collective-permute-start(bf16[8,144,256]{2,1,0:T(8,128)(2,1)S(1)} %all-to-all-done.1.own_ref), channel_id=1, source_target_pairs={{0,1},{1,0},{2,3},{3,2},{4,5},{5,4},{6,7},{7,6},{8,9},{9,8},{10,11... | collective-permute-start | bytes 1769480 | tf_op jit(solution)/shard_map/ppermute | solution.py:176
  55.5 19.5 %collective-permute-start.1 = (bf16[8,144,256]{2,1,0:T(8,128)(2,1)S(1)}, bf16[8,144,256]{2,1,0:T(8,128)(2,1)S(1)}, u32[]{:S(2)}, u32[]{:S(2)}) collective-permute-start(bf16[8,144,256]{2,1,0:T(8,128)(2,1)S(1)} %all-to-all-done.1.own_ref), channel_id=1, source_target_pairs={{0,16},{16,32},{32,48},{48,64},{64,80},{80,96},{96,112},{112,128},... | collective-permute-start | bytes 1769480 | tf_op jit(solution)/shard_map/ppermute | solution.py:177
  58.8 16.2 %collective-permute-start.2 = (bf16[8,144,256]{2,1,0:T(8,128)(2,1)S(1)}, bf16[8,144,256]{2,1,0:T(8,128)(2,1)S(1)}, u32[]{:S(2)}, u32[]{:S(2)}) collective-permute-start(bf16[8,144,256]{2,1,0:T(8,128)(2,1)S(1)} %all-to-all-done.1.own_ref), channel_id=1, source_target_pairs={{16,33},{17,32},{48,65},{49,64},{80,97},{81,96},{112,129},{113,128... | collective-permute-start | bytes 1769480 | tf_op jit(solution)/shard_map/ppermute | solution.py:178
  66.1 9.8 %collective-permute-start.3 = (bf16[8,144,256]{2,1,0:T(8,128)(2,1)S(1)}, bf16[8,144,256]{2,1,0:T(8,128)(2,1)}, u32[]{:S(2)}, u32[]{:S(2)}) collective-permute-start(bf16[8,144,256]{2,1,0:T(8,128)(2,1)S(1)} %collective-permute-done.oth_ref), channel_id=1, source_target_pairs={{0,16},{1,17},{2,18},{3,19},{4,20},{5,21},{6,22},{7,23},{8,24},{9,... | collective-permute-start | bytes 1769480 | tf_op jit(solution)/shard_map/ppermute | solution.py:183
  140.1 3.3 %collective-permute-start.5 = (bf16[2,128,2048]{2,1,0:T(8,128)(2,1)S(1)}, bf16[2,128,2048]{2,1,0:T(8,128)(2,1)S(1)}, u32[]{:S(2)}, u32[]{:S(2)}) collective-permute-start(bf16[2,128,2048]{2,1,0:T(8,128)(2,1)S(1)} %get-tuple-element.16), channel_id=1, source_target_pairs={{0,16},{16,0},{1,17},{17,1},{2,18},{18,2},{3,19},{19,3},{4,20},{20... | collective-permute-start | bytes 3145736 | tf_op jit(solution)/shard_map/ppermute | solution.py:242
  218.2 5.7 %collective-permute-start.7 = (bf16[2,128,2048]{2,1,0:T(8,128)(2,1)S(1)}, bf16[2,128,2048]{2,1,0:T(8,128)(2,1)S(1)}, u32[]{:S(2)}, u32[]{:S(2)}) collective-permute-start(bf16[2,128,2048]{2,1,0:T(8,128)(2,1)S(1)} %get-tuple-element.20), channel_id=1, source_target_pairs={{0,16},{16,0},{1,17},{17,1},{2,18},{18,2},{3,19},{19,3},{4,20},{20... | collective-permute-start | bytes 3145736 | tf_op jit(solution)/shard_map/ppermute | solution.py:242
  221.7 13.6 %collective-permute-start.6 = (bf16[128,2048]{1,0:T(8,128)(2,1)S(1)}, bf16[128,2048]{1,0:T(8,128)(2,1)S(1)}, u32[]{:S(2)}, u32[]{:S(2)}) collective-permute-start(bf16[128,2048]{1,0:T(8,128)(2,1)S(1)} %fusion.3), channel_id=1, source_target_pairs={{0,32},{32,0},{1,33},{33,1},{2,34},{34,2},{3,35},{35,3},{4,36},{36... | collective-permute-start | bytes 1572872 | tf_op jit(solution)/shard_map/ppermute | solution.py:213
  224.3 22.2 %collective-permute-start.8 = (bf16[128,2048]{1,0:T(8,128)(2,1)S(1)}, bf16[128,2048]{1,0:T(8,128)(2,1)S(1)}, u32[]{:S(2)}, u32[]{:S(2)}) collective-permute-start(bf16[128,2048]{1,0:T(8,128)(2,1)S(1)} %fusion.4), channel_id=1, source_target_pairs={{0,32},{32,0},{1,33},{33,1},{2,34},{34,2},{3,35},{35,3},{4,36},{36... | collective-permute-start | bytes 1572872 | tf_op jit(solution)/shard_map/ppermute | solution.py:213
Sparse Core Ops, SparseCore 0:
  12.8 119.0 all-gather.2
  134.5 78.6 all-gather.4

commit v3 on v2

--- a/solution.py
+++ b/solution.py
@@ -17,7 +17,7 @@
 EXP2_SCALE = math.log2(math.e) / math.sqrt(HEAD_DIM)
 MASKED = -1e30
 HALVES = 2
-VMEM_LIMIT = 48 * 1024 * 1024
+VMEM_LIMIT = 20 * 1024 * 1024
 
 AXES = ("x", "yl", "core", "zh", "zl", "yh")
 BLK = ("x", "yl", "core")
@@ -128,23 +128,35 @@
             o_ref[4 * z + 2 * (g % 2) + g // 2] = out.astype(jnp.bfloat16)
 
 
-def projection_kernel(a_ref, w_ref, mine_ref, other_ref, a_buf):
-    @pl.when(pl.program_id(0) == 0)
-    def _():
-        core = lax.axis_index("core")
-        yl = lax.axis_index("yl")
-        for t in range(2):
-            for u in range(2):
-                source = 2 * (core if t == 0 else 1 - core) + (yl if u == 0 else 1 - yl)
-                at = (2 * t + u) * ROWS
-                for z in range(Z):
-                    a_buf[at : at + ROWS, z * ROWS : (z + 1) * ROWS] = a_ref[4 * z + source]
-
-    w = w_ref[0].reshape(Z * ROWS, w_ref.shape[-1])
-    y = jnp.dot(a_buf[...], w, preferred_element_type=jnp.float32).astype(jnp.bfloat16)
-    for u in range(2):
-        mine_ref[u] = y[u * ROWS : (u + 1) * ROWS]
-        other_ref[u] = y[(2 + u) * ROWS : (3 + u) * ROWS]
+def projection_kernel(a_ref, own_ref, before_ref, after_ref, far0_ref, far1_ref, keep_ref, send_ref, other_ref, a_buf):
+    core = lax.axis_index("core")
+    yl = lax.axis_index("yl")
+    x = lax.axis_index("x")
+    for t in range(2):
+        for u in range(2):
+            source = 2 * (core if t == 0 else 1 - core) + (yl if u == 0 else 1 - yl)
+            at = (2 * t + u) * ROWS
+            for z in range(Z):
+                a_buf[at : at + ROWS, z * ROWS : (z + 1) * ROWS] = a_ref[4 * z + source]
+    piece = own_ref.shape[-1]
+    half = (Z // 2) * ROWS
+
+    def product(rows, part):
+        return jnp.dot(a_buf[:, rows], part, preferred_element_type=jnp.float32)
+
+    for shift in (0, 3, 1, 2):
+        if shift == 2:
+            y = product(slice(0, half), far0_ref[...].reshape(half, piece))
+            y = y + product(slice(half, 2 * half), far1_ref[...].reshape(half, piece))
+        else:
+            ref = {0: own_ref, 3: before_ref, 1: after_ref}[shift]
+            y = product(slice(0, 2 * half), ref[...].reshape(2 * half, piece))
+        y = y.astype(jnp.bfloat16)
+        cols = pl.ds(pl.multiple_of(lax.rem(x + shift, 4) * piece, piece), piece)
+        keep_ref[:, cols] = y[0:ROWS]
+        send_ref[:, cols] = y[ROWS : 2 * ROWS]
+        for u in range(2):
+            other_ref[u, :, cols] = y[(2 + u) * ROWS : (3 + u) * ROWS]
 
 
 def body(queries, keys, values, doc_ids, out_weight):
@@ -170,9 +182,22 @@
     ]
     mine, packed = lax.optimization_barrier((jnp.stack(mine), packed))
     mine = lax.ppermute(mine, ("yl", "yh"), [(0, 0), (1, 2), (2, 1), (3, 3)])
-    weights = [lax.all_gather(mine[j], ("x", "zh", "zl"), axis=0, tiled=False) for j in range(HALVES)]
+    right = [(i, (i + 1) % 4) for i in range(4)]
+    left = [((i + 1) % 4, i) for i in range(4)]
+    here = [lax.all_gather(mine[j], ("zh", "zl"), axis=0, tiled=False) for j in range(HALVES)]
+
+    def beside(j):
+        return lax.ppermute(here[j], "x", right), lax.ppermute(here[j], "x", left)
+
+    def beyond(before, after):
+        return (
+            lax.ppermute(before[: Z // 2], "x", right),
+            lax.ppermute(after[Z // 2 :], "x", left),
+        )
 
     own = lax.all_to_all(packed, ("zh", "zl"), 0, 0, tiled=True)
+    own, here[0] = lax.optimization_barrier((own, here[0]))
+    near0 = beside(0)
     other = lax.ppermute(own, "yh", swap)
     prev_own = lax.ppermute(own, BLK, [(i, i + 1) for i in range(15)])
     prev_other_0 = lax.ppermute(
@@ -185,6 +210,9 @@
     split = queries.reshape(ROWS, Z, GROUP * HEAD_DIM).transpose(1, 0, 2)
     query = lax.all_to_all(split, ("zh", "zl"), 0, 0, tiled=True)
 
+    query, near0, here[1] = lax.optimization_barrier((query, near0, here[1]))
+    far0 = beyond(*near0)
+    near1 = beside(1)
     attn = pl.pallas_call(
         attention_kernel,
         out_shape=jax.ShapeDtypeStruct((4 * Z, ROWS, HEAD_DIM), bf16),
@@ -201,35 +229,24 @@
         ],
         compiler_params=params,
         cost_estimate=pl.CostEstimate(
-            flops=2_000_000_000, bytes_accessed=6_000_000, transcendentals=4_000_000
+            flops=16_000_000_000, bytes_accessed=6_000_000, transcendentals=4_000_000
         ),
         name="attention",
     )(query, own, other, prev_own, prev_other_0, prev_other_1)
 
+    attn, far0 = lax.optimization_barrier((attn, far0))
     spread = lax.all_to_all(attn, ("zh", "zl", "core", "yl"), 0, 0, tiled=True)
-    half = jax.ShapeDtypeStruct((2, ROWS, cols), bf16)
-
-    def finish(summed):
-        last = lax.ppermute(summed[1].astype(bf16), "yl", swap)
-        return (summed[0] + last.astype(jnp.float32)).astype(bf16)
-
+    spread, near1 = lax.optimization_barrier((spread, near1))
+    far1 = beyond(*near1)
+    weights = ((here[0], *near0, *far0), (here[1], *near1, *far1))
+    one = jax.ShapeDtypeStruct((ROWS, cols), bf16)
+    two = jax.ShapeDtypeStruct((2, ROWS, cols), bf16)
+    f32 = jnp.float32
     parts = []
     for j in range(HALVES):
-        if parts:
-            spread, summed = lax.optimization_barrier((spread, summed))
-            parts[-1] = finish(summed)
-        own_sum, theirs = pl.pallas_call(
+        keep, send, theirs = pl.pallas_call(
             projection_kernel,
-            grid=(4,),
-            in_specs=[
-                pl.BlockSpec((4 * Z, ROWS, HEAD_DIM), lambda i: (0, 0, 0)),
-                pl.BlockSpec((1, Z, ROWS, piece), lambda i: (i, 0, 0, 0)),
-            ],
-            out_specs=[
-                pl.BlockSpec((2, ROWS, piece), lambda i: (0, 0, i)),
-                pl.BlockSpec((2, ROWS, piece), lambda i: (0, 0, i)),
-            ],
-            out_shape=[half, half],
+            out_shape=[one, one, two],
             scratch_shapes=[pltpu.VMEM((4 * ROWS, Z * ROWS), bf16)],
             compiler_params=params,
             cost_estimate=pl.CostEstimate(
@@ -238,12 +255,15 @@
                 transcendentals=0,
             ),
             name="projection",
-        )(spread, weights[j].reshape(4, Z, ROWS, piece))
+        )(spread, *weights[j])
         arrived = lax.ppermute(theirs, "core", swap)
-        summed = own_sum.astype(jnp.float32) + arrived.astype(jnp.float32)
-        parts.append(None)
-    parts[-1] = finish(summed)
-    return jnp.concatenate(parts, axis=1)
+        send = (send.astype(f32) + arrived[1].astype(f32)).astype(bf16)
+        if j + 1 < HALVES:
+            spread, send = lax.optimization_barrier((spread, send))
+        parts.append((keep, arrived[0], lax.ppermute(send, "yl", swap)))
+    return jnp.concatenate(
+        [(k.astype(f32) + a.astype(f32) + m.astype(f32)).astype(bf16) for k, a, m in parts], axis=1
+    )
 
 
 def solution(mesh):

time: 255 us -> 239 us (0.937)
  blocking collectives: 48 us -> 0 us
  starting transfers between devices: 39.6 us -> 50.2 us
  waiting for transfers between devices: 123 us -> 132 us
  local copies, waits for them, and re-layouts: 6.45 us -> 13.4 us
  Pallas kernels: 22.2 us -> 26.2 us
    all_to_all x1 -> x0, blocking collectives: 48 us -> none  [body(): spread = lax.all_to_all(attn, ('zh', 'zl', 'core', 'yl'), 0, 0, tiled=True)]
    ppermute x2 -> x10, waiting for transfers between devices: 20.8 us -> 59.6 us  [the longest x4 24.7 us: beside(): return (lax.ppermute(here[j], 'x', right), lax.ppermute(here[j], 'x', left))]
    all_gather x2, waiting for transfers between devices: 69.4 us -> 52.6 us  [body(): lax.all_gather(mine[j], ('zh', 'zl'), axis=0, tiled=False)]
    ppermute x2 -> x10, starting transfers between devices: 2.58 us -> 16.2 us  [the longest x4 8.06 us: beside(): return (lax.ppermute(here[j], 'x', right), lax.ppermute(here[j], 'x', left))]
    ppermute x1, starting transfers between devices: 10.1 us -> 0.01 us  [body(): other = lax.ppermute(own, 'yh', swap)]
    ppermute x1, waiting for transfers between devices: 7.54 us -> 0.01 us  [body(): prev_own = lax.ppermute(own, BLK, [(i, i + 1) for i in range(15)])]
    pallas_call x1, Pallas kernels: 11.1 us -> 18 us  [body(): pl.pallas_call(attention_kernel, out_shape=jax.ShapeDtypeStruct((4 * Z, R...]
    all_to_all x0 -> x1, starting transfers between devices: none -> 6.38 us  [body(): spread = lax.all_to_all(attn, ('zh', 'zl', 'core', 'yl'), 0, 0, tiled=True)]
  transfers between devices with their start and end apart: 13 -> 22, of which waited for: 10 -> 11; matrix products, arithmetic and copies ran while one was open for 1% -> 2% of each run, Pallas kernels for 6% -> 8%
where the time goes in v3:
time: 239 us; the launch traced here: 237 us
  waiting for transfers between devices  132 us (55%)
  starting transfers between devices  50.2 us (21%)
  Pallas kernels  26.2 us (11%)
  between operations  13.6 us (6%)
  local copies, waits for them, and re-layouts  13.4 us (6%)
    all_gather x2, waiting for transfers between devices, body(): lax.all_gather(mine[j], ('zh', 'zl'), axis=0, tiled=False)  52.6 us
    ppermute x4, waiting for transfers between devices, beside(): return (lax.ppermute(here[j], 'x', right), lax.ppermute(here[j], 'x', left))  24.7 us
    ppermute x2, waiting for transfers between devices, body(): parts.append((keep, arrived[0], lax.ppermute(send, 'yl', swap)))  20.6 us
    pallas_call x1, Pallas kernels, body(): pl.pallas_call(attention_kernel, out_shape=jax.ShapeDtypeStruct((4 * Z, R...  18 us
    all_to_all x1, waiting for transfers between devices, body(): own = lax.all_to_all(packed, ('zh', 'zl'), 0, 0, tiled=True)  17.4 us
    ppermute x2, waiting for transfers between devices, beyond(): lax.ppermute(after[Z // 2:], 'x', left)  11.6 us
    all_to_all x1, starting transfers between devices, body(): own = lax.all_to_all(packed, ('zh', 'zl'), 0, 0, tiled=True)  9.04 us
    ppermute x1, starting transfers between devices, body(): lax.ppermute(own, BLK + ('yh',), [(2 * i + h, 2 * (i + 1) + 1 - h) for i...  8.37 us
  transfers between devices with their start and end apart: 22, of which 11 were waited for; matrix products, arithmetic and copies ran while one was open for 2% of the time, Pallas kernels for 8%

profile of v3, /device:TPU:1, one launch (start us, length us, event | category | flops | bytes accessed | tf_op | source)
XLA Modules:
  0.0 237.0 jit_solution(15004158760707916300)
XLA Ops:
  6.5 1.1 dynamic-slice_bitcast_fusion.1
  7.7 0.0 copy-start.2
  7.7 0.9 copy-done.2
  8.6 0.9 copy-done.3
  9.6 0.7 copy-done.4
  10.2 0.9 pack_kv.1
  11.1 0.7 collective-permute-start
  11.8 0.0 collective-permute-done
  11.8 0.7 fusion.6
  12.5 0.0 all-gather.3.cloned.1.call-update
  12.6 9.0 %all-to-all-start.1 = ((bf16[8,144,256]{2,1,0:T(8,128)(2,1)}), bf16[8,144,256]{2,1,0:T(8,128)(2,1)S(1)}, u32[]{:S(2)}, u32[]{:S(2)}) async-start(bf16[8,144,256]{2,1,0:T(8,128)(2,1)} %pack_kv.1), calls=%async_computation.1 | async-start | bytes 1179648 | tf_op jit(solution)/shard_map/all_to_all | solution.py:198
  21.6 0.7 copy.8
  22.3 1.3 copy.9
  23.6 17.4 %all-to-all-done.1.own_ref = bf16[8,144,256]{2,1,0:T(8,128)(2,1)S(1)} async-done(((bf16[8,144,256]{2,1,0:T(8,128)(2,1)}), bf16[8,144,256]{2,1,0:T(8,128)(2,1)S(1)}, u32[]{:S(2)}, u32[]{:S(2)}) %all-to-all-start.1) | async-done | bytes 589856 | tf_op jit(solution)/shard_map/all_to_all | solution.py:198
  41.0 3.6 %all-to-all-start = ((bf16[8,128,512]{2,1,0:T(8,128)(2,1)}), bf16[8,128,512]{2,1,0:T(8,128)(2,1)S(1)}, u32[]{:S(2)}, u32[]{:S(2)}) async-start(bf16[8,128,512]{2,1,0:T(8,128)(2,1)} %bitcast.1), calls=%async_computation | async-start | bytes 2097152 | tf_op jit(solution)/shard_map/all_to_all | solution.py:211
  44.5 0.0 all-gather.5.cloned.1.call-start
  44.6 0.7 all-gather.5.cloned.1.call-update
  45.3 26.9 %all-gather.3.cloned.1.call-done.own_ref = bf16[8,128,512]{2,1,0:T(8,128)(2,1)} async-done(((bf16[1,128,512]{2,1,0:T(8,128)(2,1)}), bf16[8,128,512]{2,1,0:T(8,128)(2,1)}) %all-gather.3.cloned.1.call-update) | async-done | bytes 1048592 | tf_op jit(solution)/shard_map/all_gather | solution.py:187
  72.2 0.0 collective-permute-start.3
  72.2 2.6 %collective-permute-start.2 = (bf16[8,128,512]{2,1,0:T(8,128)(2,1)}, bf16[8,128,512]{2,1,0:T(8,128)(2,1)S(1)}, u32[]{:S(2)}, u32[]{:S(2)}) collective-permute-start(bf16[8,128,512]{2,1,0:T(8,128)(2,1)} %all-gather.3.cloned.1.call-done.own_ref), channel_id=1, source_target_pairs={{64,0},{128,64},{192,128},{0,192},{65,1},{129,65},{193,129},{1,193... | collective-permute-start | bytes 3145736 | tf_op jit(solution)/shard_map/ppermute | solution.py:190
  74.8 0.0 collective-permute-start.1
  74.8 8.4 %collective-permute-start.5 = (bf16[8,144,256]{2,1,0:T(8,128)(2,1)S(1)}, bf16[8,144,256]{2,1,0:T(8,128)(2,1)}, u32[]{:S(2)}, u32[]{:S(2)}) collective-permute-start(bf16[8,144,256]{2,1,0:T(8,128)(2,1)S(1)} %all-to-all-done.1.own_ref), channel_id=1, source_target_pairs={{16,33},{17,32},{48,65},{49,64},{80,97},{81,96},{112,129},{113,128... | collective-permute-start | bytes 1769480 | tf_op jit(solution)/shard_map/ppermute | solution.py:203
  83.2 1.9 collective-permute-start.4
  85.1 0.6 collective-permute-done.3.oth_ref
  85.7 1.3 collective-permute-start.6
  87.0 0.0 all-to-all-done.q_ref
  87.0 25.6 %all-gather.5.cloned.1.call-done.own_ref = bf16[8,128,512]{2,1,0:T(8,128)(2,1)} async-done(((bf16[1,128,512]{2,1,0:T(8,128)(2,1)}), bf16[8,128,512]{2,1,0:T(8,128)(2,1)}) %all-gather.5.cloned.1.call-update) | async-done | bytes 1048592 | tf_op jit(solution)/shard_map/all_gather | solution.py:187
  112.6 1.1 slice.32
  113.7 3.1 %collective-permute-start.8 = (bf16[4,128,512]{2,1,0:T(8,128)(2,1)S(1)}, bf16[4,128,512]{2,1,0:T(8,128)(2,1)S(1)}, u32[]{:S(2)}, u32[]{:S(2)}) collective-permute-start(bf16[4,128,512]{2,1,0:T(8,128)(2,1)S(1)} %slice.33), channel_id=1, source_target_pairs={{64,0},{128,64},{192,128},{0,192},{65,1},{129,65},{193,129},{1,193... | collective-permute-start | bytes 1572872 | tf_op jit(solution)/shard_map/ppermute | solution.py:195
  116.8 0.0 collective-permute-done.6.poth1_ref
  116.9 18.0 %attention.1 = bf16[32,128,128]{2,1,0:T(8,128)(2,1)} custom-call(bf16[8,128,512]{2,1,0:T(8,128)(2,1)S(1)} %all-to-all-done.q_ref, bf16[8,144,256]{2,1,0:T(8,128)(2,1)S(1)} %all-to-all-done.1.own_ref, bf16[8,144,256]{2,1,0:T(8,128)(2,1)S(1)} %collective-permute-done.3.oth_ref, bf16[8,144,256]{2,1,0:T(8,128)(2,1)} %collective-permute-done.4.pown_ref, ...), custom_call_target="tpu_custom_call" | custom-call | flops 16000000000 | bytes 6000000 | tf_op jit(solution)/shard_map/attention/pallas_call | solution.py:216
  134.9 0.0 collective-permute-done.8.far1_ref
  134.9 0.8 copy-done.7
  135.7 0.0 collective-permute-done.7.far0_ref
  135.7 0.8 copy-done.9
  136.5 6.4 %all-to-all-start.2 = ((bf16[32,128,128]{2,1,0:T(8,128)(2,1)}), bf16[32,128,128]{2,1,0:T(8,128)(2,1)S(1)}, u32[]{:S(2)}, u32[]{:S(2)}) async-start(bf16[32,128,128]{2,1,0:T(8,128)(2,1)} %attention.1), calls=%async_computation.2 | async-start | bytes 2097152 | tf_op jit(solution)/shard_map/all_to_all | solution.py:238
  142.9 5.5 %collective-permute-start.10 = (bf16[8,128,512]{2,1,0:T(8,128)(2,1)}, bf16[8,128,512]{2,1,0:T(8,128)(2,1)S(1)}, u32[]{:S(2)}, u32[]{:S(2)}) collective-permute-start(bf16[8,128,512]{2,1,0:T(8,128)(2,1)} %all-gather.5.cloned.1.call-done.own_ref), channel_id=1, source_target_pairs={{64,0},{128,64},{192,128},{0,192},{65,1},{129,65},{193,129},{1,193... | collective-permute-start | bytes 3145736 | tf_op jit(solution)/shard_map/ppermute | solution.py:190
  148.4 0.0 collective-permute-start.9
  148.4 23.3 %collective-permute-done.10.after_ref = bf16[8,128,512]{2,1,0:T(8,128)(2,1)S(1)} collective-permute-done((bf16[8,128,512]{2,1,0:T(8,128)(2,1)}, bf16[8,128,512]{2,1,0:T(8,128)(2,1)S(1)}, u32[]{:S(2)}, u32[]{:S(2)}) %collective-permute-start.10) | collective-permute-done | bytes 1048608 | tf_op jit(solution)/shard_map/ppermute | solution.py:190
  171.7 1.0 copy-done
  172.7 1.5 collective-permute-done.9.before_ref
  174.1 0.0 all-to-all-done.2.a_ref
  174.1 1.2 copy-done.6
  175.4 1.0 copy-done.10
  176.4 3.7 %projection.2 = (bf16[128,2048]{1,0:T(8,128)(2,1)S(1)}, bf16[128,2048]{1,0:T(8,128)(2,1)S(1)}, bf16[2,128,2048]{2,1,0:T(8,128)(2,1)S(1)}) custom-call(bf16[32,128,128]{2,1,0:T(8,128)(2,1)S(1)} %all-to-all-done.2.a_ref, bf16[8,128,512]{2,1,0:T(8,128)(2,1)S(1)} %copy-done.6, bf16[8,128,512]{2,1,0:T(8,128)(2,1)} %collective-permute-done.1.before_ref, ...), custom_call_target="tpu_custom_call" | custom-call | flops 2147483648 | bytes 6291456 | tf_op jit(solution)/shard_map/projection/pallas_call | solution.py:247
  180.1 1.5 collective-permute-start.11
  181.5 1.1 slice.36
  182.7 2.3 collective-permute-start.14
  184.9 0.0 collective-permute-start.13
  184.9 0.0 collective-permute-done.11
  184.9 0.1 fusion.3
  185.1 11.6 %collective-permute-done.14.far1_ref = bf16[4,128,512]{2,1,0:T(8,128)(2,1)S(1)} collective-permute-done((bf16[4,128,512]{2,1,0:T(8,128)(2,1)S(1)}, bf16[4,128,512]{2,1,0:T(8,128)(2,1)S(1)}, u32[]{:S(2)}, u32[]{:S(2)}) %collective-permute-start.14) | collective-permute-done | bytes 524320 | tf_op jit(solution)/shard_map/ppermute | solution.py:195
  196.7 2.6 %collective-permute-done.13.far0_ref = bf16[4,128,512]{2,1,0:T(8,128)(2,1)S(1)} collective-permute-done((bf16[4,128,512]{2,1,0:T(8,128)(2,1)S(1)}, bf16[4,128,512]{2,1,0:T(8,128)(2,1)S(1)}, u32[]{:S(2)}, u32[]{:S(2)}) %collective-permute-start.13) | collective-permute-done | bytes 524320 | tf_op jit(solution)/shard_map/ppermute | solution.py:194
  199.3 3.6 %projection.3 = (bf16[128,2048]{1,0:T(8,128)(2,1)S(1)}, bf16[128,2048]{1,0:T(8,128)(2,1)S(1)}, bf16[2,128,2048]{2,1,0:T(8,128)(2,1)S(1)}) custom-call(bf16[32,128,128]{2,1,0:T(8,128)(2,1)S(1)} %all-to-all-done.2.a_ref, bf16[8,128,512]{2,1,0:T(8,128)(2,1)S(1)} %copy-done.5, bf16[8,128,512]{2,1,0:T(8,128)(2,1)} %collective-permute-done.9.before_ref, ...), custom_call_target="tpu_custom_call" | custom-call | flops 2147483648 | bytes 6291456 | tf_op jit(solution)/shard_map/projection/pallas_call | solution.py:247
  202.9 1.3 collective-permute-start.15
  204.1 1.4 collective-permute-start.12
  205.5 0.9 collective-permute-done.15
  206.4 0.1 fusion
  206.5 1.4 collective-permute-start.16
  208.0 9.6 %collective-permute-done.12 = bf16[128,2048]{1,0:T(8,128)(2,1)S(1)} collective-permute-done((bf16[128,2048]{1,0:T(8,128)(2,1)S(1)}, bf16[128,2048]{1,0:T(8,128)(2,1)S(1)}, u32[]{:S(2)}, u32[]{:S(2)}) %collective-permute-start.12) | collective-permute-done | bytes 524320 | tf_op jit(solution)/shard_map/ppermute | solution.py:263
  217.6 0.2 fusion.5
  217.9 11.0 %collective-permute-done.16 = bf16[128,2048]{1,0:T(8,128)(2,1)S(1)} collective-permute-done((bf16[128,2048]{1,0:T(8,128)(2,1)S(1)}, bf16[128,2048]{1,0:T(8,128)(2,1)S(1)}, u32[]{:S(2)}, u32[]{:S(2)}) %collective-permute-start.16) | collective-permute-done | bytes 524320 | tf_op jit(solution)/shard_map/ppermute | solution.py:263
  228.8 0.2 fusion.2
  229.1 1.1 pad_maximum_fusion
  (24 shorter events, 0.1 us)
Async XLA Ops:
  6.5 15.1 %copy-start.11 = (bf16[128,4096]{1,0:T(8,128)(2,1)S(1)}, bf16[128,4096]{1,0:T(8,128)(2,1)}, u32[]{:S(2)}) copy-start(bf16[128,4096]{1,0:T(8,128)(2,1)} %param.5) | copy-start | bytes 3145732
  6.5 65.7 %all-gather.3.cloned.1.call-start = ((), (), s32[]{:S(2)}) async-start(), calls=%async_computation.3 | async-start | bytes 1179648 | tf_op jit(solution)/shard_map/all_gather | solution.py:187
  7.7 1.0 copy-start.2
  8.6 0.9 copy-start.3
  9.6 0.7 copy-start.4
  11.1 0.7 collective-permute-start
  12.6 28.4 %all-to-all-start.1 = ((bf16[8,144,256]{2,1,0:T(8,128)(2,1)}), bf16[8,144,256]{2,1,0:T(8,128)(2,1)S(1)}, u32[]{:S(2)}, u32[]{:S(2)}) async-start(bf16[8,144,256]{2,1,0:T(8,128)(2,1)} %pack_kv.1), calls=%async_computation.1 | async-start | bytes 1179648 | tf_op jit(solution)/shard_map/all_to_all | solution.py:198
  41.0 46.0 %all-to-all-start = ((bf16[8,128,512]{2,1,0:T(8,128)(2,1)}), bf16[8,128,512]{2,1,0:T(8,128)(2,1)S(1)}, u32[]{:S(2)}, u32[]{:S(2)}) async-start(bf16[8,128,512]{2,1,0:T(8,128)(2,1)} %bitcast.1), calls=%async_computation | async-start | bytes 2097152 | tf_op jit(solution)/shard_map/all_to_all | solution.py:211
  44.5 68.1 %all-gather.5.cloned.1.call-start = ((), (), s32[]{:S(2)}) async-start(), calls=%async_computation.4 | async-start | bytes 1179648 | tf_op jit(solution)/shard_map/all_gather | solution.py:187
  72.2 13.5 %collective-permute-start.3 = (bf16[8,144,256]{2,1,0:T(8,128)(2,1)S(1)}, bf16[8,144,256]{2,1,0:T(8,128)(2,1)S(1)}, u32[]{:S(2)}, u32[]{:S(2)}) collective-permute-start(bf16[8,144,256]{2,1,0:T(8,128)(2,1)S(1)} %all-to-all-done.1.own_ref), channel_id=1, source_target_pairs={{0,1},{1,0},{2,3},{3,2},{4,5},{5,4},{6,7},{7,6},{8,9},{9,8},{10,11... | collective-permute-start | bytes 1769480 | tf_op jit(solution)/shard_map/ppermute | solution.py:201
  72.2 40.4 %collective-permute-start.2 = (bf16[8,128,512]{2,1,0:T(8,128)(2,1)}, bf16[8,128,512]{2,1,0:T(8,128)(2,1)S(1)}, u32[]{:S(2)}, u32[]{:S(2)}) collective-permute-start(bf16[8,128,512]{2,1,0:T(8,128)(2,1)} %all-gather.3.cloned.1.call-done.own_ref), channel_id=1, source_target_pairs={{64,0},{128,64},{192,128},{0,192},{65,1},{129,65},{193,129},{1,193... | collective-permute-start | bytes 3145736 | tf_op jit(solution)/shard_map/ppermute | solution.py:190
  74.8 37.8 %collective-permute-start.1 = (bf16[8,128,512]{2,1,0:T(8,128)(2,1)}, bf16[8,128,512]{2,1,0:T(8,128)(2,1)}, u32[]{:S(2)}, u32[]{:S(2)}) collective-permute-start(bf16[8,128,512]{2,1,0:T(8,128)(2,1)} %all-gather.3.cloned.1.call-done.own_ref), channel_id=1, source_target_pairs={{0,64},{64,128},{128,192},{192,0},{1,65},{65,129},{129,193},{193,1... | collective-permute-start | bytes 3145736 | tf_op jit(solution)/shard_map/ppermute | solution.py:190
  74.8 42.1 %collective-permute-start.5 = (bf16[8,144,256]{2,1,0:T(8,128)(2,1)S(1)}, bf16[8,144,256]{2,1,0:T(8,128)(2,1)}, u32[]{:S(2)}, u32[]{:S(2)}) collective-permute-start(bf16[8,144,256]{2,1,0:T(8,128)(2,1)S(1)} %all-to-all-done.1.own_ref), channel_id=1, source_target_pairs={{16,33},{17,32},{48,65},{49,64},{80,97},{81,96},{112,129},{113,128... | collective-permute-start | bytes 1769480 | tf_op jit(solution)/shard_map/ppermute | solution.py:203
  83.2 33.7 %collective-permute-start.4 = (bf16[8,144,256]{2,1,0:T(8,128)(2,1)S(1)}, bf16[8,144,256]{2,1,0:T(8,128)(2,1)}, u32[]{:S(2)}, u32[]{:S(2)}) collective-permute-start(bf16[8,144,256]{2,1,0:T(8,128)(2,1)S(1)} %all-to-all-done.1.own_ref), channel_id=1, source_target_pairs={{0,16},{16,32},{32,48},{48,64},{64,80},{80,96},{96,112},{112,128},... | collective-permute-start | bytes 1769480 | tf_op jit(solution)/shard_map/ppermute | solution.py:202
  85.7 31.2 %collective-permute-start.6 = (bf16[8,144,256]{2,1,0:T(8,128)(2,1)S(1)}, bf16[8,144,256]{2,1,0:T(8,128)(2,1)}, u32[]{:S(2)}, u32[]{:S(2)}) collective-permute-start(bf16[8,144,256]{2,1,0:T(8,128)(2,1)S(1)} %collective-permute-done.3.oth_ref), channel_id=1, source_target_pairs={{0,16},{1,17},{2,18},{3,19},{4,20},{5,21},{6,22},{7,23},{8,24},{9,... | collective-permute-start | bytes 1769480 | tf_op jit(solution)/shard_map/ppermute | solution.py:208
  113.7 21.1 %collective-permute-start.8 = (bf16[4,128,512]{2,1,0:T(8,128)(2,1)S(1)}, bf16[4,128,512]{2,1,0:T(8,128)(2,1)S(1)}, u32[]{:S(2)}, u32[]{:S(2)}) collective-permute-start(bf16[4,128,512]{2,1,0:T(8,128)(2,1)S(1)} %slice.33), channel_id=1, source_target_pairs={{64,0},{128,64},{192,128},{0,192},{65,1},{129,65},{193,129},{1,193... | collective-permute-start | bytes 1572872 | tf_op jit(solution)/shard_map/ppermute | solution.py:195
  116.8 18.9 %collective-permute-start.7 = (bf16[4,128,512]{2,1,0:T(8,128)(2,1)S(1)}, bf16[4,128,512]{2,1,0:T(8,128)(2,1)S(1)}, u32[]{:S(2)}, u32[]{:S(2)}) collective-permute-start(bf16[4,128,512]{2,1,0:T(8,128)(2,1)S(1)} %slice.32), channel_id=1, source_target_pairs={{0,64},{64,128},{128,192},{192,0},{1,65},{65,129},{129,193},{193,1... | collective-permute-start | bytes 1572872 | tf_op jit(solution)/shard_map/ppermute | solution.py:194
  134.9 0.8 copy-start.7
  135.7 0.8 copy-start.9
  136.5 37.6 %copy-start.8 = (bf16[4,128,512]{2,1,0:T(8,128)(2,1)S(1)}, bf16[4,128,512]{2,1,0:T(8,128)(2,1)}, u32[]{:S(2)}) copy-start(bf16[4,128,512]{2,1,0:T(8,128)(2,1)} %copy-done.7) | copy-start | bytes 1572868
  136.5 37.6 %all-to-all-start.2 = ((bf16[32,128,128]{2,1,0:T(8,128)(2,1)}), bf16[32,128,128]{2,1,0:T(8,128)(2,1)S(1)}, u32[]{:S(2)}, u32[]{:S(2)}) async-start(bf16[32,128,128]{2,1,0:T(8,128)(2,1)} %attention.1), calls=%async_computation.2 | async-start | bytes 2097152 | tf_op jit(solution)/shard_map/all_to_all | solution.py:238
  142.9 28.8 %collective-permute-start.10 = (bf16[8,128,512]{2,1,0:T(8,128)(2,1)}, bf16[8,128,512]{2,1,0:T(8,128)(2,1)S(1)}, u32[]{:S(2)}, u32[]{:S(2)}) collective-permute-start(bf16[8,128,512]{2,1,0:T(8,128)(2,1)} %all-gather.5.cloned.1.call-done.own_ref), channel_id=1, source_target_pairs={{64,0},{128,64},{192,128},{0,192},{65,1},{129,65},{193,129},{1,193... | collective-permute-start | bytes 3145736 | tf_op jit(solution)/shard_map/ppermute | solution.py:190
  148.4 25.7 %collective-permute-start.9 = (bf16[8,128,512]{2,1,0:T(8,128)(2,1)}, bf16[8,128,512]{2,1,0:T(8,128)(2,1)}, u32[]{:S(2)}, u32[]{:S(2)}) collective-permute-start(bf16[8,128,512]{2,1,0:T(8,128)(2,1)} %all-gather.5.cloned.1.call-done.own_ref), channel_id=1, source_target_pairs={{0,64},{64,128},{128,192},{192,0},{1,65},{65,129},{129,193},{193,1... | collective-permute-start | bytes 3145736 | tf_op jit(solution)/shard_map/ppermute | solution.py:190
  171.7 1.0 copy-start
  174.1 1.2 copy-start.6
  175.4 1.0 copy-start.10
  176.4 6.2 %copy-start.1 = (bf16[8,128,512]{2,1,0:T(8,128)(2,1)S(1)}, bf16[8,128,512]{2,1,0:T(8,128)(2,1)}, u32[]{:S(2)}) copy-start(bf16[8,128,512]{2,1,0:T(8,128)(2,1)} %copy-done) | copy-start | bytes 3145732
  180.1 19.2 %copy-start.5 = (bf16[8,128,512]{2,1,0:T(8,128)(2,1)S(1)}, bf16[8,128,512]{2,1,0:T(8,128)(2,1)}, u32[]{:S(2)}) copy-start(bf16[8,128,512]{2,1,0:T(8,128)(2,1)} %all-gather.5.cloned.1.call-done.own_ref) | copy-start | bytes 3145732
  180.1 4.8 %collective-permute-start.11 = (bf16[2,128,2048]{2,1,0:T(8,128)(2,1)S(1)}, bf16[2,128,2048]{2,1,0:T(8,128)(2,1)S(1)}, u32[]{:S(2)}, u32[]{:S(2)}) collective-permute-start(bf16[2,128,2048]{2,1,0:T(8,128)(2,1)S(1)} %get-tuple-element.40), channel_id=1, source_target_pairs={{0,16},{16,0},{1,17},{17,1},{2,18},{18,2},{3,19},{19,3},{4,20},{20... | collective-permute-start | bytes 3145736 | tf_op jit(solution)/shard_map/ppermute | solution.py:259
  182.7 14.0 %collective-permute-start.14 = (bf16[4,128,512]{2,1,0:T(8,128)(2,1)S(1)}, bf16[4,128,512]{2,1,0:T(8,128)(2,1)S(1)}, u32[]{:S(2)}, u32[]{:S(2)}) collective-permute-start(bf16[4,128,512]{2,1,0:T(8,128)(2,1)S(1)} %slice.37), channel_id=1, source_target_pairs={{64,0},{128,64},{192,128},{0,192},{65,1},{129,65},{193,129},{1,193... | collective-permute-start | bytes 1572872 | tf_op jit(solution)/shard_map/ppermute | solution.py:195
  184.9 14.4 %collective-permute-start.13 = (bf16[4,128,512]{2,1,0:T(8,128)(2,1)S(1)}, bf16[4,128,512]{2,1,0:T(8,128)(2,1)S(1)}, u32[]{:S(2)}, u32[]{:S(2)}) collective-permute-start(bf16[4,128,512]{2,1,0:T(8,128)(2,1)S(1)} %slice.36), channel_id=1, source_target_pairs={{0,64},{64,128},{128,192},{192,0},{1,65},{65,129},{129,193},{193,1... | collective-permute-start | bytes 1572872 | tf_op jit(solution)/shard_map/ppermute | solution.py:194
  202.9 3.6 %collective-permute-start.15 = (bf16[2,128,2048]{2,1,0:T(8,128)(2,1)S(1)}, bf16[2,128,2048]{2,1,0:T(8,128)(2,1)S(1)}, u32[]{:S(2)}, u32[]{:S(2)}) collective-permute-start(bf16[2,128,2048]{2,1,0:T(8,128)(2,1)S(1)} %get-tuple-element.47), channel_id=1, source_target_pairs={{0,16},{16,0},{1,17},{17,1},{2,18},{18,2},{3,19},{19,3},{4,20},{20... | collective-permute-start | bytes 3145736 | tf_op jit(solution)/shard_map/ppermute | solution.py:259
  204.1 13.5 %collective-permute-start.12 = (bf16[128,2048]{1,0:T(8,128)(2,1)S(1)}, bf16[128,2048]{1,0:T(8,128)(2,1)S(1)}, u32[]{:S(2)}, u32[]{:S(2)}) collective-permute-start(bf16[128,2048]{1,0:T(8,128)(2,1)S(1)} %fusion.3), channel_id=1, source_target_pairs={{0,32},{32,0},{1,33},{33,1},{2,34},{34,2},{3,35},{35,3},{4,36},{36... | collective-permute-start | bytes 1572872 | tf_op jit(solution)/shard_map/ppermute | solution.py:263
  206.5 22.3 %collective-permute-start.16 = (bf16[128,2048]{1,0:T(8,128)(2,1)S(1)}, bf16[128,2048]{1,0:T(8,128)(2,1)S(1)}, u32[]{:S(2)}, u32[]{:S(2)}) collective-permute-start(bf16[128,2048]{1,0:T(8,128)(2,1)S(1)} %fusion), channel_id=1, source_target_pairs={{0,32},{32,0},{1,33},{33,1},{2,34},{34,2},{3,35},{35,3},{4,36},{36... | collective-permute-start | bytes 1572872 | tf_op jit(solution)/shard_map/ppermute | solution.py:263
Sparse Core Ops, SparseCore 0:
  12.7 59.4 all-gather.2
  74.0 38.5 all-gather.4

commit v4 on v3

--- a/solution.py
+++ b/solution.py
@@ -16,8 +16,9 @@
 PAIRS = 16
 EXP2_SCALE = math.log2(math.e) / math.sqrt(HEAD_DIM)
 MASKED = -1e30
+Z_ORDER = (0, 7, 1, 6, 2, 5, 3, 4)
 HALVES = 2
-VMEM_LIMIT = 20 * 1024 * 1024
+VMEM_LIMIT = 56 * 1024 * 1024
 
 AXES = ("x", "yl", "core", "zh", "zl", "yh")
 BLK = ("x", "yl", "core")
@@ -128,29 +129,27 @@
             o_ref[4 * z + 2 * (g % 2) + g // 2] = out.astype(jnp.bfloat16)
 
 
-def projection_kernel(a_ref, own_ref, before_ref, after_ref, far0_ref, far1_ref, keep_ref, send_ref, other_ref, a_buf):
+def projection_kernel(a_ref, *refs):
+    w_refs, (keep_ref, send_ref, other_ref, a_buf) = refs[:-4], refs[-4:]
     core = lax.axis_index("core")
     yl = lax.axis_index("yl")
+    z_here = 2 * lax.axis_index("zh") + lax.axis_index("zl")
     x = lax.axis_index("x")
     for t in range(2):
         for u in range(2):
             source = 2 * (core if t == 0 else 1 - core) + (yl if u == 0 else 1 - yl)
             at = (2 * t + u) * ROWS
-            for z in range(Z):
-                a_buf[at : at + ROWS, z * ROWS : (z + 1) * ROWS] = a_ref[4 * z + source]
-    piece = own_ref.shape[-1]
-    half = (Z // 2) * ROWS
-
-    def product(rows, part):
-        return jnp.dot(a_buf[:, rows], part, preferred_element_type=jnp.float32)
-
-    for shift in (0, 3, 1, 2):
-        if shift == 2:
-            y = product(slice(0, half), far0_ref[...].reshape(half, piece))
-            y = y + product(slice(half, 2 * half), far1_ref[...].reshape(half, piece))
-        else:
-            ref = {0: own_ref, 3: before_ref, 1: after_ref}[shift]
-            y = product(slice(0, 2 * half), ref[...].reshape(2 * half, piece))
+            for k, shift in enumerate(Z_ORDER):
+                z = lax.rem(z_here + shift, Z)
+                a_buf[at : at + ROWS, k * ROWS : (k + 1) * ROWS] = a_ref[4 * z + source]
+    piece = keep_ref.shape[-1] // 4
+    for n, shift in enumerate((0, 3, 1, 2)):
+        y, at = None, 0
+        for ref in w_refs[3 * n : 3 * n + 3]:
+            depth = ref.shape[0] * ROWS
+            part = ref[...].reshape(depth, piece)
+            term = jnp.dot(a_buf[:, at : at + depth], part, preferred_element_type=jnp.float32)
+            y, at = (term if y is None else y + term), at + depth
         y = y.astype(jnp.bfloat16)
         cols = pl.ds(pl.multiple_of(lax.rem(x + shift, 4) * piece, piece), piece)
         keep_ref[:, cols] = y[0:ROWS]
@@ -159,13 +158,28 @@
             other_ref[u, :, cols] = y[(2 + u) * ROWS : (3 + u) * ROWS]
 
 
+def column_half(j, _):
+    return 0, 0, j
+
+
+def finish_kernel(*refs):
+    o_ref, piece = refs[-1], refs[0].shape[-1] // 4
+    for j in range(HALVES):
+        keep, arrived, last = refs[3 * j : 3 * j + 3]
+        for n in range(4):
+            cols = slice(n * piece, (n + 1) * piece)
+            total = keep[:, cols].astype(jnp.float32) + arrived[0, :, cols].astype(jnp.float32)
+            total = total + last[:, cols].astype(jnp.float32)
+            at = (HALVES * n + j) * piece
+            o_ref[:, at : at + piece] = total.astype(jnp.bfloat16)
+
+
 def body(queries, keys, values, doc_ids, out_weight):
     bf16 = jnp.bfloat16
     params = pltpu.CompilerParams(vmem_limit_bytes=VMEM_LIMIT)
     core = lax.axis_index("core")
     out_cols = out_weight.shape[1]
     cols = out_cols // HALVES
-    piece = cols // 4
     swap = [(0, 1), (1, 0)]
 
     packed = pl.pallas_call(
@@ -174,30 +188,29 @@
         compiler_params=params,
         name="pack_kv",
     )(keys, values, doc_ids.reshape(1, ROWS))
-    mine = [
-        lax.dynamic_slice(
-            out_weight, (core * ROWS, j * cols + lax.axis_index("x") * piece), (ROWS, piece)
-        )
-        for j in range(HALVES)
-    ]
-    mine, packed = lax.optimization_barrier((jnp.stack(mine), packed))
-    mine = lax.ppermute(mine, ("yl", "yh"), [(0, 0), (1, 2), (2, 1), (3, 3)])
-    right = [(i, (i + 1) % 4) for i in range(4)]
-    left = [((i + 1) % 4, i) for i in range(4)]
-    here = [lax.all_gather(mine[j], ("zh", "zl"), axis=0, tiled=False) for j in range(HALVES)]
-
-    def beside(j):
-        return lax.ppermute(here[j], "x", right), lax.ppermute(here[j], "x", left)
-
-    def beyond(before, after):
-        return (
-            lax.ppermute(before[: Z // 2], "x", right),
-            lax.ppermute(after[Z // 2 :], "x", left),
-        )
+    def ring(axis, size, step):
+        return lambda a: lax.ppermute(a, axis, [(i, (i + step) % size) for i in range(size)])
+
+    z_up, z_down = ring(("zh", "zl"), Z, 1), ring(("zh", "zl"), Z, -1)
+    x_up, x_down = ring("x", 4, 1), ring("x", 4, -1)
+
+    def beside(group):
+        return x_up(group), x_down(group)
+
+    piece = lax.dynamic_slice(
+        out_weight, (core * ROWS, lax.axis_index("x") * (out_cols // 4)), (ROWS, out_cols // 4)
+    )
+    piece = lax.ppermute(piece, ("yl", "yh"), [(0, 0), (1, 2), (2, 1), (3, 3)])
+    up1, down1 = z_up(piece), z_down(piece)
 
     own = lax.all_to_all(packed, ("zh", "zl"), 0, 0, tiled=True)
-    own, here[0] = lax.optimization_barrier((own, here[0]))
-    near0 = beside(0)
+    own, up1, down1 = lax.optimization_barrier((own, up1, down1))
+    group1 = jnp.stack([piece, up1, down1])
+    near1 = beside(group1)
+    up2, down2 = z_up(up1), z_down(down1)
+    up3, down3 = z_up(up2), z_down(down2)
+    group2 = jnp.stack([up2, down2, up3, down3])
+    group3 = z_up(up3)[None]
     other = lax.ppermute(own, "yh", swap)
     prev_own = lax.ppermute(own, BLK, [(i, i + 1) for i in range(15)])
     prev_other_0 = lax.ppermute(
@@ -210,9 +223,9 @@
     split = queries.reshape(ROWS, Z, GROUP * HEAD_DIM).transpose(1, 0, 2)
     query = lax.all_to_all(split, ("zh", "zl"), 0, 0, tiled=True)
 
-    query, near0, here[1] = lax.optimization_barrier((query, near0, here[1]))
-    far0 = beyond(*near0)
-    near1 = beside(1)
+    query, near1, group2, group3 = lax.optimization_barrier((query, near1, group2, group3))
+    far1 = x_up(near1[0])
+    near2, near3 = beside(group2), beside(group3)
     attn = pl.pallas_call(
         attention_kernel,
         out_shape=jax.ShapeDtypeStruct((4 * Z, ROWS, HEAD_DIM), bf16),
@@ -234,11 +247,15 @@
         name="attention",
     )(query, own, other, prev_own, prev_other_0, prev_other_1)
 
-    attn, far0 = lax.optimization_barrier((attn, far0))
+    attn, far1, near2, near3 = lax.optimization_barrier((attn, far1, near2, near3))
+    far2, far3 = x_down(near2[1]), x_up(near3[0])
+    weights = (
+        group1, group2, group3,
+        near1[0], near2[0], near3[0],
+        near1[1], near2[1], near3[1],
+        far1, far2, far3,
+    )
     spread = lax.all_to_all(attn, ("zh", "zl", "core", "yl"), 0, 0, tiled=True)
-    spread, near1 = lax.optimization_barrier((spread, near1))
-    far1 = beyond(*near1)
-    weights = ((here[0], *near0, *far0), (here[1], *near1, *far1))
     one = jax.ShapeDtypeStruct((ROWS, cols), bf16)
     two = jax.ShapeDtypeStruct((2, ROWS, cols), bf16)
     f32 = jnp.float32
@@ -246,6 +263,12 @@
     for j in range(HALVES):
         keep, send, theirs = pl.pallas_call(
             projection_kernel,
+            grid=(1,),
+            in_specs=[pl.BlockSpec(memory_space=pltpu.VMEM)]
+            + [
+                pl.BlockSpec((w.shape[0], ROWS, cols // 4), functools.partial(column_half, j))
+                for w in weights
+            ],
             out_shape=[one, one, two],
             scratch_shapes=[pltpu.VMEM((4 * ROWS, Z * ROWS), bf16)],
             compiler_params=params,
@@ -255,15 +278,18 @@
                 transcendentals=0,
             ),
             name="projection",
-        )(spread, *weights[j])
+        )(spread, *weights)
         arrived = lax.ppermute(theirs, "core", swap)
         send = (send.astype(f32) + arrived[1].astype(f32)).astype(bf16)
         if j + 1 < HALVES:
             spread, send = lax.optimization_barrier((spread, send))
-        parts.append((keep, arrived[0], lax.ppermute(send, "yl", swap)))
-    return jnp.concatenate(
-        [(k.astype(f32) + a.astype(f32) + m.astype(f32)).astype(bf16) for k, a, m in parts], axis=1
-    )
+        parts += (keep, arrived, lax.ppermute(send, "yl", swap))
+    return pl.pallas_call(
+        finish_kernel,
+        out_shape=jax.ShapeDtypeStruct((ROWS, out_cols), bf16),
+        compiler_params=params,
+        name="finish",
+    )(*parts)
 
 
 def solution(mesh):

time: 239 us -> 233 us (0.975)
  between operations: 13.6 us -> 0.21 us
  starting transfers between devices: 50.2 us -> 62.1 us
  local copies, waits for them, and re-layouts: 13.4 us -> 6.52 us
  Pallas kernels: 26.2 us -> 32 us
  waiting for transfers between devices: 132 us -> 128 us
    all_gather x2 -> x0, waiting for transfers between devices: 52.6 us -> none  [body(): lax.all_gather(mine[j], ('zh', 'zl'), axis=0, tiled=False)]
    ppermute x11 -> x19, waiting for transfers between devices: 59.6 us -> 104 us  [the longest x16 84.6 us: ring(): lax.ppermute(a, axis, [(i, (i + step) % size) for i in range(size)])]
    pallas_call x2 -> x3, Pallas kernels: 7.22 us -> 16.8 us  [the longest x2 13.3 us: body(): pl.pallas_call(projection_kernel, grid=(1,), in_specs=[pl.BlockSpec(memor...]
    pallas_call x1, Pallas kernels: 18 us -> 13.1 us  [body(): pl.pallas_call(attention_kernel, out_shape=jax.ShapeDtypeStruct((4 * Z, R...]
    ppermute x1, starting transfers between devices: 1.91 us -> 6.28 us  [body(): prev_own = lax.ppermute(own, BLK, [(i, i + 1) for i in range(15)])]
    ppermute x11 -> x19, starting transfers between devices: 16.9 us -> 21.2 us  [the longest x16 17.8 us: ring(): lax.ppermute(a, axis, [(i, (i + step) % size) for i in range(size)])]
    unnamed x25 -> x33, local copies, waits for them, and re-layouts: 8.09 us -> 4.24 us
    all_to_all x1, starting transfers between devices: 6.38 us -> 9.99 us  [body(): spread = lax.all_to_all(attn, ('zh', 'zl', 'core', 'yl'), 0, 0, tiled=True)]
  transfers between devices with their start and end apart: 22 -> 28, of which waited for: 11 -> 14; matrix products, arithmetic and copies ran while one was open for 2% -> 2% of each run, Pallas kernels for 8% -> 6%
where the time goes in v4:
time: 233 us; the launch traced here: 232 us
  waiting for transfers between devices  128 us (55%)
  starting transfers between devices  62.1 us (27%)
  Pallas kernels  32 us (14%)
  local copies, waits for them, and re-layouts  6.52 us (3%)
  other arithmetic  3.26 us (1%)
    ppermute x16, waiting for transfers between devices, ring(): lax.ppermute(a, axis, [(i, (i + step) % size) for i in range(size)])  84.6 us
    ppermute x2, waiting for transfers between devices, body(): parts += (keep, arrived, lax.ppermute(send, 'yl', swap))  19.2 us
    ppermute x16, starting transfers between devices, ring(): lax.ppermute(a, axis, [(i, (i + step) % size) for i in range(size)])  17.8 us
    all_to_all x1, waiting for transfers between devices, body(): own = lax.all_to_all(packed, ('zh', 'zl'), 0, 0, tiled=True)  17.5 us
    pallas_call x2, Pallas kernels, body(): pl.pallas_call(projection_kernel, grid=(1,), in_specs=[pl.BlockSpec(memor...  13.3 us
    pallas_call x1, Pallas kernels, body(): pl.pallas_call(attention_kernel, out_shape=jax.ShapeDtypeStruct((4 * Z, R...  13.1 us
    all_to_all x1, starting transfers between devices, body(): spread = lax.all_to_all(attn, ('zh', 'zl', 'core', 'yl'), 0, 0, tiled=True)  9.99 us
    all_to_all x1, starting transfers between devices, body(): own = lax.all_to_all(packed, ('zh', 'zl'), 0, 0, tiled=True)  9.01 us
  transfers between devices with their start and end apart: 28, of which 14 were waited for; matrix products, arithmetic and copies ran while one was open for 2% of the time, Pallas kernels for 6%

profile of v4, /device:TPU:1, one launch (start us, length us, event | category | flops | bytes accessed | tf_op | source)
XLA Modules:
  0.0 232.5 jit_solution(13607603948103255768)
XLA Ops:
  0.0 2.0 pack_kv.1
  2.0 9.0 %all-to-all-start.1 = ((bf16[8,144,256]{2,1,0:T(8,128)(2,1)}), bf16[8,144,256]{2,1,0:T(8,128)(2,1)}, u32[]{:S(2)}, u32[]{:S(2)}) async-start(bf16[8,144,256]{2,1,0:T(8,128)(2,1)} %pack_kv.1), calls=%async_computation.1 | async-start | bytes 1179648 | tf_op jit(solution)/shard_map/all_to_all | solution.py:206
  11.1 0.7 copy.6
  11.7 1.3 copy.7
  13.0 17.5 %all-to-all-done.1.own_ref = bf16[8,144,256]{2,1,0:T(8,128)(2,1)} async-done(((bf16[8,144,256]{2,1,0:T(8,128)(2,1)}), bf16[8,144,256]{2,1,0:T(8,128)(2,1)}, u32[]{:S(2)}, u32[]{:S(2)}) %all-to-all-start.1) | async-done | bytes 589856 | tf_op jit(solution)/shard_map/all_to_all | solution.py:206
  30.5 4.2 %all-to-all-start = ((bf16[8,128,512]{2,1,0:T(8,128)(2,1)}), bf16[8,128,512]{2,1,0:T(8,128)(2,1)}, u32[]{:S(2)}, u32[]{:S(2)}) async-start(bf16[8,128,512]{2,1,0:T(8,128)(2,1)} %bitcast.1), calls=%async_computation | async-start | bytes 2097152 | tf_op jit(solution)/shard_map/all_to_all | solution.py:224
  34.8 1.0 dynamic_slice.3
  35.7 0.7 collective-permute-start
  36.4 1.4 collective-permute-start.1
  37.8 1.4 collective-permute-start.2
  39.2 26.8 %collective-permute-done.1 = bf16[128,1024]{1,0:T(8,128)(2,1)S(1)} collective-permute-done((bf16[128,1024]{1,0:T(8,128)(2,1)S(1)}, bf16[128,1024]{1,0:T(8,128)(2,1)S(1)}, u32[]{:S(2)}, u32[]{:S(2)}) %collective-permute-start.1) | collective-permute-done | bytes 262176 | tf_op jit(solution)/shard_map/ppermute | solution.py:192
  66.0 0.0 collective-permute-done.2
  66.0 1.3 collective-permute-start.6
  67.2 0.2 collective-permute-start.5
  67.4 2.9 %collective-permute-start.10 = (bf16[8,144,256]{2,1,0:T(8,128)(2,1)}, bf16[8,144,256]{2,1,0:T(8,128)(2,1)}, u32[]{:S(2)}, u32[]{:S(2)}) collective-permute-start(bf16[8,144,256]{2,1,0:T(8,128)(2,1)} %all-to-all-done.1.own_ref), channel_id=1, source_target_pairs={{0,1},{1,0},{2,3},{3,2},{4,5},{5,4},{6,7},{7,6},{8,9},{9,8},{10,11... | collective-permute-start | bytes 1769480 | tf_op jit(solution)/shard_map/ppermute | solution.py:214
  70.3 0.1 pad_maximum_fusion.1.refs_0_
  70.4 1.3 collective-permute-start.3
  71.7 0.7 collective-permute-done.6
  72.4 2.5 %collective-permute-start.8 = (bf16[128,1024]{1,0:T(8,128)(2,1)S(1)}, bf16[128,1024]{1,0:T(8,128)(2,1)S(1)}, u32[]{:S(2)}, u32[]{:S(2)}) collective-permute-start(bf16[128,1024]{1,0:T(8,128)(2,1)S(1)} %collective-permute-done.6), channel_id=1, source_target_pairs={{0,14},{2,0},{4,2},{6,4},{8,6},{10,8},{12,10},{14,12},{1,15},{3,1}... | collective-permute-start | bytes 786440 | tf_op jit(solution)/shard_map/ppermute | solution.py:192
  74.9 0.0 collective-permute-done.5
  74.9 0.0 collective-permute-start.7
  74.9 2.5 %collective-permute-start.4 = (bf16[3,128,1024]{2,1,0:T(8,128)(2,1)S(1)}, bf16[3,128,1024]{2,1,0:T(8,128)(2,1)S(1)}, u32[]{:S(2)}, u32[]{:S(2)}) collective-permute-start(bf16[3,128,1024]{2,1,0:T(8,128)(2,1)S(1)} %pad_maximum_fusion.1.refs_0_), channel_id=1, source_target_pairs={{0,192},{64,0},{128,64},{192,128},{1,193},{65,1},{129,65},{193,129... | collective-permute-start | bytes 2359304 | tf_op jit(solution)/shard_map/ppermute | solution.py:192
  77.4 0.8 collective-permute-done.8
  78.2 6.3 %collective-permute-start.11 = (bf16[8,144,256]{2,1,0:T(8,128)(2,1)}, bf16[8,144,256]{2,1,0:T(8,128)(2,1)}, u32[]{:S(2)}, u32[]{:S(2)}) collective-permute-start(bf16[8,144,256]{2,1,0:T(8,128)(2,1)} %all-to-all-done.1.own_ref), channel_id=1, source_target_pairs={{0,16},{16,32},{32,48},{48,64},{64,80},{80,96},{96,112},{112,128},... | collective-permute-start | bytes 1769480 | tf_op jit(solution)/shard_map/ppermute | solution.py:215
  84.5 0.0 collective-permute-done.7
  84.5 5.9 %collective-permute-start.12 = (bf16[8,144,256]{2,1,0:T(8,128)(2,1)}, bf16[8,144,256]{2,1,0:T(8,128)(2,1)}, u32[]{:S(2)}, u32[]{:S(2)}) collective-permute-start(bf16[8,144,256]{2,1,0:T(8,128)(2,1)} %all-to-all-done.1.own_ref), channel_id=1, source_target_pairs={{16,33},{17,32},{48,65},{49,64},{80,97},{81,96},{112,129},{113,128... | collective-permute-start | bytes 1769480 | tf_op jit(solution)/shard_map/ppermute | solution.py:216
  90.4 1.3 collective-permute-start.13
  91.7 0.1 collective-permute-start.9
  91.8 0.9 copy-done.4
  92.6 0.1 pad_maximum_fusion.refs_1_
  92.8 0.0 collective-permute-done.4.refs_6_
  92.8 6.1 %collective-permute-done.9 = bf16[128,1024]{1,0:T(8,128)(2,1)S(1)} collective-permute-done((bf16[128,1024]{1,0:T(8,128)(2,1)S(1)}, bf16[128,1024]{1,0:T(8,128)(2,1)S(1)}, u32[]{:S(2)}, u32[]{:S(2)}) %collective-permute-start.9) | collective-permute-done | bytes 262176 | tf_op jit(solution)/shard_map/ppermute | solution.py:192
  98.9 0.0 all-to-all-done.q_ref
  98.9 1.4 collective-permute-start.15
  100.3 1.4 collective-permute-start.16
  101.7 0.1 collective-permute-start.17
  101.8 2.6 %collective-permute-start.18 = (bf16[1,128,1024]{2,1,0:T(8,128)(2,1)S(1)}, bf16[1,128,1024]{2,1,0:T(8,128)(2,1)S(1)}, u32[]{:S(2)}, u32[]{:S(2)}) collective-permute-start(bf16[1,128,1024]{2,1,0:T(8,128)(2,1)S(1)} %bitcast.23), channel_id=1, source_target_pairs={{0,192},{64,0},{128,64},{192,128},{1,193},{65,1},{129,65},{193,129... | collective-permute-start | bytes 786440 | tf_op jit(solution)/shard_map/ppermute | solution.py:192
  104.4 0.0 collective-permute-start.14
  104.4 13.1 %attention.1 = bf16[32,128,128]{2,1,0:T(8,128)(2,1)} custom-call(bf16[8,128,512]{2,1,0:T(8,128)(2,1)} %all-to-all-done.q_ref, bf16[8,144,256]{2,1,0:T(8,128)(2,1)} %all-to-all-done.1.own_ref, bf16[8,144,256]{2,1,0:T(8,128)(2,1)} %collective-permute-done.10.oth_ref, bf16[8,144,256]{2,1,0:T(8,128)(2,1)} %collective-permute-done.11.pown_ref, ...), custom_call_target="tpu_custom_call" | custom-call | flops 16000000000 | bytes 6000000 | tf_op jit(solution)/shard_map/attention/pallas_call | solution.py:229
  117.5 10.2 %collective-permute-done.17.refs_5_ = bf16[1,128,1024]{2,1,0:T(8,128)(2,1)S(1)} collective-permute-done((bf16[1,128,1024]{2,1,0:T(8,128)(2,1)S(1)}, bf16[1,128,1024]{2,1,0:T(8,128)(2,1)S(1)}, u32[]{:S(2)}, u32[]{:S(2)}) %collective-permute-start.17) | collective-permute-done | bytes 262176 | tf_op jit(solution)/shard_map/ppermute | solution.py:192
  127.7 0.0 collective-permute-done.18.refs_8_
  127.7 16.8 %collective-permute-done.14.refs_9_ = bf16[3,128,1024]{2,1,0:T(8,128)(2,1)S(1)} collective-permute-done((bf16[3,128,1024]{2,1,0:T(8,128)(2,1)}, bf16[3,128,1024]{2,1,0:T(8,128)(2,1)S(1)}, u32[]{:S(2)}, u32[]{:S(2)}) %collective-permute-start.14) | collective-permute-done | bytes 786464 | tf_op jit(solution)/shard_map/ppermute | solution.py:192
  144.6 0.9 copy-done.6
  145.5 10.0 %all-to-all-start.2 = ((bf16[32,128,128]{2,1,0:T(8,128)(2,1)}), bf16[32,128,128]{2,1,0:T(8,128)(2,1)S(1)}, u32[]{:S(2)}, u32[]{:S(2)}) async-start(bf16[32,128,128]{2,1,0:T(8,128)(2,1)} %attention.1), calls=%async_computation.2 | async-start | bytes 2097152 | tf_op jit(solution)/shard_map/all_to_all | solution.py:258
  155.5 1.8 collective-permute-start.19
  157.2 8.6 %collective-permute-done.20.refs_11_ = bf16[1,128,1024]{2,1,0:T(8,128)(2,1)S(1)} collective-permute-done((bf16[1,128,1024]{2,1,0:T(8,128)(2,1)S(1)}, bf16[1,128,1024]{2,1,0:T(8,128)(2,1)S(1)}, u32[]{:S(2)}, u32[]{:S(2)}) %collective-permute-start.20) | collective-permute-done | bytes 262176 | tf_op jit(solution)/shard_map/ppermute | solution.py:192
  165.8 14.6 %collective-permute-done.19.refs_10_ = bf16[4,128,1024]{2,1,0:T(8,128)(2,1)} collective-permute-done((bf16[4,128,1024]{2,1,0:T(8,128)(2,1)}, bf16[4,128,1024]{2,1,0:T(8,128)(2,1)}, u32[]{:S(2)}, u32[]{:S(2)}) %collective-permute-start.19) | collective-permute-done | bytes 1048608 | tf_op jit(solution)/shard_map/ppermute | solution.py:192
  180.4 3.5 %all-to-all-done.2.a_ref = bf16[32,128,128]{2,1,0:T(8,128)(2,1)S(1)} async-done(((bf16[32,128,128]{2,1,0:T(8,128)(2,1)}), bf16[32,128,128]{2,1,0:T(8,128)(2,1)S(1)}, u32[]{:S(2)}, u32[]{:S(2)}) %all-to-all-start.2) | async-done | bytes 1048608 | tf_op jit(solution)/shard_map/all_to_all | solution.py:258
  183.9 0.0 copy-start.1
  183.9 1.0 copy-done.1
  184.9 6.7 %projection.2 = (bf16[128,2048]{1,0:T(8,128)(2,1)}, bf16[128,2048]{1,0:T(8,128)(2,1)}, bf16[2,128,2048]{2,1,0:T(8,128)(2,1)}) custom-call(bf16[32,128,128]{2,1,0:T(8,128)(2,1)} %copy-done.1, bf16[3,128,1024]{2,1,0:T(8,128)(2,1)} %copy-done.2, bf16[4,128,1024]{2,1,0:T(8,128)(2,1)} %copy-done, bf16[1,128,1024]{2,1,0:T(8,128)(2,1)} %bitcast.24, ...), custom_call_target="tpu_custom_call" | custom-call | flops 2147483648 | bytes 6291456 | tf_op jit(solution)/shard_map/projection/pallas_call | solution.py:264
  191.5 0.9 collective-permute-start.21
  192.5 2.5 %collective-permute-done.21.refs_1_ = bf16[2,128,2048]{2,1,0:T(8,128)(2,1)S(1)} collective-permute-done((bf16[2,128,2048]{2,1,0:T(8,128)(2,1)}, bf16[2,128,2048]{2,1,0:T(8,128)(2,1)S(1)}, u32[]{:S(2)}, u32[]{:S(2)}) %collective-permute-start.21) | collective-permute-done | bytes 1048608 | tf_op jit(solution)/shard_map/ppermute | solution.py:282
  195.0 1.5 fusion.1
  196.5 6.7 %projection.3 = (bf16[128,2048]{1,0:T(8,128)(2,1)}, bf16[128,2048]{1,0:T(8,128)(2,1)}, bf16[2,128,2048]{2,1,0:T(8,128)(2,1)}) custom-call(bf16[32,128,128]{2,1,0:T(8,128)(2,1)} %copy-done.1, bf16[3,128,1024]{2,1,0:T(8,128)(2,1)} %copy-done.2, bf16[4,128,1024]{2,1,0:T(8,128)(2,1)} %copy-done, bf16[1,128,1024]{2,1,0:T(8,128)(2,1)} %bitcast.25, ...), custom_call_target="tpu_custom_call" | custom-call | flops 2147483648 | bytes 6291456 | tf_op jit(solution)/shard_map/projection/pallas_call | solution.py:264
  203.2 0.4 collective-permute-start.23
  203.5 1.3 collective-permute-start.22
  204.9 1.2 collective-permute-done.23.refs_4_
  206.0 1.5 fusion
  207.6 1.4 collective-permute-start.24
  209.0 7.9 %collective-permute-done.22.refs_2_ = bf16[128,2048]{1,0:T(8,128)(2,1)S(1)} collective-permute-done((bf16[128,2048]{1,0:T(8,128)(2,1)S(1)}, bf16[128,2048]{1,0:T(8,128)(2,1)S(1)}, u32[]{:S(2)}, u32[]{:S(2)}) %collective-permute-start.22) | collective-permute-done | bytes 524320 | tf_op jit(solution)/shard_map/ppermute | solution.py:286
  216.9 11.2 %collective-permute-done.24.refs_5_ = bf16[128,2048]{1,0:T(8,128)(2,1)S(1)} collective-permute-done((bf16[128,2048]{1,0:T(8,128)(2,1)S(1)}, bf16[128,2048]{1,0:T(8,128)(2,1)S(1)}, u32[]{:S(2)}, u32[]{:S(2)}) %collective-permute-start.24) | collective-permute-done | bytes 524320 | tf_op jit(solution)/shard_map/ppermute | solution.py:286
  228.2 0.8 copy-done.15
  229.0 3.5 %finish.1 = bf16[128,4096]{1,0:T(8,128)(2,1)} custom-call(bf16[128,2048]{1,0:T(8,128)(2,1)} %get-tuple-element.41.refs_0_, bf16[2,128,2048]{2,1,0:T(8,128)(2,1)} %copy-done.7, bf16[128,2048]{1,0:T(8,128)(2,1)} %copy-done.14, bf16[128,2048]{1,0:T(8,128)(2,1)} %get-tuple-element.46.refs_3_, bf16[2,128,2048]{2,1,0:T(8,128)(2,1)} %copy-done.8, ...), custom_call_target="tpu_custom_call" | custom-call | tf_op jit(solution)/shard_map/finish/pallas_call | solution.py:287
  (36 shorter events, 0.1 us)
Async XLA Ops:
  0.0 11.1 %copy-start.13 = (bf16[128,4096]{1,0:T(8,128)(2,1)S(1)}, bf16[128,4096]{1,0:T(8,128)(2,1)}, u32[]{:S(2)}) copy-start(bf16[128,4096]{1,0:T(8,128)(2,1)} %param.5) | copy-start | bytes 3145732
  2.0 28.5 %all-to-all-start.1 = ((bf16[8,144,256]{2,1,0:T(8,128)(2,1)}), bf16[8,144,256]{2,1,0:T(8,128)(2,1)}, u32[]{:S(2)}, u32[]{:S(2)}) async-start(bf16[8,144,256]{2,1,0:T(8,128)(2,1)} %pack_kv.1), calls=%async_computation.1 | async-start | bytes 1179648 | tf_op jit(solution)/shard_map/all_to_all | solution.py:206
  30.5 68.4 %all-to-all-start = ((bf16[8,128,512]{2,1,0:T(8,128)(2,1)}), bf16[8,128,512]{2,1,0:T(8,128)(2,1)}, u32[]{:S(2)}, u32[]{:S(2)}) async-start(bf16[8,128,512]{2,1,0:T(8,128)(2,1)} %bitcast.1), calls=%async_computation | async-start | bytes 2097152 | tf_op jit(solution)/shard_map/all_to_all | solution.py:224
  35.7 0.7 collective-permute-start
  36.4 29.5 %collective-permute-start.1 = (bf16[128,1024]{1,0:T(8,128)(2,1)S(1)}, bf16[128,1024]{1,0:T(8,128)(2,1)S(1)}, u32[]{:S(2)}, u32[]{:S(2)}) collective-permute-start(bf16[128,1024]{1,0:T(8,128)(2,1)S(1)} %collective-permute-done), channel_id=1, source_target_pairs={{0,2},{2,4},{4,6},{6,8},{8,10},{10,12},{12,14},{14,0},{1,3},{3,5},... | collective-permute-start | bytes 786440 | tf_op jit(solution)/shard_map/ppermute | solution.py:192
  37.8 28.1 %collective-permute-start.2 = (bf16[128,1024]{1,0:T(8,128)(2,1)S(1)}, bf16[128,1024]{1,0:T(8,128)(2,1)S(1)}, u32[]{:S(2)}, u32[]{:S(2)}) collective-permute-start(bf16[128,1024]{1,0:T(8,128)(2,1)S(1)} %collective-permute-done), channel_id=1, source_target_pairs={{0,14},{2,0},{4,2},{6,4},{8,6},{10,8},{12,10},{14,12},{1,15},{3,1}... | collective-permute-start | bytes 786440 | tf_op jit(solution)/shard_map/ppermute | solution.py:192
  66.0 6.5 %collective-permute-start.6 = (bf16[128,1024]{1,0:T(8,128)(2,1)S(1)}, bf16[128,1024]{1,0:T(8,128)(2,1)S(1)}, u32[]{:S(2)}, u32[]{:S(2)}) collective-permute-start(bf16[128,1024]{1,0:T(8,128)(2,1)S(1)} %collective-permute-done.2), channel_id=1, source_target_pairs={{0,14},{2,0},{4,2},{6,4},{8,6},{10,8},{12,10},{14,12},{1,15},{3,1}... | collective-permute-start | bytes 786440 | tf_op jit(solution)/shard_map/ppermute | solution.py:192
  67.2 7.7 %collective-permute-start.5 = (bf16[128,1024]{1,0:T(8,128)(2,1)S(1)}, bf16[128,1024]{1,0:T(8,128)(2,1)S(1)}, u32[]{:S(2)}, u32[]{:S(2)}) collective-permute-start(bf16[128,1024]{1,0:T(8,128)(2,1)S(1)} %collective-permute-done.1), channel_id=1, source_target_pairs={{0,2},{2,4},{4,6},{6,8},{8,10},{10,12},{12,14},{14,0},{1,3},{3,5},... | collective-permute-start | bytes 786440 | tf_op jit(solution)/shard_map/ppermute | solution.py:192
  67.4 23.0 %collective-permute-start.10 = (bf16[8,144,256]{2,1,0:T(8,128)(2,1)}, bf16[8,144,256]{2,1,0:T(8,128)(2,1)}, u32[]{:S(2)}, u32[]{:S(2)}) collective-permute-start(bf16[8,144,256]{2,1,0:T(8,128)(2,1)} %all-to-all-done.1.own_ref), channel_id=1, source_target_pairs={{0,1},{1,0},{2,3},{3,2},{4,5},{5,4},{6,7},{7,6},{8,9},{9,8},{10,11... | collective-permute-start | bytes 1769480 | tf_op jit(solution)/shard_map/ppermute | solution.py:214
  70.4 47.1 %copy-start.2 = (bf16[3,128,1024]{2,1,0:T(8,128)(2,1)}, bf16[3,128,1024]{2,1,0:T(8,128)(2,1)S(1)}, u32[]{:S(2)}) copy-start(bf16[3,128,1024]{2,1,0:T(8,128)(2,1)S(1)} %pad_maximum_fusion.1.refs_0_) | copy-start | bytes 2359300
  70.4 21.2 %collective-permute-start.3 = (bf16[3,128,1024]{2,1,0:T(8,128)(2,1)S(1)}, bf16[3,128,1024]{2,1,0:T(8,128)(2,1)S(1)}, u32[]{:S(2)}, u32[]{:S(2)}) collective-permute-start(bf16[3,128,1024]{2,1,0:T(8,128)(2,1)S(1)} %pad_maximum_fusion.1.refs_0_), channel_id=1, source_target_pairs={{0,64},{64,128},{128,192},{192,0},{1,65},{65,129},{129,193},{193,1... | collective-permute-start | bytes 2359304 | tf_op jit(solution)/shard_map/ppermute | solution.py:192
  72.4 5.8 %collective-permute-start.8 = (bf16[128,1024]{1,0:T(8,128)(2,1)S(1)}, bf16[128,1024]{1,0:T(8,128)(2,1)S(1)}, u32[]{:S(2)}, u32[]{:S(2)}) collective-permute-start(bf16[128,1024]{1,0:T(8,128)(2,1)S(1)} %collective-permute-done.6), channel_id=1, source_target_pairs={{0,14},{2,0},{4,2},{6,4},{8,6},{10,8},{12,10},{14,12},{1,15},{3,1}... | collective-permute-start | bytes 786440 | tf_op jit(solution)/shard_map/ppermute | solution.py:192
  74.9 9.6 %collective-permute-start.7 = (bf16[128,1024]{1,0:T(8,128)(2,1)S(1)}, bf16[128,1024]{1,0:T(8,128)(2,1)S(1)}, u32[]{:S(2)}, u32[]{:S(2)}) collective-permute-start(bf16[128,1024]{1,0:T(8,128)(2,1)S(1)} %collective-permute-done.5), channel_id=1, source_target_pairs={{0,2},{2,4},{4,6},{6,8},{8,10},{10,12},{12,14},{14,0},{1,3},{3,5},... | collective-permute-start | bytes 786440 | tf_op jit(solution)/shard_map/ppermute | solution.py:192
  74.9 17.9 %collective-permute-start.4 = (bf16[3,128,1024]{2,1,0:T(8,128)(2,1)S(1)}, bf16[3,128,1024]{2,1,0:T(8,128)(2,1)S(1)}, u32[]{:S(2)}, u32[]{:S(2)}) collective-permute-start(bf16[3,128,1024]{2,1,0:T(8,128)(2,1)S(1)} %pad_maximum_fusion.1.refs_0_), channel_id=1, source_target_pairs={{0,192},{64,0},{128,64},{192,128},{1,193},{65,1},{129,65},{193,129... | collective-permute-start | bytes 2359304 | tf_op jit(solution)/shard_map/ppermute | solution.py:192
  78.2 23.5 %collective-permute-start.11 = (bf16[8,144,256]{2,1,0:T(8,128)(2,1)}, bf16[8,144,256]{2,1,0:T(8,128)(2,1)}, u32[]{:S(2)}, u32[]{:S(2)}) collective-permute-start(bf16[8,144,256]{2,1,0:T(8,128)(2,1)} %all-to-all-done.1.own_ref), channel_id=1, source_target_pairs={{0,16},{16,32},{32,48},{48,64},{64,80},{80,96},{96,112},{112,128},... | collective-permute-start | bytes 1769480 | tf_op jit(solution)/shard_map/ppermute | solution.py:215
  84.5 17.3 %collective-permute-start.12 = (bf16[8,144,256]{2,1,0:T(8,128)(2,1)}, bf16[8,144,256]{2,1,0:T(8,128)(2,1)}, u32[]{:S(2)}, u32[]{:S(2)}) collective-permute-start(bf16[8,144,256]{2,1,0:T(8,128)(2,1)} %all-to-all-done.1.own_ref), channel_id=1, source_target_pairs={{16,33},{17,32},{48,65},{49,64},{80,97},{81,96},{112,129},{113,128... | collective-permute-start | bytes 1769480 | tf_op jit(solution)/shard_map/ppermute | solution.py:216
  90.4 14.0 %collective-permute-start.13 = (bf16[8,144,256]{2,1,0:T(8,128)(2,1)}, bf16[8,144,256]{2,1,0:T(8,128)(2,1)}, u32[]{:S(2)}, u32[]{:S(2)}) collective-permute-start(bf16[8,144,256]{2,1,0:T(8,128)(2,1)} %collective-permute-done.10.oth_ref), channel_id=1, source_target_pairs={{0,16},{1,17},{2,18},{3,19},{4,20},{5,21},{6,22},{7,23},{8,24},{9,... | collective-permute-start | bytes 1769480 | tf_op jit(solution)/shard_map/ppermute | solution.py:221
  91.7 1.0 copy-start.4
  91.7 7.2 %collective-permute-start.9 = (bf16[128,1024]{1,0:T(8,128)(2,1)S(1)}, bf16[128,1024]{1,0:T(8,128)(2,1)S(1)}, u32[]{:S(2)}, u32[]{:S(2)}) collective-permute-start(bf16[128,1024]{1,0:T(8,128)(2,1)S(1)} %collective-permute-done.7), channel_id=1, source_target_pairs={{0,2},{2,4},{4,6},{6,8},{8,10},{10,12},{12,14},{14,0},{1,3},{3,5},... | collective-permute-start | bytes 786440 | tf_op jit(solution)/shard_map/ppermute | solution.py:192
  92.8 24.8 %copy-start = (bf16[4,128,1024]{2,1,0:T(8,128)(2,1)}, bf16[4,128,1024]{2,1,0:T(8,128)(2,1)S(1)}, u32[]{:S(2)}) copy-start(bf16[4,128,1024]{2,1,0:T(8,128)(2,1)S(1)} %pad_maximum_fusion.refs_1_) | copy-start | bytes 3145732
  92.8 6.1 %copy-start.5 = (bf16[3,128,1024]{2,1,0:T(8,128)(2,1)}, bf16[3,128,1024]{2,1,0:T(8,128)(2,1)S(1)}, u32[]{:S(2)}) copy-start(bf16[3,128,1024]{2,1,0:T(8,128)(2,1)S(1)} %collective-permute-done.4.refs_6_) | copy-start | bytes 2359300
  98.9 18.6 %copy-start.9 = (bf16[128,1024]{1,0:T(8,128)(2,1)}, bf16[128,1024]{1,0:T(8,128)(2,1)S(1)}, u32[]{:S(2)}) copy-start(bf16[128,1024]{1,0:T(8,128)(2,1)S(1)} %collective-permute-done.9) | copy-start | bytes 786436
  98.9 45.6 %collective-permute-start.15 = (bf16[4,128,1024]{2,1,0:T(8,128)(2,1)S(1)}, bf16[4,128,1024]{2,1,0:T(8,128)(2,1)S(1)}, u32[]{:S(2)}, u32[]{:S(2)}) collective-permute-start(bf16[4,128,1024]{2,1,0:T(8,128)(2,1)S(1)} %pad_maximum_fusion.refs_1_), channel_id=1, source_target_pairs={{0,64},{64,128},{128,192},{192,0},{1,65},{65,129},{129,193},{193,1... | collective-permute-start | bytes 3145736 | tf_op jit(solution)/shard_map/ppermute | solution.py:192
  100.3 45.1 %collective-permute-start.16 = (bf16[4,128,1024]{2,1,0:T(8,128)(2,1)S(1)}, bf16[4,128,1024]{2,1,0:T(8,128)(2,1)}, u32[]{:S(2)}, u32[]{:S(2)}) collective-permute-start(bf16[4,128,1024]{2,1,0:T(8,128)(2,1)S(1)} %pad_maximum_fusion.refs_1_), channel_id=1, source_target_pairs={{0,192},{64,0},{128,64},{192,128},{1,193},{65,1},{129,65},{193,129... | collective-permute-start | bytes 3145736 | tf_op jit(solution)/shard_map/ppermute | solution.py:192
  101.7 26.0 %collective-permute-start.17 = (bf16[1,128,1024]{2,1,0:T(8,128)(2,1)S(1)}, bf16[1,128,1024]{2,1,0:T(8,128)(2,1)S(1)}, u32[]{:S(2)}, u32[]{:S(2)}) collective-permute-start(bf16[1,128,1024]{2,1,0:T(8,128)(2,1)S(1)} %bitcast.22), channel_id=1, source_target_pairs={{0,64},{64,128},{128,192},{192,0},{1,65},{65,129},{129,193},{193,1... | collective-permute-start | bytes 786440 | tf_op jit(solution)/shard_map/ppermute | solution.py:192
  101.8 25.9 %collective-permute-start.18 = (bf16[1,128,1024]{2,1,0:T(8,128)(2,1)S(1)}, bf16[1,128,1024]{2,1,0:T(8,128)(2,1)S(1)}, u32[]{:S(2)}, u32[]{:S(2)}) collective-permute-start(bf16[1,128,1024]{2,1,0:T(8,128)(2,1)S(1)} %bitcast.23), channel_id=1, source_target_pairs={{0,192},{64,0},{128,64},{192,128},{1,193},{65,1},{129,65},{193,129... | collective-permute-start | bytes 786440 | tf_op jit(solution)/shard_map/ppermute | solution.py:192
  104.4 40.2 %collective-permute-start.14 = (bf16[3,128,1024]{2,1,0:T(8,128)(2,1)}, bf16[3,128,1024]{2,1,0:T(8,128)(2,1)S(1)}, u32[]{:S(2)}, u32[]{:S(2)}) collective-permute-start(bf16[3,128,1024]{2,1,0:T(8,128)(2,1)} %copy-done.4), channel_id=1, source_target_pairs={{0,64},{64,128},{128,192},{192,0},{1,65},{65,129},{129,193},{193,1... | collective-permute-start | bytes 2359304 | tf_op jit(solution)/shard_map/ppermute | solution.py:192
  127.7 56.2 %copy-start.10 = (bf16[1,128,1024]{2,1,0:T(8,128)(2,1)}, bf16[1,128,1024]{2,1,0:T(8,128)(2,1)S(1)}, u32[]{:S(2)}) copy-start(bf16[1,128,1024]{2,1,0:T(8,128)(2,1)S(1)} %collective-permute-done.17.refs_5_) | copy-start | bytes 786436
  127.7 16.8 %copy-start.11 = (bf16[1,128,1024]{2,1,0:T(8,128)(2,1)}, bf16[1,128,1024]{2,1,0:T(8,128)(2,1)S(1)}, u32[]{:S(2)}) copy-start(bf16[1,128,1024]{2,1,0:T(8,128)(2,1)S(1)} %collective-permute-done.18.refs_8_) | copy-start | bytes 786436
  144.5 0.9 copy-start.6
  145.5 38.4 %copy-start.3 = (bf16[4,128,1024]{2,1,0:T(8,128)(2,1)}, bf16[4,128,1024]{2,1,0:T(8,128)(2,1)S(1)}, u32[]{:S(2)}) copy-start(bf16[4,128,1024]{2,1,0:T(8,128)(2,1)S(1)} %collective-permute-done.15.refs_4_) | copy-start | bytes 3145732
  145.5 38.4 %all-to-all-start.2 = ((bf16[32,128,128]{2,1,0:T(8,128)(2,1)}), bf16[32,128,128]{2,1,0:T(8,128)(2,1)S(1)}, u32[]{:S(2)}, u32[]{:S(2)}) async-start(bf16[32,128,128]{2,1,0:T(8,128)(2,1)} %attention.1), calls=%async_computation.2 | async-start | bytes 2097152 | tf_op jit(solution)/shard_map/all_to_all | solution.py:258
  155.5 24.9 %collective-permute-start.19 = (bf16[4,128,1024]{2,1,0:T(8,128)(2,1)}, bf16[4,128,1024]{2,1,0:T(8,128)(2,1)}, u32[]{:S(2)}, u32[]{:S(2)}) collective-permute-start(bf16[4,128,1024]{2,1,0:T(8,128)(2,1)} %collective-permute-done.16.refs_7_), channel_id=1, source_target_pairs={{0,192},{64,0},{128,64},{192,128},{1,193},{65,1},{129,65},{193,129... | collective-permute-start | bytes 3145736 | tf_op jit(solution)/shard_map/ppermute | solution.py:192
  157.2 8.6 %collective-permute-start.20 = (bf16[1,128,1024]{2,1,0:T(8,128)(2,1)S(1)}, bf16[1,128,1024]{2,1,0:T(8,128)(2,1)S(1)}, u32[]{:S(2)}, u32[]{:S(2)}) collective-permute-start(bf16[1,128,1024]{2,1,0:T(8,128)(2,1)S(1)} %collective-permute-done.17.refs_5_), channel_id=1, source_target_pairs={{0,64},{64,128},{128,192},{192,0},{1,65},{65,129},{129,193},{193,1... | collective-permute-start | bytes 786440 | tf_op jit(solution)/shard_map/ppermute | solution.py:192
  165.8 18.1 %copy-start.12 = (bf16[1,128,1024]{2,1,0:T(8,128)(2,1)}, bf16[1,128,1024]{2,1,0:T(8,128)(2,1)S(1)}, u32[]{:S(2)}) copy-start(bf16[1,128,1024]{2,1,0:T(8,128)(2,1)S(1)} %collective-permute-done.20.refs_11_) | copy-start | bytes 786436
  183.9 1.0 copy-start.1
  191.5 3.4 %collective-permute-start.21 = (bf16[2,128,2048]{2,1,0:T(8,128)(2,1)}, bf16[2,128,2048]{2,1,0:T(8,128)(2,1)S(1)}, u32[]{:S(2)}, u32[]{:S(2)}) collective-permute-start(bf16[2,128,2048]{2,1,0:T(8,128)(2,1)} %get-tuple-element.42), channel_id=1, source_target_pairs={{0,16},{16,0},{1,17},{17,1},{2,18},{18,2},{3,19},{19,3},{4,20},{20... | collective-permute-start | bytes 3145736 | tf_op jit(solution)/shard_map/ppermute | solution.py:282
  195.0 8.2 %copy-start.7 = (bf16[2,128,2048]{2,1,0:T(8,128)(2,1)}, bf16[2,128,2048]{2,1,0:T(8,128)(2,1)S(1)}, u32[]{:S(2)}) copy-start(bf16[2,128,2048]{2,1,0:T(8,128)(2,1)S(1)} %collective-permute-done.21.refs_1_) | copy-start | bytes 3145732
  203.2 2.9 %collective-permute-start.23 = (bf16[2,128,2048]{2,1,0:T(8,128)(2,1)}, bf16[2,128,2048]{2,1,0:T(8,128)(2,1)S(1)}, u32[]{:S(2)}, u32[]{:S(2)}) collective-permute-start(bf16[2,128,2048]{2,1,0:T(8,128)(2,1)} %get-tuple-element.47), channel_id=1, source_target_pairs={{0,16},{16,0},{1,17},{17,1},{2,18},{18,2},{3,19},{19,3},{4,20},{20... | collective-permute-start | bytes 3145736 | tf_op jit(solution)/shard_map/ppermute | solution.py:282
  203.5 13.4 %collective-permute-start.22 = (bf16[128,2048]{1,0:T(8,128)(2,1)S(1)}, bf16[128,2048]{1,0:T(8,128)(2,1)S(1)}, u32[]{:S(2)}, u32[]{:S(2)}) collective-permute-start(bf16[128,2048]{1,0:T(8,128)(2,1)S(1)} %fusion.1), channel_id=1, source_target_pairs={{0,32},{32,0},{1,33},{33,1},{2,34},{34,2},{3,35},{35,3},{4,36},{36... | collective-permute-start | bytes 1572872 | tf_op jit(solution)/shard_map/ppermute | solution.py:286
  206.0 22.1 %copy-start.8 = (bf16[2,128,2048]{2,1,0:T(8,128)(2,1)}, bf16[2,128,2048]{2,1,0:T(8,128)(2,1)S(1)}, u32[]{:S(2)}) copy-start(bf16[2,128,2048]{2,1,0:T(8,128)(2,1)S(1)} %collective-permute-done.23.refs_4_) | copy-start | bytes 3145732
  207.6 20.6 %collective-permute-start.24 = (bf16[128,2048]{1,0:T(8,128)(2,1)S(1)}, bf16[128,2048]{1,0:T(8,128)(2,1)S(1)}, u32[]{:S(2)}, u32[]{:S(2)}) collective-permute-start(bf16[128,2048]{1,0:T(8,128)(2,1)S(1)} %fusion), channel_id=1, source_target_pairs={{0,32},{32,0},{1,33},{33,1},{2,34},{34,2},{3,35},{35,3},{4,36},{36... | collective-permute-start | bytes 1572872 | tf_op jit(solution)/shard_map/ppermute | solution.py:286
  216.9 11.2 %copy-start.14 = (bf16[128,2048]{1,0:T(8,128)(2,1)}, bf16[128,2048]{1,0:T(8,128)(2,1)S(1)}, u32[]{:S(2)}) copy-start(bf16[128,2048]{1,0:T(8,128)(2,1)S(1)} %collective-permute-done.22.refs_2_) | copy-start | bytes 1572868
  228.1 0.8 copy-start.15

commit v5 on v4

--- a/solution.py
+++ b/solution.py
@@ -16,9 +16,7 @@
 PAIRS = 16
 EXP2_SCALE = math.log2(math.e) / math.sqrt(HEAD_DIM)
 MASKED = -1e30
-Z_ORDER = (0, 7, 1, 6, 2, 5, 3, 4)
-HALVES = 2
-VMEM_LIMIT = 56 * 1024 * 1024
+MIB = 1024 * 1024
 
 AXES = ("x", "yl", "core", "zh", "zl", "yh")
 BLK = ("x", "yl", "core")
@@ -129,88 +127,80 @@
             o_ref[4 * z + 2 * (g % 2) + g // 2] = out.astype(jnp.bfloat16)
 
 
-def projection_kernel(a_ref, *refs):
+def projection_kernel(spread_ref, *refs):
     w_refs, (keep_ref, send_ref, other_ref, a_buf) = refs[:-4], refs[-4:]
     core = lax.axis_index("core")
     yl = lax.axis_index("yl")
-    z_here = 2 * lax.axis_index("zh") + lax.axis_index("zl")
-    x = lax.axis_index("x")
     for t in range(2):
         for u in range(2):
             source = 2 * (core if t == 0 else 1 - core) + (yl if u == 0 else 1 - yl)
             at = (2 * t + u) * ROWS
-            for k, shift in enumerate(Z_ORDER):
-                z = lax.rem(z_here + shift, Z)
-                a_buf[at : at + ROWS, k * ROWS : (k + 1) * ROWS] = a_ref[4 * z + source]
-    piece = keep_ref.shape[-1] // 4
-    for n, shift in enumerate((0, 3, 1, 2)):
-        y, at = None, 0
-        for ref in w_refs[3 * n : 3 * n + 3]:
-            depth = ref.shape[0] * ROWS
-            part = ref[...].reshape(depth, piece)
-            term = jnp.dot(a_buf[:, at : at + depth], part, preferred_element_type=jnp.float32)
-            y, at = (term if y is None else y + term), at + depth
+            for z in range(Z):
+                a_buf[at : at + ROWS, z * ROWS : (z + 1) * ROWS] = spread_ref[4 * z + source]
+    at = 0
+    for ref in w_refs:
+        y, done = None, 0
+        for part in ref if isinstance(ref, tuple) else (ref,):
+            depth = part.shape[0] * ROWS
+            term = jnp.dot(
+                a_buf[:, done : done + depth],
+                part[...].reshape(depth, part.shape[-1]),
+                preferred_element_type=jnp.float32,
+            )
+            y, done = (term if y is None else y + term), done + depth
         y = y.astype(jnp.bfloat16)
-        cols = pl.ds(pl.multiple_of(lax.rem(x + shift, 4) * piece, piece), piece)
+        cols = slice(at, at + y.shape[1])
+        at += y.shape[1]
         keep_ref[:, cols] = y[0:ROWS]
         send_ref[:, cols] = y[ROWS : 2 * ROWS]
         for u in range(2):
             other_ref[u, :, cols] = y[(2 + u) * ROWS : (3 + u) * ROWS]
 
 
-def column_half(j, _):
-    return 0, 0, j
+def far_kernel(spread_ref, low_ref, high_ref, *refs):
+    projection_kernel(spread_ref, (low_ref, high_ref), *refs)
 
 
 def finish_kernel(*refs):
-    o_ref, piece = refs[-1], refs[0].shape[-1] // 4
-    for j in range(HALVES):
-        keep, arrived, last = refs[3 * j : 3 * j + 3]
-        for n in range(4):
-            cols = slice(n * piece, (n + 1) * piece)
-            total = keep[:, cols].astype(jnp.float32) + arrived[0, :, cols].astype(jnp.float32)
-            total = total + last[:, cols].astype(jnp.float32)
-            at = (HALVES * n + j) * piece
-            o_ref[:, at : at + piece] = total.astype(jnp.bfloat16)
+    o_ref = refs[-1]
+    piece = o_ref.shape[-1] // 4
+    x = lax.axis_index("x")
+    for n, shift in enumerate((0, 3, 1, 2)):
+        keep, arrived, last = refs[0:3] if n < 3 else refs[3:6]
+        cols = slice((n % 3) * piece, (n % 3 + 1) * piece)
+        total = keep[:, cols].astype(jnp.float32) + arrived[0, :, cols].astype(jnp.float32)
+        total = total + last[:, cols].astype(jnp.float32)
+        at = pl.multiple_of(lax.rem(x + shift, 4) * piece, piece)
+        o_ref[:, pl.ds(at, piece)] = total.astype(jnp.bfloat16)
 
 
 def body(queries, keys, values, doc_ids, out_weight):
     bf16 = jnp.bfloat16
-    params = pltpu.CompilerParams(vmem_limit_bytes=VMEM_LIMIT)
+    def params(mib):
+        return pltpu.CompilerParams(vmem_limit_bytes=mib * MIB)
+
     core = lax.axis_index("core")
     out_cols = out_weight.shape[1]
-    cols = out_cols // HALVES
     swap = [(0, 1), (1, 0)]
 
     packed = pl.pallas_call(
         pack_kernel,
         out_shape=jax.ShapeDtypeStruct((Z, ROWS + 16, 2 * HEAD_DIM), bf16),
-        compiler_params=params,
+        compiler_params=params(8),
         name="pack_kv",
     )(keys, values, doc_ids.reshape(1, ROWS))
     def ring(axis, size, step):
         return lambda a: lax.ppermute(a, axis, [(i, (i + step) % size) for i in range(size)])
 
-    z_up, z_down = ring(("zh", "zl"), Z, 1), ring(("zh", "zl"), Z, -1)
     x_up, x_down = ring("x", 4, 1), ring("x", 4, -1)
-
-    def beside(group):
-        return x_up(group), x_down(group)
 
     piece = lax.dynamic_slice(
         out_weight, (core * ROWS, lax.axis_index("x") * (out_cols // 4)), (ROWS, out_cols // 4)
     )
     piece = lax.ppermute(piece, ("yl", "yh"), [(0, 0), (1, 2), (2, 1), (3, 3)])
-    up1, down1 = z_up(piece), z_down(piece)
-
+    piece, packed = lax.optimization_barrier((piece, packed))
     own = lax.all_to_all(packed, ("zh", "zl"), 0, 0, tiled=True)
-    own, up1, down1 = lax.optimization_barrier((own, up1, down1))
-    group1 = jnp.stack([piece, up1, down1])
-    near1 = beside(group1)
-    up2, down2 = z_up(up1), z_down(down1)
-    up3, down3 = z_up(up2), z_down(down2)
-    group2 = jnp.stack([up2, down2, up3, down3])
-    group3 = z_up(up3)[None]
+    here = lax.all_gather(piece, ("zh", "zl"), axis=0, tiled=False)
     other = lax.ppermute(own, "yh", swap)
     prev_own = lax.ppermute(own, BLK, [(i, i + 1) for i in range(15)])
     prev_other_0 = lax.ppermute(
@@ -222,10 +212,8 @@
 
     split = queries.reshape(ROWS, Z, GROUP * HEAD_DIM).transpose(1, 0, 2)
     query = lax.all_to_all(split, ("zh", "zl"), 0, 0, tiled=True)
-
-    query, near1, group2, group3 = lax.optimization_barrier((query, near1, group2, group3))
-    far1 = x_up(near1[0])
-    near2, near3 = beside(group2), beside(group3)
+    query, here = lax.optimization_barrier((query, here))
+    before, after = x_up(here), x_down(here)
     attn = pl.pallas_call(
         attention_kernel,
         out_shape=jax.ShapeDtypeStruct((4 * Z, ROWS, HEAD_DIM), bf16),
@@ -240,38 +228,31 @@
             pltpu.VMEM((GROUP * ROWS, ROWS), jnp.float32),
             pltpu.VMEM((GROUP * ROWS, 2 * HEAD_DIM), jnp.float32),
         ],
-        compiler_params=params,
+        compiler_params=params(24),
         cost_estimate=pl.CostEstimate(
             flops=16_000_000_000, bytes_accessed=6_000_000, transcendentals=4_000_000
         ),
         name="attention",
     )(query, own, other, prev_own, prev_other_0, prev_other_1)
 
-    attn, far1, near2, near3 = lax.optimization_barrier((attn, far1, near2, near3))
-    far2, far3 = x_down(near2[1]), x_up(near3[0])
-    weights = (
-        group1, group2, group3,
-        near1[0], near2[0], near3[0],
-        near1[1], near2[1], near3[1],
-        far1, far2, far3,
-    )
     spread = lax.all_to_all(attn, ("zh", "zl", "core", "yl"), 0, 0, tiled=True)
-    one = jax.ShapeDtypeStruct((ROWS, cols), bf16)
-    two = jax.ShapeDtypeStruct((2, ROWS, cols), bf16)
+    far_low, far_high = x_up(before[: Z // 2]), x_down(after[Z // 2 :])
     f32 = jnp.float32
     parts = []
-    for j in range(HALVES):
+    for kernel, weights, blocks in (
+        (projection_kernel, (here, before, after), 3),
+        (far_kernel, (far_low, far_high), 1),
+    ):
+        cols = blocks * out_cols // 4
+        if parts:
+            spread, parts[2] = lax.optimization_barrier((spread, parts[2]))
+            parts[2] = lax.ppermute(parts[2], "yl", swap)
+        one = jax.ShapeDtypeStruct((ROWS, cols), bf16)
         keep, send, theirs = pl.pallas_call(
-            projection_kernel,
-            grid=(1,),
-            in_specs=[pl.BlockSpec(memory_space=pltpu.VMEM)]
-            + [
-                pl.BlockSpec((w.shape[0], ROWS, cols // 4), functools.partial(column_half, j))
-                for w in weights
-            ],
-            out_shape=[one, one, two],
+            kernel,
+            out_shape=[one, one, jax.ShapeDtypeStruct((2, ROWS, cols), bf16)],
             scratch_shapes=[pltpu.VMEM((4 * ROWS, Z * ROWS), bf16)],
-            compiler_params=params,
+            compiler_params=params(40),
             cost_estimate=pl.CostEstimate(
                 flops=2 * 4 * ROWS * Z * ROWS * cols,
                 bytes_accessed=2 * Z * ROWS * cols + 8 * ROWS * cols,
@@ -280,14 +261,12 @@
             name="projection",
         )(spread, *weights)
         arrived = lax.ppermute(theirs, "core", swap)
-        send = (send.astype(f32) + arrived[1].astype(f32)).astype(bf16)
-        if j + 1 < HALVES:
-            spread, send = lax.optimization_barrier((spread, send))
-        parts += (keep, arrived, lax.ppermute(send, "yl", swap))
+        parts += [keep, arrived, (send.astype(f32) + arrived[1].astype(f32)).astype(bf16)]
+    parts[5] = lax.ppermute(parts[5], "yl", swap)
     return pl.pallas_call(
         finish_kernel,
         out_shape=jax.ShapeDtypeStruct((ROWS, out_cols), bf16),
-        compiler_params=params,
+        compiler_params=params(16),
         name="finish",
     )(*parts)
 

time: 233 us -> 207 us (0.89)
  waiting for transfers between devices: 128 us -> 83.7 us
  blocking collectives: 0 us -> 35 us
  starting transfers between devices: 62.1 us -> 42.7 us
  between operations: 0.21 us -> 13.5 us
  Pallas kernels: 32 us -> 24.3 us
  other arithmetic: 3.26 us -> 0.25 us
    ppermute x16 -> x4, waiting for transfers between devices: 84.6 us -> 25.3 us  [ring(): lax.ppermute(a, axis, [(i, (i + step) % size) for i in range(size)])]
    all_to_all x0 -> x1, blocking collectives: none -> 35 us  [body(): spread = lax.all_to_all(attn, ('zh', 'zl', 'core', 'yl'), 0, 0, tiled=True)]
    all_to_all x1, waiting for transfers between devices: 0.01 us -> 18.5 us  [body(): query = lax.all_to_all(split, ('zh', 'zl'), 0, 0, tiled=True)]
    ppermute x16 -> x4, starting transfers between devices: 17.8 us -> 5.35 us  [ring(): lax.ppermute(a, axis, [(i, (i + step) % size) for i in range(size)])]
    all_to_all x1 -> x0, starting transfers between devices: 9.99 us -> none  [body(): spread = lax.all_to_all(attn, ('zh', 'zl', 'core', 'yl'), 0, 0, tiled=True)]
    pallas_call x2, Pallas kernels: 13.3 us -> 4.69 us  [body(): pl.pallas_call(kernel, out_shape=[one, one, jax.ShapeDtypeStruct((2, ROWS...]
    ppermute x1, starting transfers between devices: 2.91 us -> 9.2 us  [body(): other = lax.ppermute(own, 'yh', swap)]
    pallas_call x1, Pallas kernels: 13.1 us -> 17.3 us  [body(): pl.pallas_call(attention_kernel, out_shape=jax.ShapeDtypeStruct((4 * Z, R...]
  transfers between devices with their start and end apart: 28 -> 16, of which waited for: 14 -> 8; matrix products, arithmetic and copies ran while one was open for 2% -> 1% of each run, Pallas kernels for 6% -> 9%
where the time goes in v5:
time: 207 us; the launch traced here: 206 us
  waiting for transfers between devices  83.7 us (40%)
  starting transfers between devices  42.7 us (21%)
  blocking collectives  35 us (17%)
  Pallas kernels  24.3 us (12%)
  between operations  13.5 us (7%)
  local copies, waits for them, and re-layouts  6.36 us (3%)
    all_to_all x1, blocking collectives, body(): spread = lax.all_to_all(attn, ('zh', 'zl', 'core', 'yl'), 0, 0, tiled=True)  35 us
    ppermute x4, waiting for transfers between devices, ring(): lax.ppermute(a, axis, [(i, (i + step) % size) for i in range(size)])  25.3 us
    ppermute x1, waiting for transfers between devices, body(): parts[5] = lax.ppermute(parts[5], 'yl', swap)  21.7 us
    all_to_all x1, waiting for transfers between devices, body(): query = lax.all_to_all(split, ('zh', 'zl'), 0, 0, tiled=True)  18.5 us
    pallas_call x1, Pallas kernels, body(): pl.pallas_call(attention_kernel, out_shape=jax.ShapeDtypeStruct((4 * Z, R...  17.3 us
    all_to_all x1, waiting for transfers between devices, body(): own = lax.all_to_all(packed, ('zh', 'zl'), 0, 0, tiled=True)  16.6 us
    ppermute x1, starting transfers between devices, body(): other = lax.ppermute(own, 'yh', swap)  9.2 us
    all_to_all x1, starting transfers between devices, body(): own = lax.all_to_all(packed, ('zh', 'zl'), 0, 0, tiled=True)  9.04 us
  transfers between devices with their start and end apart: 16, of which 8 were waited for; matrix products, arithmetic and copies ran while one was open for 1% of the time, Pallas kernels for 9%

profile of v5, /device:TPU:1, one launch (start us, length us, event | category | flops | bytes accessed | tf_op | source)
XLA Modules:
  0.0 205.7 jit_solution(7531070906854931525)
XLA Ops:
  6.5 0.0 all-gather.3.cloned.1.call-start
  6.5 1.0 dynamic_slice.3
  7.5 0.7 collective-permute-start
  8.2 0.0 copy-start
  8.2 0.9 copy-done
  9.1 0.0 copy-start.1
  9.1 0.9 copy-done.1
  10.1 0.0 copy-start.2
  10.1 0.7 copy-done.2
  10.8 0.0 copy-start.4
  10.8 0.9 pack_kv.1
  11.7 0.0 collective-permute-done
  11.7 0.0 copy-start.5
  11.7 0.7 copy-done.5
  12.4 0.0 all-gather.3.cloned.1.call-update
  12.4 9.0 %all-to-all-start.1 = ((bf16[8,144,256]{2,1,0:T(8,128)(2,1)}), bf16[8,144,256]{2,1,0:T(8,128)(2,1)S(1)}, u32[]{:S(2)}, u32[]{:S(2)}) async-start(bf16[8,144,256]{2,1,0:T(8,128)(2,1)} %pack_kv.1), calls=%async_computation.1 | async-start | bytes 1179648 | tf_op jit(solution)/shard_map/all_to_all | solution.py:202
  21.5 0.0 copy-done.4
  21.5 0.7 copy.6
  22.2 1.3 copy.7
  23.5 16.6 %all-to-all-done.1.own_ref = bf16[8,144,256]{2,1,0:T(8,128)(2,1)S(1)} async-done(((bf16[8,144,256]{2,1,0:T(8,128)(2,1)}), bf16[8,144,256]{2,1,0:T(8,128)(2,1)S(1)}, u32[]{:S(2)}, u32[]{:S(2)}) %all-to-all-start.1) | async-done | bytes 589856 | tf_op jit(solution)/shard_map/all_to_all | solution.py:202
  40.0 3.6 %all-to-all-start = ((bf16[8,128,512]{2,1,0:T(8,128)(2,1)}), bf16[8,128,512]{2,1,0:T(8,128)(2,1)S(1)}, u32[]{:S(2)}, u32[]{:S(2)}) async-start(bf16[8,128,512]{2,1,0:T(8,128)(2,1)} %bitcast.1), calls=%async_computation | async-start | bytes 2097152 | tf_op jit(solution)/shard_map/all_to_all | solution.py:214
  43.6 9.2 %collective-permute-start.1 = (bf16[8,144,256]{2,1,0:T(8,128)(2,1)S(1)}, bf16[8,144,256]{2,1,0:T(8,128)(2,1)S(1)}, u32[]{:S(2)}, u32[]{:S(2)}) collective-permute-start(bf16[8,144,256]{2,1,0:T(8,128)(2,1)S(1)} %all-to-all-done.1.own_ref), channel_id=1, source_target_pairs={{0,1},{1,0},{2,3},{3,2},{4,5},{5,4},{6,7},{7,6},{8,9},{9,8},{10,11... | collective-permute-start | bytes 1769480 | tf_op jit(solution)/shard_map/ppermute | solution.py:204
  52.8 4.0 %collective-permute-start.2 = (bf16[8,144,256]{2,1,0:T(8,128)(2,1)S(1)}, bf16[8,144,256]{2,1,0:T(8,128)(2,1)S(1)}, u32[]{:S(2)}, u32[]{:S(2)}) collective-permute-start(bf16[8,144,256]{2,1,0:T(8,128)(2,1)S(1)} %all-to-all-done.1.own_ref), channel_id=1, source_target_pairs={{0,16},{16,32},{32,48},{48,64},{64,80},{80,96},{96,112},{112,128},... | collective-permute-start | bytes 1769480 | tf_op jit(solution)/shard_map/ppermute | solution.py:205
  56.8 4.6 %collective-permute-start.3 = (bf16[8,144,256]{2,1,0:T(8,128)(2,1)S(1)}, bf16[8,144,256]{2,1,0:T(8,128)(2,1)S(1)}, u32[]{:S(2)}, u32[]{:S(2)}) collective-permute-start(bf16[8,144,256]{2,1,0:T(8,128)(2,1)S(1)} %all-to-all-done.1.own_ref), channel_id=1, source_target_pairs={{16,33},{17,32},{48,65},{49,64},{80,97},{81,96},{112,129},{113,128... | collective-permute-start | bytes 1769480 | tf_op jit(solution)/shard_map/ppermute | solution.py:206
  61.4 1.3 collective-permute-done.1.oth_ref
  62.7 1.3 collective-permute-start.4
  64.0 18.5 %all-to-all-done.q_ref = bf16[8,128,512]{2,1,0:T(8,128)(2,1)S(1)} async-done(((bf16[8,128,512]{2,1,0:T(8,128)(2,1)}), bf16[8,128,512]{2,1,0:T(8,128)(2,1)S(1)}, u32[]{:S(2)}, u32[]{:S(2)}) %all-to-all-start) | async-done | bytes 1048608 | tf_op jit(solution)/shard_map/all_to_all | solution.py:214
  82.5 0.0 all-gather.3.cloned.1.call-done
  82.5 1.2 collective-permute-start.5
  83.7 1.4 collective-permute-start.6
  85.1 0.0 collective-permute-done.2.pown_ref
  85.1 0.0 collective-permute-done.3.poth0_ref
  85.1 0.0 collective-permute-done.4.poth1_ref
  85.2 17.3 %attention.1 = bf16[32,128,128]{2,1,0:T(8,128)(2,1)S(1)} custom-call(bf16[8,128,512]{2,1,0:T(8,128)(2,1)S(1)} %all-to-all-done.q_ref, bf16[8,144,256]{2,1,0:T(8,128)(2,1)S(1)} %all-to-all-done.1.own_ref, bf16[8,144,256]{2,1,0:T(8,128)(2,1)S(1)} %collective-permute-done.1.oth_ref, bf16[8,144,256]{2,1,0:T(8,128)(2,1)S(1)} %collective-permute-done.2.pown_ref, ...), custom_call_target="tpu_custom_call" | custom-call | flops 16000000000 | bytes 6000000 | tf_op jit(solution)/shard_map/attention/pallas_call | solution.py:217
  102.5 0.0 copy-start.3
  102.5 35.0 %all_to_all.15.spread_ref = bf16[32,128,128]{2,1,0:T(8,128)(2,1)S(1)} all-to-all(bf16[32,128,128]{2,1,0:T(8,128)(2,1)S(1)} %attention.1), channel_id=1, replica_groups=mesh['x'=4,'yl'=2,'core'=2,'zh'=4,'zl'=2,'yh'=2] {'zh','zl','core','yl'}, dimensions={0} | all-to-all | bytes 2097152 | tf_op jit(solution)/shard_map/all_to_all | solution.py:238
  137.4 0.0 collective-permute-done.5.refs_1_
  137.4 0.0 collective-permute-done.6.refs_2_
  137.4 0.0 copy-done.3
  137.4 3.4 %projection.2 = (bf16[128,3072]{1,0:T(8,128)(2,1)S(1)}, bf16[128,3072]{1,0:T(8,128)(2,1)S(1)}, bf16[2,128,3072]{2,1,0:T(8,128)(2,1)S(1)}) custom-call(bf16[32,128,128]{2,1,0:T(8,128)(2,1)S(1)} %all_to_all.15.spread_ref, bf16[8,128,1024]{2,1,0:T(8,128)(2,1)S(1)} %bitcast.17, bf16[8,128,1024]{2,1,0:T(8,128)(2,1)S(1)} %collective-permute-done.5.refs_1_, ...), custom_call_target="tpu_custom_call" | custom-call | flops 3221225472 | bytes 9437184 | tf_op jit(solution)/shard_map/projection/pallas_call | solution.py:251
  140.9 1.0 collective-permute-start.7
  141.9 0.1 slice.18
  141.9 2.6 %collective-permute-start.10 = (bf16[4,128,1024]{2,1,0:T(8,128)(2,1)S(1)}, bf16[4,128,1024]{2,1,0:T(8,128)(2,1)S(1)}, u32[]{:S(2)}, u32[]{:S(2)}) collective-permute-start(bf16[4,128,1024]{2,1,0:T(8,128)(2,1)S(1)} %slice.18), channel_id=1, source_target_pairs={{0,192},{64,0},{128,64},{192,128},{1,193},{65,1},{129,65},{193,129... | collective-permute-start | bytes 3145736 | tf_op jit(solution)/shard_map/ppermute | solution.py:193
  144.5 0.1 slice.17
  144.6 0.1 collective-permute-start.9
  144.7 0.2 collective-permute-done.7.refs_1_
  144.9 0.2 fusion
  145.1 22.0 %collective-permute-done.10.high_ref = bf16[4,128,1024]{2,1,0:T(8,128)(2,1)S(1)} collective-permute-done((bf16[4,128,1024]{2,1,0:T(8,128)(2,1)S(1)}, bf16[4,128,1024]{2,1,0:T(8,128)(2,1)S(1)}, u32[]{:S(2)}, u32[]{:S(2)}) %collective-permute-start.10) | collective-permute-done | bytes 1048608 | tf_op jit(solution)/shard_map/ppermute | solution.py:193
  167.1 3.2 %collective-permute-done.9.low_ref = bf16[4,128,1024]{2,1,0:T(8,128)(2,1)S(1)} collective-permute-done((bf16[4,128,1024]{2,1,0:T(8,128)(2,1)S(1)}, bf16[4,128,1024]{2,1,0:T(8,128)(2,1)S(1)}, u32[]{:S(2)}, u32[]{:S(2)}) %collective-permute-start.9) | collective-permute-done | bytes 1048608 | tf_op jit(solution)/shard_map/ppermute | solution.py:193
  170.4 1.3 projection.3
  171.6 1.2 collective-permute-start.11
  172.8 1.4 collective-permute-start.8
  174.2 0.2 collective-permute-done.11.refs_4_
  174.4 0.1 fusion.1
  174.4 1.4 collective-permute-start.12
  175.9 21.7 %collective-permute-done.12.refs_5_ = bf16[128,1024]{1,0:T(8,128)(2,1)S(1)} collective-permute-done((bf16[128,1024]{1,0:T(8,128)(2,1)S(1)}, bf16[128,1024]{1,0:T(8,128)(2,1)S(1)}, u32[]{:S(2)}, u32[]{:S(2)}) %collective-permute-start.12) | collective-permute-done | bytes 262176 | tf_op jit(solution)/shard_map/ppermute | solution.py:265
  197.5 0.0 collective-permute-done.8.refs_2_
  197.6 1.3 finish.1
Async XLA Ops:
  6.5 75.9 %all-gather.3.cloned.1.call-start = ((), (), s32[]{:S(2)}) async-start(), calls=%async_computation.3 | async-start | bytes 2359296 | tf_op jit(solution)/shard_map/all_gather | solution.py:203
  7.5 4.2 %collective-permute-start = (bf16[128,1024]{1,0:T(8,128)(2,1)S(1)}, bf16[128,1024]{1,0:T(8,128)(2,1)S(1)}, u32[]{:S(2)}, u32[]{:S(2)}) collective-permute-start(bf16[128,1024]{1,0:T(8,128)(2,1)S(1)} %dynamic_slice.3), channel_id=1, source_target_pairs={{0,0},{1,32},{32,1},{33,33},{2,2},{3,34},{34,3},{35,35},{4,4},{5,3... | collective-permute-start | bytes 786440 | tf_op jit(solution)/shard_map/ppermute | solution.py:200
  8.2 1.0 copy-start
  9.1 0.9 copy-start.1
  10.1 0.7 copy-start.2
  10.8 10.7 %copy-start.4 = (bf16[128,4096]{1,0:T(8,128)(2,1)S(1)}, bf16[128,4096]{1,0:T(8,128)(2,1)}, u32[]{:S(2)}) copy-start(bf16[128,4096]{1,0:T(8,128)(2,1)} %param.5) | copy-start | bytes 3145732
  11.7 0.7 copy-start.5
  12.4 27.6 %all-to-all-start.1 = ((bf16[8,144,256]{2,1,0:T(8,128)(2,1)}), bf16[8,144,256]{2,1,0:T(8,128)(2,1)S(1)}, u32[]{:S(2)}, u32[]{:S(2)}) async-start(bf16[8,144,256]{2,1,0:T(8,128)(2,1)} %pack_kv.1), calls=%async_computation.1 | async-start | bytes 1179648 | tf_op jit(solution)/shard_map/all_to_all | solution.py:202
  40.0 42.4 %all-to-all-start = ((bf16[8,128,512]{2,1,0:T(8,128)(2,1)}), bf16[8,128,512]{2,1,0:T(8,128)(2,1)S(1)}, u32[]{:S(2)}, u32[]{:S(2)}) async-start(bf16[8,128,512]{2,1,0:T(8,128)(2,1)} %bitcast.1), calls=%async_computation | async-start | bytes 2097152 | tf_op jit(solution)/shard_map/all_to_all | solution.py:214
  43.6 19.0 %collective-permute-start.1 = (bf16[8,144,256]{2,1,0:T(8,128)(2,1)S(1)}, bf16[8,144,256]{2,1,0:T(8,128)(2,1)S(1)}, u32[]{:S(2)}, u32[]{:S(2)}) collective-permute-start(bf16[8,144,256]{2,1,0:T(8,128)(2,1)S(1)} %all-to-all-done.1.own_ref), channel_id=1, source_target_pairs={{0,1},{1,0},{2,3},{3,2},{4,5},{5,4},{6,7},{7,6},{8,9},{9,8},{10,11... | collective-permute-start | bytes 1769480 | tf_op jit(solution)/shard_map/ppermute | solution.py:204
  52.8 32.3 %collective-permute-start.2 = (bf16[8,144,256]{2,1,0:T(8,128)(2,1)S(1)}, bf16[8,144,256]{2,1,0:T(8,128)(2,1)S(1)}, u32[]{:S(2)}, u32[]{:S(2)}) collective-permute-start(bf16[8,144,256]{2,1,0:T(8,128)(2,1)S(1)} %all-to-all-done.1.own_ref), channel_id=1, source_target_pairs={{0,16},{16,32},{32,48},{48,64},{64,80},{80,96},{96,112},{112,128},... | collective-permute-start | bytes 1769480 | tf_op jit(solution)/shard_map/ppermute | solution.py:205
  56.8 28.4 %collective-permute-start.3 = (bf16[8,144,256]{2,1,0:T(8,128)(2,1)S(1)}, bf16[8,144,256]{2,1,0:T(8,128)(2,1)S(1)}, u32[]{:S(2)}, u32[]{:S(2)}) collective-permute-start(bf16[8,144,256]{2,1,0:T(8,128)(2,1)S(1)} %all-to-all-done.1.own_ref), channel_id=1, source_target_pairs={{16,33},{17,32},{48,65},{49,64},{80,97},{81,96},{112,129},{113,128... | collective-permute-start | bytes 1769480 | tf_op jit(solution)/shard_map/ppermute | solution.py:206
  62.7 22.5 %collective-permute-start.4 = (bf16[8,144,256]{2,1,0:T(8,128)(2,1)S(1)}, bf16[8,144,256]{2,1,0:T(8,128)(2,1)}, u32[]{:S(2)}, u32[]{:S(2)}) collective-permute-start(bf16[8,144,256]{2,1,0:T(8,128)(2,1)S(1)} %collective-permute-done.1.oth_ref), channel_id=1, source_target_pairs={{0,16},{1,17},{2,18},{3,19},{4,20},{5,21},{6,22},{7,23},{8,24},{9,... | collective-permute-start | bytes 1769480 | tf_op jit(solution)/shard_map/ppermute | solution.py:211
  82.5 55.0 %collective-permute-start.5 = (bf16[8,128,1024]{2,1,0:T(8,128)(2,1)}, bf16[8,128,1024]{2,1,0:T(8,128)(2,1)S(1)}, u32[]{:S(2)}, u32[]{:S(2)}) collective-permute-start(bf16[8,128,1024]{2,1,0:T(8,128)(2,1)} %bitcast.15), channel_id=1, source_target_pairs={{0,64},{64,128},{128,192},{192,0},{1,65},{65,129},{129,193},{193,1... | collective-permute-start | bytes 6291464 | tf_op jit(solution)/shard_map/ppermute | solution.py:193
  83.7 53.7 %collective-permute-start.6 = (bf16[8,128,1024]{2,1,0:T(8,128)(2,1)}, bf16[8,128,1024]{2,1,0:T(8,128)(2,1)S(1)}, u32[]{:S(2)}, u32[]{:S(2)}) collective-permute-start(bf16[8,128,1024]{2,1,0:T(8,128)(2,1)} %bitcast.16), channel_id=1, source_target_pairs={{0,192},{64,0},{128,64},{192,128},{1,193},{65,1},{129,65},{193,129... | collective-permute-start | bytes 6291464 | tf_op jit(solution)/shard_map/ppermute | solution.py:193
  102.5 35.0 %copy-start.3 = (bf16[1024,1024]{1,0:T(8,128)(2,1)S(1)}, bf16[1024,1024]{1,0:T(8,128)(2,1)}, u32[]{:S(2)}) copy-start(bf16[1024,1024]{1,0:T(8,128)(2,1)} %all-gather.3.cloned.1.call-done) | copy-start | bytes 6291460
  140.9 4.0 %collective-permute-start.7 = (bf16[2,128,3072]{2,1,0:T(8,128)(2,1)S(1)}, bf16[2,128,3072]{2,1,0:T(8,128)(2,1)S(1)}, u32[]{:S(2)}, u32[]{:S(2)}) collective-permute-start(bf16[2,128,3072]{2,1,0:T(8,128)(2,1)S(1)} %get-tuple-element.22), channel_id=1, source_target_pairs={{0,16},{16,0},{1,17},{17,1},{2,18},{18,2},{3,19},{19,3},{4,20},{20... | collective-permute-start | bytes 4718600 | tf_op jit(solution)/shard_map/ppermute | solution.py:263
  141.9 25.2 %collective-permute-start.10 = (bf16[4,128,1024]{2,1,0:T(8,128)(2,1)S(1)}, bf16[4,128,1024]{2,1,0:T(8,128)(2,1)S(1)}, u32[]{:S(2)}, u32[]{:S(2)}) collective-permute-start(bf16[4,128,1024]{2,1,0:T(8,128)(2,1)S(1)} %slice.18), channel_id=1, source_target_pairs={{0,192},{64,0},{128,64},{192,128},{1,193},{65,1},{129,65},{193,129... | collective-permute-start | bytes 3145736 | tf_op jit(solution)/shard_map/ppermute | solution.py:193
  144.6 25.7 %collective-permute-start.9 = (bf16[4,128,1024]{2,1,0:T(8,128)(2,1)S(1)}, bf16[4,128,1024]{2,1,0:T(8,128)(2,1)S(1)}, u32[]{:S(2)}, u32[]{:S(2)}) collective-permute-start(bf16[4,128,1024]{2,1,0:T(8,128)(2,1)S(1)} %slice.17), channel_id=1, source_target_pairs={{0,64},{64,128},{128,192},{192,0},{1,65},{65,129},{129,193},{193,1... | collective-permute-start | bytes 3145736 | tf_op jit(solution)/shard_map/ppermute | solution.py:193
  171.6 2.7 %collective-permute-start.11 = (bf16[2,128,1024]{2,1,0:T(8,128)(2,1)S(1)}, bf16[2,128,1024]{2,1,0:T(8,128)(2,1)S(1)}, u32[]{:S(2)}, u32[]{:S(2)}) collective-permute-start(bf16[2,128,1024]{2,1,0:T(8,128)(2,1)S(1)} %get-tuple-element.27), channel_id=1, source_target_pairs={{0,16},{16,0},{1,17},{17,1},{2,18},{18,2},{3,19},{19,3},{4,20},{20... | collective-permute-start | bytes 1572872 | tf_op jit(solution)/shard_map/ppermute | solution.py:263
  172.8 24.7 %collective-permute-start.8 = (bf16[128,3072]{1,0:T(8,128)(2,1)S(1)}, bf16[128,3072]{1,0:T(8,128)(2,1)S(1)}, u32[]{:S(2)}, u32[]{:S(2)}) collective-permute-start(bf16[128,3072]{1,0:T(8,128)(2,1)S(1)} %fusion), channel_id=1, source_target_pairs={{0,32},{32,0},{1,33},{33,1},{2,34},{34,2},{3,35},{35,3},{4,36},{36... | collective-permute-start | bytes 2359304 | tf_op jit(solution)/shard_map/ppermute | solution.py:249
  174.4 23.1 %collective-permute-start.12 = (bf16[128,1024]{1,0:T(8,128)(2,1)S(1)}, bf16[128,1024]{1,0:T(8,128)(2,1)S(1)}, u32[]{:S(2)}, u32[]{:S(2)}) collective-permute-start(bf16[128,1024]{1,0:T(8,128)(2,1)S(1)} %fusion.1), channel_id=1, source_target_pairs={{0,32},{32,0},{1,33},{33,1},{2,34},{34,2},{3,35},{35,3},{4,36},{36... | collective-permute-start | bytes 786440 | tf_op jit(solution)/shard_map/ppermute | solution.py:265
Sparse Core Ops, SparseCore 0:
  12.6 68.9 all-gather.2

commit v6 on v5

--- a/solution.py
+++ b/solution.py
@@ -131,47 +131,32 @@
     w_refs, (keep_ref, send_ref, other_ref, a_buf) = refs[:-4], refs[-4:]
     core = lax.axis_index("core")
     yl = lax.axis_index("yl")
+    x = lax.axis_index("x")
     for t in range(2):
         for u in range(2):
             source = 2 * (core if t == 0 else 1 - core) + (yl if u == 0 else 1 - yl)
             at = (2 * t + u) * ROWS
             for z in range(Z):
                 a_buf[at : at + ROWS, z * ROWS : (z + 1) * ROWS] = spread_ref[4 * z + source]
-    at = 0
-    for ref in w_refs:
-        y, done = None, 0
-        for part in ref if isinstance(ref, tuple) else (ref,):
+    piece = w_refs[0].shape[-1]
+    for shift, parts in ((0, w_refs[0:1]), (3, w_refs[1:3]), (1, w_refs[3:5]), (2, w_refs[5:7])):
+        y, at = None, 0
+        for part in parts:
             depth = part.shape[0] * ROWS
-            term = jnp.dot(
-                a_buf[:, done : done + depth],
-                part[...].reshape(depth, part.shape[-1]),
-                preferred_element_type=jnp.float32,
-            )
-            y, done = (term if y is None else y + term), done + depth
+            w = part[...].reshape(depth, piece)
+            term = jnp.dot(a_buf[:, at : at + depth], w, preferred_element_type=jnp.float32)
+            y, at = (term if y is None else y + term), at + depth
         y = y.astype(jnp.bfloat16)
-        cols = slice(at, at + y.shape[1])
-        at += y.shape[1]
+        cols = pl.ds(pl.multiple_of(lax.rem(x + shift, 4) * piece, piece), piece)
         keep_ref[:, cols] = y[0:ROWS]
         send_ref[:, cols] = y[ROWS : 2 * ROWS]
         for u in range(2):
             other_ref[u, :, cols] = y[(2 + u) * ROWS : (3 + u) * ROWS]
 
 
-def far_kernel(spread_ref, low_ref, high_ref, *refs):
-    projection_kernel(spread_ref, (low_ref, high_ref), *refs)
-
-
-def finish_kernel(*refs):
-    o_ref = refs[-1]
-    piece = o_ref.shape[-1] // 4
-    x = lax.axis_index("x")
-    for n, shift in enumerate((0, 3, 1, 2)):
-        keep, arrived, last = refs[0:3] if n < 3 else refs[3:6]
-        cols = slice((n % 3) * piece, (n % 3 + 1) * piece)
-        total = keep[:, cols].astype(jnp.float32) + arrived[0, :, cols].astype(jnp.float32)
-        total = total + last[:, cols].astype(jnp.float32)
-        at = pl.multiple_of(lax.rem(x + shift, 4) * piece, piece)
-        o_ref[:, pl.ds(at, piece)] = total.astype(jnp.bfloat16)
+def finish_kernel(keep_ref, arrived_ref, last_ref, o_ref):
+    total = keep_ref[...].astype(jnp.float32) + arrived_ref[0].astype(jnp.float32)
+    o_ref[...] = (total + last_ref[...].astype(jnp.float32)).astype(jnp.bfloat16)
 
 
 def body(queries, keys, values, doc_ids, out_weight):
@@ -211,9 +196,11 @@
     prev_other_1 = lax.ppermute(other, "core", [(0, 1)])
 
     split = queries.reshape(ROWS, Z, GROUP * HEAD_DIM).transpose(1, 0, 2)
+    split, here = lax.optimization_barrier((split, here))
     query = lax.all_to_all(split, ("zh", "zl"), 0, 0, tiled=True)
-    query, here = lax.optimization_barrier((query, here))
-    before, after = x_up(here), x_down(here)
+    before6, after6 = x_up(here[:6]), x_down(here[2:])
+    query, before6, after6 = lax.optimization_barrier((query, before6, after6))
+    before2, after2 = x_up(here[6:]), x_down(here[:2])
     attn = pl.pallas_call(
         attention_kernel,
         out_shape=jax.ShapeDtypeStruct((4 * Z, ROWS, HEAD_DIM), bf16),
@@ -235,40 +222,32 @@
         name="attention",
     )(query, own, other, prev_own, prev_other_0, prev_other_1)
 
+    attn, before2, after2 = lax.optimization_barrier((attn, before2, after2))
+    far_low, far_high = x_up(before6[:4]), x_down(after6[2:])
     spread = lax.all_to_all(attn, ("zh", "zl", "core", "yl"), 0, 0, tiled=True)
-    far_low, far_high = x_up(before[: Z // 2]), x_down(after[Z // 2 :])
+    weights = (here, before6, before2, after2, after6, far_low, far_high)
     f32 = jnp.float32
-    parts = []
-    for kernel, weights, blocks in (
-        (projection_kernel, (here, before, after), 3),
-        (far_kernel, (far_low, far_high), 1),
-    ):
-        cols = blocks * out_cols // 4
-        if parts:
-            spread, parts[2] = lax.optimization_barrier((spread, parts[2]))
-            parts[2] = lax.ppermute(parts[2], "yl", swap)
-        one = jax.ShapeDtypeStruct((ROWS, cols), bf16)
-        keep, send, theirs = pl.pallas_call(
-            kernel,
-            out_shape=[one, one, jax.ShapeDtypeStruct((2, ROWS, cols), bf16)],
-            scratch_shapes=[pltpu.VMEM((4 * ROWS, Z * ROWS), bf16)],
-            compiler_params=params(40),
-            cost_estimate=pl.CostEstimate(
-                flops=2 * 4 * ROWS * Z * ROWS * cols,
-                bytes_accessed=2 * Z * ROWS * cols + 8 * ROWS * cols,
-                transcendentals=0,
-            ),
-            name="projection",
-        )(spread, *weights)
-        arrived = lax.ppermute(theirs, "core", swap)
-        parts += [keep, arrived, (send.astype(f32) + arrived[1].astype(f32)).astype(bf16)]
-    parts[5] = lax.ppermute(parts[5], "yl", swap)
+    one = jax.ShapeDtypeStruct((ROWS, out_cols), bf16)
+    keep, send, theirs = pl.pallas_call(
+        projection_kernel,
+        out_shape=[one, one, jax.ShapeDtypeStruct((2, ROWS, out_cols), bf16)],
+        scratch_shapes=[pltpu.VMEM((4 * ROWS, Z * ROWS), bf16)],
+        compiler_params=params(54),
+        cost_estimate=pl.CostEstimate(
+            flops=2 * 4 * ROWS * Z * ROWS * out_cols,
+            bytes_accessed=2 * Z * ROWS * out_cols + 8 * ROWS * out_cols,
+            transcendentals=0,
+        ),
+        name="projection",
+    )(spread, *weights)
+    arrived = lax.ppermute(theirs, "core", swap)
+    last = lax.ppermute((send.astype(f32) + arrived[1].astype(f32)).astype(bf16), "yl", swap)
     return pl.pallas_call(
         finish_kernel,
-        out_shape=jax.ShapeDtypeStruct((ROWS, out_cols), bf16),
+        out_shape=one,
         compiler_params=params(16),
         name="finish",
-    )(*parts)
+    )(keep, arrived, last)
 
 
 def solution(mesh):

time: 207 us -> 228 us (1.10)
  blocking collectives: 35 us -> 0 us
  starting transfers between devices: 42.7 us -> 72.6 us
  waiting for transfers between devices: 83.7 us -> 101 us
  local copies, waits for them, and re-layouts: 6.36 us -> 14.3 us
    all_gather x1, waiting for transfers between devices: 0.01 us -> 37.9 us  [body(): here = lax.all_gather(piece, ('zh', 'zl'), axis=0, tiled=False)]
    all_to_all x1 -> x0, blocking collectives: 35 us -> none  [body(): spread = lax.all_to_all(attn, ('zh', 'zl', 'core', 'yl'), 0, 0, tiled=True)]
    all_to_all x0 -> x1, starting transfers between devices: none -> 31.4 us  [body(): spread = lax.all_to_all(attn, ('zh', 'zl', 'core', 'yl'), 0, 0, tiled=True)]
    all_to_all x1, waiting for transfers between devices: 18.5 us -> 0.01 us  [body(): query = lax.all_to_all(split, ('zh', 'zl'), 0, 0, tiled=True)]
    all_to_all x1, waiting for transfers between devices: 16.6 us -> 0.01 us  [body(): own = lax.all_to_all(packed, ('zh', 'zl'), 0, 0, tiled=True)]
    ppermute x4 -> x6, waiting for transfers between devices: 25.3 us -> 35.6 us  [ring(): lax.ppermute(a, axis, [(i, (i + step) % size) for i in range(size)])]
    pallas_call x3 -> x2, Pallas kernels: 6.03 us -> 11.4 us  [the longest x1 10.1 us: body(): pl.pallas_call(projection_kernel, out_shape=[one, one, jax.ShapeDtypeStru...]
    slice x2 -> x4, local copies, waits for them, and re-layouts: 0.14 us -> 4.84 us  [the longest x1 2.42 us: body(): before6, after6 = (x_up(here[:6]), x_down(here[2:]))]
  transfers between devices with their start and end apart: 16 -> 17, of which waited for: 8 -> 6; matrix products, arithmetic and copies ran while one was open for 1% -> 3% of each run, Pallas kernels for 9% -> 6%
where the time goes in v6:
time: 228 us
  waiting for transfers between devices  101 us (44%)
  starting transfers between devices  72.6 us (32%)
  Pallas kernels  25.7 us (11%)
  local copies, waits for them, and re-layouts  14.3 us (6%)
  between operations  13.6 us (6%)
    all_gather x1, waiting for transfers between devices, body(): here = lax.all_gather(piece, ('zh', 'zl'), axis=0, tiled=False)  37.9 us
    ppermute x6, waiting for transfers between devices, ring(): lax.ppermute(a, axis, [(i, (i + step) % size) for i in range(size)])  35.6 us
    all_to_all x1, starting transfers between devices, body(): spread = lax.all_to_all(attn, ('zh', 'zl', 'core', 'yl'), 0, 0, tiled=True)  31.4 us
    ppermute x1, waiting for transfers between devices, body(): lax.ppermute((send.astype(f32) + arrived[1].astype(f32)).astype(bf16), 'y...  23 us
    pallas_call x1, Pallas kernels, body(): pl.pallas_call(attention_kernel, out_shape=jax.ShapeDtypeStruct((4 * Z, R...  13.3 us
    pallas_call x1, Pallas kernels, body(): pl.pallas_call(projection_kernel, out_shape=[one, one, jax.ShapeDtypeStru...  10.1 us
    all_to_all x1, starting transfers between devices, body(): own = lax.all_to_all(packed, ('zh', 'zl'), 0, 0, tiled=True)  9.04 us
    ppermute x1, starting transfers between devices, body(): lax.ppermute(own, BLK + ('yh',), [(2 * i + h, 2 * (i + 1) + 1 - h) for i...  7.57 us
  transfers between devices with their start and end apart: 17, of which 6 were waited for; matrix products, arithmetic and copies ran while one was open for 3% of the time, Pallas kernels for 6%

profile of v6, /device:TPU:1, one launch (start us, length us, event | category | flops | bytes accessed | tf_op | source)
XLA Modules:
  0.0 228.2 jit_solution(1081052247592327672)
XLA Ops:
  6.5 0.0 all-gather.3.cloned.1.call-start
  6.5 1.0 dynamic_slice.3
  7.5 0.7 collective-permute-start
  8.2 0.0 copy-start.1
  8.2 0.9 copy-done.1
  9.1 0.0 copy-start.2
  9.1 0.9 copy-done.2
  10.1 0.0 copy-start.3
  10.1 0.7 copy-done.3
  10.8 0.0 copy-start.5
  10.8 0.9 pack_kv.1
  11.7 0.0 collective-permute-done
  11.7 0.7 copy-done.10
  12.4 0.0 all-gather.3.cloned.1.call-update
  12.4 9.0 %all-to-all-start.1 = ((bf16[8,144,256]{2,1,0:T(8,128)(2,1)}), bf16[8,144,256]{2,1,0:T(8,128)(2,1)S(1)}, u32[]{:S(2)}, u32[]{:S(2)}) async-start(bf16[8,144,256]{2,1,0:T(8,128)(2,1)} %pack_kv.1), calls=%async_computation.1 | async-start | bytes 1179648 | tf_op jit(solution)/shard_map/all_to_all | solution.py:187
  21.4 0.0 copy-done.5
  21.4 0.7 copy.6
  22.1 1.3 copy.7
  23.4 37.9 %all-gather.3.cloned.1.call-done = bf16[1024,1024]{1,0:T(8,128)(2,1)} async-done(((bf16[128,1024]{1,0:T(8,128)(2,1)}), bf16[1024,1024]{1,0:T(8,128)(2,1)}) %all-gather.3.cloned.1.call-update) | async-done | bytes 2097168 | tf_op jit(solution)/shard_map/all_gather | solution.py:188
  61.4 0.0 all-to-all-done.1.own_ref
  61.4 3.6 %all-to-all-start = ((bf16[8,128,512]{2,1,0:T(8,128)(2,1)}), bf16[8,128,512]{2,1,0:T(8,128)(2,1)S(1)}, u32[]{:S(2)}, u32[]{:S(2)}) async-start(bf16[8,128,512]{2,1,0:T(8,128)(2,1)} %bitcast.1), calls=%async_computation | async-start | bytes 2097152 | tf_op jit(solution)/shard_map/all_to_all | solution.py:200
  65.0 2.4 %fusion.2 = (bf16[6,128,1024]{2,1,0:T(8,128)(2,1)S(1)}, bf16[6,128,1024]{2,1,0:T(8,128)(2,1)S(1)}) fusion(bf16[8,128,1024]{2,1,0:T(8,128)(2,1)} %bitcast.10), kind=kLoop, calls=%fused_computation.4 | loop fusion | bytes 6291456 | tf_op jit(solution)/shard_map/slice | solution.py:201
  67.4 2.5 %collective-permute-start.2 = (bf16[6,128,1024]{2,1,0:T(8,128)(2,1)S(1)}, bf16[6,128,1024]{2,1,0:T(8,128)(2,1)S(1)}, u32[]{:S(2)}, u32[]{:S(2)}) collective-permute-start(bf16[6,128,1024]{2,1,0:T(8,128)(2,1)S(1)} %get-tuple-element.33), channel_id=1, source_target_pairs={{0,192},{64,0},{128,64},{192,128},{1,193},{65,1},{129,65},{193,129... | collective-permute-start | bytes 4718600 | tf_op jit(solution)/shard_map/ppermute | solution.py:178
  69.9 0.0 collective-permute-start.1
  69.9 7.0 %collective-permute-start.3 = (bf16[8,144,256]{2,1,0:T(8,128)(2,1)S(1)}, bf16[8,144,256]{2,1,0:T(8,128)(2,1)S(1)}, u32[]{:S(2)}, u32[]{:S(2)}) collective-permute-start(bf16[8,144,256]{2,1,0:T(8,128)(2,1)S(1)} %all-to-all-done.1.own_ref), channel_id=1, source_target_pairs={{0,1},{1,0},{2,3},{3,2},{4,5},{5,4},{6,7},{7,6},{8,9},{9,8},{10,11... | collective-permute-start | bytes 1769480 | tf_op jit(solution)/shard_map/ppermute | solution.py:189
  77.0 7.6 %collective-permute-start.5 = (bf16[8,144,256]{2,1,0:T(8,128)(2,1)S(1)}, bf16[8,144,256]{2,1,0:T(8,128)(2,1)S(1)}, u32[]{:S(2)}, u32[]{:S(2)}) collective-permute-start(bf16[8,144,256]{2,1,0:T(8,128)(2,1)S(1)} %all-to-all-done.1.own_ref), channel_id=1, source_target_pairs={{16,33},{17,32},{48,65},{49,64},{80,97},{81,96},{112,129},{113,128... | collective-permute-start | bytes 1769480 | tf_op jit(solution)/shard_map/ppermute | solution.py:191
  84.6 1.9 collective-permute-start.4
  86.5 0.0 collective-permute-done.3.oth_ref
  86.5 1.3 collective-permute-start.6
  87.8 0.0 copy-done.4
  87.8 1.1 fusion.1
  88.9 9.8 %collective-permute-done.2.refs_4_ = bf16[6,128,1024]{2,1,0:T(8,128)(2,1)S(1)} collective-permute-done((bf16[6,128,1024]{2,1,0:T(8,128)(2,1)S(1)}, bf16[6,128,1024]{2,1,0:T(8,128)(2,1)S(1)}, u32[]{:S(2)}, u32[]{:S(2)}) %collective-permute-start.2) | collective-permute-done | bytes 1572896 | tf_op jit(solution)/shard_map/ppermute | solution.py:178
  98.7 3.4 %collective-permute-start.8 = (bf16[2,128,1024]{2,1,0:T(8,128)(2,1)}, bf16[2,128,1024]{2,1,0:T(8,128)(2,1)}, u32[]{:S(2)}, u32[]{:S(2)}) collective-permute-start(bf16[2,128,1024]{2,1,0:T(8,128)(2,1)} %get-tuple-element.31), channel_id=1, source_target_pairs={{0,192},{64,0},{128,64},{192,128},{1,193},{65,1},{129,65},{193,129... | collective-permute-start | bytes 1572872 | tf_op jit(solution)/shard_map/ppermute | solution.py:178
  102.1 0.0 collective-permute-done.1.refs_1_
  102.1 0.0 copy-done.7
  102.1 1.2 copy-done.9
  103.3 0.0 collective-permute-start.7
  103.3 0.0 all-to-all-done.q_ref
  103.3 0.0 collective-permute-done.5.poth0_ref
  103.3 0.0 collective-permute-done.4.pown_ref
  103.3 0.0 collective-permute-done.6.poth1_ref
  103.3 13.3 %attention.1 = bf16[32,128,128]{2,1,0:T(8,128)(2,1)} custom-call(bf16[8,128,512]{2,1,0:T(8,128)(2,1)S(1)} %all-to-all-done.q_ref, bf16[8,144,256]{2,1,0:T(8,128)(2,1)S(1)} %all-to-all-done.1.own_ref, bf16[8,144,256]{2,1,0:T(8,128)(2,1)S(1)} %collective-permute-done.3.oth_ref, bf16[8,144,256]{2,1,0:T(8,128)(2,1)S(1)} %collective-permute-done.4.pown_ref, ...), custom_call_target="tpu_custom_call" | custom-call | flops 16000000000 | bytes 6000000 | tf_op jit(solution)/shard_map/attention/pallas_call | solution.py:204
  116.7 0.0 collective-permute-done.8.refs_3_
  116.7 0.0 collective-permute-done.7.refs_2_
  116.7 31.4 %all-to-all-start.2 = ((bf16[32,128,128]{2,1,0:T(8,128)(2,1)}), bf16[32,128,128]{2,1,0:T(8,128)(2,1)S(1)}, u32[]{:S(2)}, u32[]{:S(2)}) async-start(bf16[32,128,128]{2,1,0:T(8,128)(2,1)} %attention.1), calls=%async_computation.2 | async-start | bytes 2097152 | tf_op jit(solution)/shard_map/all_to_all | solution.py:227
  148.1 1.3 slice.25
  149.4 0.0 copy-done.8
  149.4 0.1 slice.26
  149.5 0.1 collective-permute-start.10
  149.6 1.5 collective-permute-start.9
  151.0 23.1 %collective-permute-done.10.refs_6_ = bf16[4,128,1024]{2,1,0:T(8,128)(2,1)S(1)} collective-permute-done((bf16[4,128,1024]{2,1,0:T(8,128)(2,1)S(1)}, bf16[4,128,1024]{2,1,0:T(8,128)(2,1)S(1)}, u32[]{:S(2)}, u32[]{:S(2)}) %collective-permute-start.10) | collective-permute-done | bytes 1048608 | tf_op jit(solution)/shard_map/ppermute | solution.py:178
  174.1 2.7 %collective-permute-done.9.refs_5_ = bf16[4,128,1024]{2,1,0:T(8,128)(2,1)S(1)} collective-permute-done((bf16[4,128,1024]{2,1,0:T(8,128)(2,1)S(1)}, bf16[4,128,1024]{2,1,0:T(8,128)(2,1)S(1)}, u32[]{:S(2)}, u32[]{:S(2)}) %collective-permute-start.9) | collective-permute-done | bytes 1048608 | tf_op jit(solution)/shard_map/ppermute | solution.py:178
  176.8 0.0 all-to-all-done.2.spread_ref
  176.8 0.0 copy-done.11
  176.8 1.1 copy-done.12
  177.9 1.0 copy-done.6
  178.9 10.1 %projection.1 = (bf16[128,4096]{1,0:T(8,128)(2,1)}, bf16[128,4096]{1,0:T(8,128)(2,1)}, bf16[2,128,4096]{2,1,0:T(8,128)(2,1)}) custom-call(bf16[32,128,128]{2,1,0:T(8,128)(2,1)} %copy-done.6, bf16[8,128,1024]{2,1,0:T(8,128)(2,1)} %bitcast.11, bf16[6,128,1024]{2,1,0:T(8,128)(2,1)} %copy-done.9, bf16[2,128,1024]{2,1,0:T(8,128)(2,1)} %collective-permute-done.7.refs_2_, ...), custom_call_target="tpu_custom_call" | custom-call | flops 4294967296 | bytes 12582912 | tf_op jit(solution)/shard_map/projection/pallas_call | solution.py:231
  188.9 1.0 collective-permute-start.11
  190.0 4.0 %collective-permute-done.11.arrived_ref = bf16[2,128,4096]{2,1,0:T(8,128)(2,1)S(1)} collective-permute-done((bf16[2,128,4096]{2,1,0:T(8,128)(2,1)}, bf16[2,128,4096]{2,1,0:T(8,128)(2,1)S(1)}, u32[]{:S(2)}, u32[]{:S(2)}) %collective-permute-start.11) | collective-permute-done | bytes 2097184 | tf_op jit(solution)/shard_map/ppermute | solution.py:243
  194.0 1.5 fusion
  195.5 1.5 collective-permute-start.12
  196.9 23.0 %collective-permute-done.12.last_ref = bf16[128,4096]{1,0:T(8,128)(2,1)S(1)} collective-permute-done((bf16[128,4096]{1,0:T(8,128)(2,1)S(1)}, bf16[128,4096]{1,0:T(8,128)(2,1)S(1)}, u32[]{:S(2)}, u32[]{:S(2)}) %collective-permute-start.12) | collective-permute-done | bytes 1048608 | tf_op jit(solution)/shard_map/ppermute | solution.py:244
  219.9 0.0 copy-done
  219.9 1.4 finish.1
  (9 shorter events, 0.0 us)
Async XLA Ops:
  6.5 54.8 %all-gather.3.cloned.1.call-start = ((), (), s32[]{:S(2)}) async-start(), calls=%async_computation.3 | async-start | bytes 2359296 | tf_op jit(solution)/shard_map/all_gather | solution.py:188
  7.5 4.2 %collective-permute-start = (bf16[128,1024]{1,0:T(8,128)(2,1)S(1)}, bf16[128,1024]{1,0:T(8,128)(2,1)S(1)}, u32[]{:S(2)}, u32[]{:S(2)}) collective-permute-start(bf16[128,1024]{1,0:T(8,128)(2,1)S(1)} %dynamic_slice.3), channel_id=1, source_target_pairs={{0,0},{1,32},{32,1},{33,33},{2,2},{3,34},{34,3},{35,35},{4,4},{5,3... | collective-permute-start | bytes 786440 | tf_op jit(solution)/shard_map/ppermute | solution.py:185
  8.2 1.0 copy-start.1
  9.1 0.9 copy-start.2
  10.1 0.7 copy-start.3
  10.8 10.7 %copy-start.5 = (bf16[128,4096]{1,0:T(8,128)(2,1)S(1)}, bf16[128,4096]{1,0:T(8,128)(2,1)}, u32[]{:S(2)}) copy-start(bf16[128,4096]{1,0:T(8,128)(2,1)} %param.5) | copy-start | bytes 3145732
  11.7 0.7 copy-start.10
  12.4 49.0 %all-to-all-start.1 = ((bf16[8,144,256]{2,1,0:T(8,128)(2,1)}), bf16[8,144,256]{2,1,0:T(8,128)(2,1)S(1)}, u32[]{:S(2)}, u32[]{:S(2)}) async-start(bf16[8,144,256]{2,1,0:T(8,128)(2,1)} %pack_kv.1), calls=%async_computation.1 | async-start | bytes 1179648 | tf_op jit(solution)/shard_map/all_to_all | solution.py:187
  61.4 41.9 %all-to-all-start = ((bf16[8,128,512]{2,1,0:T(8,128)(2,1)}), bf16[8,128,512]{2,1,0:T(8,128)(2,1)S(1)}, u32[]{:S(2)}, u32[]{:S(2)}) async-start(bf16[8,128,512]{2,1,0:T(8,128)(2,1)} %bitcast.1), calls=%async_computation | async-start | bytes 2097152 | tf_op jit(solution)/shard_map/all_to_all | solution.py:200
  65.0 22.8 %copy-start.4 = (bf16[1024,1024]{1,0:T(8,128)(2,1)S(1)}, bf16[1024,1024]{1,0:T(8,128)(2,1)}, u32[]{:S(2)}) copy-start(bf16[1024,1024]{1,0:T(8,128)(2,1)} %all-gather.3.cloned.1.call-done) | copy-start | bytes 6291460
  67.4 31.3 %collective-permute-start.2 = (bf16[6,128,1024]{2,1,0:T(8,128)(2,1)S(1)}, bf16[6,128,1024]{2,1,0:T(8,128)(2,1)S(1)}, u32[]{:S(2)}, u32[]{:S(2)}) collective-permute-start(bf16[6,128,1024]{2,1,0:T(8,128)(2,1)S(1)} %get-tuple-element.33), channel_id=1, source_target_pairs={{0,192},{64,0},{128,64},{192,128},{1,193},{65,1},{129,65},{193,129... | collective-permute-start | bytes 4718600 | tf_op jit(solution)/shard_map/ppermute | solution.py:178
  69.9 32.2 %collective-permute-start.1 = (bf16[6,128,1024]{2,1,0:T(8,128)(2,1)S(1)}, bf16[6,128,1024]{2,1,0:T(8,128)(2,1)S(1)}, u32[]{:S(2)}, u32[]{:S(2)}) collective-permute-start(bf16[6,128,1024]{2,1,0:T(8,128)(2,1)S(1)} %get-tuple-element.34), channel_id=1, source_target_pairs={{0,64},{64,128},{128,192},{192,0},{1,65},{65,129},{129,193},{193,1... | collective-permute-start | bytes 4718600 | tf_op jit(solution)/shard_map/ppermute | solution.py:178
  69.9 16.6 %collective-permute-start.3 = (bf16[8,144,256]{2,1,0:T(8,128)(2,1)S(1)}, bf16[8,144,256]{2,1,0:T(8,128)(2,1)S(1)}, u32[]{:S(2)}, u32[]{:S(2)}) collective-permute-start(bf16[8,144,256]{2,1,0:T(8,128)(2,1)S(1)} %all-to-all-done.1.own_ref), channel_id=1, source_target_pairs={{0,1},{1,0},{2,3},{3,2},{4,5},{5,4},{6,7},{7,6},{8,9},{9,8},{10,11... | collective-permute-start | bytes 1769480 | tf_op jit(solution)/shard_map/ppermute | solution.py:189
  77.0 26.3 %collective-permute-start.5 = (bf16[8,144,256]{2,1,0:T(8,128)(2,1)S(1)}, bf16[8,144,256]{2,1,0:T(8,128)(2,1)S(1)}, u32[]{:S(2)}, u32[]{:S(2)}) collective-permute-start(bf16[8,144,256]{2,1,0:T(8,128)(2,1)S(1)} %all-to-all-done.1.own_ref), channel_id=1, source_target_pairs={{16,33},{17,32},{48,65},{49,64},{80,97},{81,96},{112,129},{113,128... | collective-permute-start | bytes 1769480 | tf_op jit(solution)/shard_map/ppermute | solution.py:191
  84.6 18.8 %collective-permute-start.4 = (bf16[8,144,256]{2,1,0:T(8,128)(2,1)S(1)}, bf16[8,144,256]{2,1,0:T(8,128)(2,1)S(1)}, u32[]{:S(2)}, u32[]{:S(2)}) collective-permute-start(bf16[8,144,256]{2,1,0:T(8,128)(2,1)S(1)} %all-to-all-done.1.own_ref), channel_id=1, source_target_pairs={{0,16},{16,32},{32,48},{48,64},{64,80},{80,96},{96,112},{112,128},... | collective-permute-start | bytes 1769480 | tf_op jit(solution)/shard_map/ppermute | solution.py:190
  86.5 16.8 %collective-permute-start.6 = (bf16[8,144,256]{2,1,0:T(8,128)(2,1)S(1)}, bf16[8,144,256]{2,1,0:T(8,128)(2,1)}, u32[]{:S(2)}, u32[]{:S(2)}) collective-permute-start(bf16[8,144,256]{2,1,0:T(8,128)(2,1)S(1)} %collective-permute-done.3.oth_ref), channel_id=1, source_target_pairs={{0,16},{1,17},{2,18},{3,19},{4,20},{5,21},{6,22},{7,23},{8,24},{9,... | collective-permute-start | bytes 1769480 | tf_op jit(solution)/shard_map/ppermute | solution.py:196
  98.7 3.4 %copy-start.7 = (bf16[6,128,1024]{2,1,0:T(8,128)(2,1)}, bf16[6,128,1024]{2,1,0:T(8,128)(2,1)S(1)}, u32[]{:S(2)}) copy-start(bf16[6,128,1024]{2,1,0:T(8,128)(2,1)S(1)} %collective-permute-done.2.refs_4_) | copy-start | bytes 4718596
  98.7 18.0 %collective-permute-start.8 = (bf16[2,128,1024]{2,1,0:T(8,128)(2,1)}, bf16[2,128,1024]{2,1,0:T(8,128)(2,1)}, u32[]{:S(2)}, u32[]{:S(2)}) collective-permute-start(bf16[2,128,1024]{2,1,0:T(8,128)(2,1)} %get-tuple-element.31), channel_id=1, source_target_pairs={{0,192},{64,0},{128,64},{192,128},{1,193},{65,1},{129,65},{193,129... | collective-permute-start | bytes 1572872 | tf_op jit(solution)/shard_map/ppermute | solution.py:178
  102.1 1.2 copy-start.9
  103.3 13.4 %collective-permute-start.7 = (bf16[2,128,1024]{2,1,0:T(8,128)(2,1)}, bf16[2,128,1024]{2,1,0:T(8,128)(2,1)}, u32[]{:S(2)}, u32[]{:S(2)}) collective-permute-start(bf16[2,128,1024]{2,1,0:T(8,128)(2,1)} %get-tuple-element.32), channel_id=1, source_target_pairs={{0,64},{64,128},{128,192},{192,0},{1,65},{65,129},{129,193},{193,1... | collective-permute-start | bytes 1572872 | tf_op jit(solution)/shard_map/ppermute | solution.py:178
  116.7 32.7 %copy-start.8 = (bf16[6,128,1024]{2,1,0:T(8,128)(2,1)S(1)}, bf16[6,128,1024]{2,1,0:T(8,128)(2,1)}, u32[]{:S(2)}) copy-start(bf16[6,128,1024]{2,1,0:T(8,128)(2,1)} %copy-done.7) | copy-start | bytes 4718596
  116.7 60.2 %all-to-all-start.2 = ((bf16[32,128,128]{2,1,0:T(8,128)(2,1)}), bf16[32,128,128]{2,1,0:T(8,128)(2,1)S(1)}, u32[]{:S(2)}, u32[]{:S(2)}) async-start(bf16[32,128,128]{2,1,0:T(8,128)(2,1)} %attention.1), calls=%async_computation.2 | async-start | bytes 2097152 | tf_op jit(solution)/shard_map/all_to_all | solution.py:227
  149.5 24.6 %collective-permute-start.10 = (bf16[4,128,1024]{2,1,0:T(8,128)(2,1)S(1)}, bf16[4,128,1024]{2,1,0:T(8,128)(2,1)S(1)}, u32[]{:S(2)}, u32[]{:S(2)}) collective-permute-start(bf16[4,128,1024]{2,1,0:T(8,128)(2,1)S(1)} %slice.26), channel_id=1, source_target_pairs={{0,192},{64,0},{128,64},{192,128},{1,193},{65,1},{129,65},{193,129... | collective-permute-start | bytes 3145736 | tf_op jit(solution)/shard_map/ppermute | solution.py:178
  149.6 27.2 %collective-permute-start.9 = (bf16[4,128,1024]{2,1,0:T(8,128)(2,1)S(1)}, bf16[4,128,1024]{2,1,0:T(8,128)(2,1)S(1)}, u32[]{:S(2)}, u32[]{:S(2)}) collective-permute-start(bf16[4,128,1024]{2,1,0:T(8,128)(2,1)S(1)} %slice.25), channel_id=1, source_target_pairs={{0,64},{64,128},{128,192},{192,0},{1,65},{65,129},{129,193},{193,1... | collective-permute-start | bytes 3145736 | tf_op jit(solution)/shard_map/ppermute | solution.py:178
  174.1 2.7 %copy-start.11 = (bf16[4,128,1024]{2,1,0:T(8,128)(2,1)}, bf16[4,128,1024]{2,1,0:T(8,128)(2,1)S(1)}, u32[]{:S(2)}) copy-start(bf16[4,128,1024]{2,1,0:T(8,128)(2,1)S(1)} %collective-permute-done.10.refs_6_) | copy-start | bytes 3145732
  176.8 1.1 copy-start.12
  177.9 1.0 copy-start.6
  188.9 31.0 %copy-start = (bf16[128,4096]{1,0:T(8,128)(2,1)S(1)}, bf16[128,4096]{1,0:T(8,128)(2,1)}, u32[]{:S(2)}) copy-start(bf16[128,4096]{1,0:T(8,128)(2,1)} %get-tuple-element.28.keep_ref) | copy-start | bytes 3145732
  188.9 5.0 %collective-permute-start.11 = (bf16[2,128,4096]{2,1,0:T(8,128)(2,1)}, bf16[2,128,4096]{2,1,0:T(8,128)(2,1)S(1)}, u32[]{:S(2)}, u32[]{:S(2)}) collective-permute-start(bf16[2,128,4096]{2,1,0:T(8,128)(2,1)} %get-tuple-element.29), channel_id=1, source_target_pairs={{0,16},{16,0},{1,17},{17,1},{2,18},{18,2},{3,19},{19,3},{4,20},{20... | collective-permute-start | bytes 6291464 | tf_op jit(solution)/shard_map/ppermute | solution.py:243
  195.5 24.5 %collective-permute-start.12 = (bf16[128,4096]{1,0:T(8,128)(2,1)S(1)}, bf16[128,4096]{1,0:T(8,128)(2,1)S(1)}, u32[]{:S(2)}, u32[]{:S(2)}) collective-permute-start(bf16[128,4096]{1,0:T(8,128)(2,1)S(1)} %fusion), channel_id=1, source_target_pairs={{0,32},{32,0},{1,33},{33,1},{2,34},{34,2},{3,35},{35,3},{4,36},{36... | collective-permute-start | bytes 3145736 | tf_op jit(solution)/shard_map/ppermute | solution.py:244
Sparse Core Ops, SparseCore 0:
  12.5 48.7 all-gather.2

commit v7 on v6

--- a/solution.py
+++ b/solution.py
@@ -129,25 +129,28 @@
 
 def projection_kernel(spread_ref, *refs):
     w_refs, (keep_ref, send_ref, other_ref, a_buf) = refs[:-4], refs[-4:]
-    core = lax.axis_index("core")
-    yl = lax.axis_index("yl")
+    step, steps = pl.program_id(0), pl.num_programs(0)
     x = lax.axis_index("x")
-    for t in range(2):
-        for u in range(2):
-            source = 2 * (core if t == 0 else 1 - core) + (yl if u == 0 else 1 - yl)
-            at = (2 * t + u) * ROWS
-            for z in range(Z):
-                a_buf[at : at + ROWS, z * ROWS : (z + 1) * ROWS] = spread_ref[4 * z + source]
-    piece = w_refs[0].shape[-1]
-    for shift, parts in ((0, w_refs[0:1]), (3, w_refs[1:3]), (1, w_refs[3:5]), (2, w_refs[5:7])):
-        y, at = None, 0
-        for part in parts:
-            depth = part.shape[0] * ROWS
-            w = part[...].reshape(depth, piece)
-            term = jnp.dot(a_buf[:, at : at + depth], w, preferred_element_type=jnp.float32)
-            y, at = (term if y is None else y + term), at + depth
+
+    @pl.when(step == 0)
+    def _():
+        core = lax.axis_index("core")
+        yl = lax.axis_index("yl")
+        for t in range(2):
+            for u in range(2):
+                source = 2 * (core if t == 0 else 1 - core) + (yl if u == 0 else 1 - yl)
+                at = (2 * t + u) * ROWS
+                for z in range(Z):
+                    a_buf[at : at + ROWS, z * ROWS : (z + 1) * ROWS] = spread_ref[4 * z + source]
+
+    half, piece = Z * ROWS // 2, w_refs[0].shape[-1]
+    for n, shift in enumerate((0, 3, 1, 2)):
+        low, high = (ref[...].reshape(half, piece) for ref in w_refs[2 * n : 2 * n + 2])
+        y = jnp.dot(a_buf[:, 0:half], low, preferred_element_type=jnp.float32)
+        y = y + jnp.dot(a_buf[:, half : 2 * half], high, preferred_element_type=jnp.float32)
         y = y.astype(jnp.bfloat16)
-        cols = pl.ds(pl.multiple_of(lax.rem(x + shift, 4) * piece, piece), piece)
+        block = lax.rem(x + shift, 4) * steps + step
+        cols = pl.ds(pl.multiple_of(block * piece, piece), piece)
         keep_ref[:, cols] = y[0:ROWS]
         send_ref[:, cols] = y[ROWS : 2 * ROWS]
         for u in range(2):
@@ -196,11 +199,11 @@
     prev_other_1 = lax.ppermute(other, "core", [(0, 1)])
 
     split = queries.reshape(ROWS, Z, GROUP * HEAD_DIM).transpose(1, 0, 2)
-    split, here = lax.optimization_barrier((split, here))
     query = lax.all_to_all(split, ("zh", "zl"), 0, 0, tiled=True)
-    before6, after6 = x_up(here[:6]), x_down(here[2:])
-    query, before6, after6 = lax.optimization_barrier((query, before6, after6))
-    before2, after2 = x_up(here[6:]), x_down(here[:2])
+    query, here = lax.optimization_barrier((query, here))
+    low, high = here[: Z // 2], here[Z // 2 :]
+    before_low, after_high = x_up(low), x_down(high)
+    before_high, after_low = x_up(high), x_down(low)
     attn = pl.pallas_call(
         attention_kernel,
         out_shape=jax.ShapeDtypeStruct((4 * Z, ROWS, HEAD_DIM), bf16),
@@ -222,17 +225,22 @@
         name="attention",
     )(query, own, other, prev_own, prev_other_0, prev_other_1)
 
-    attn, before2, after2 = lax.optimization_barrier((attn, before2, after2))
-    far_low, far_high = x_up(before6[:4]), x_down(after6[2:])
+    far_low, far_high = x_up(before_low), x_down(after_high)
     spread = lax.all_to_all(attn, ("zh", "zl", "core", "yl"), 0, 0, tiled=True)
-    weights = (here, before6, before2, after2, after6, far_low, far_high)
+    weights = (low, high, before_low, before_high, after_low, after_high, far_low, far_high)
     f32 = jnp.float32
     one = jax.ShapeDtypeStruct((ROWS, out_cols), bf16)
+    steps = 4
+    whole = pl.BlockSpec(memory_space=pltpu.VMEM)
     keep, send, theirs = pl.pallas_call(
         projection_kernel,
+        grid=(steps,),
+        in_specs=[whole]
+        + [pl.BlockSpec((Z // 2, ROWS, out_cols // 4 // steps), lambda i: (0, 0, i))] * len(weights),
+        out_specs=[whole] * 3,
         out_shape=[one, one, jax.ShapeDtypeStruct((2, ROWS, out_cols), bf16)],
         scratch_shapes=[pltpu.VMEM((4 * ROWS, Z * ROWS), bf16)],
-        compiler_params=params(54),
+        compiler_params=params(40),
         cost_estimate=pl.CostEstimate(
             flops=2 * 4 * ROWS * Z * ROWS * out_cols,
             bytes_accessed=2 * Z * ROWS * out_cols + 8 * ROWS * out_cols,

time: 228 us -> 214 us (0.939)
  starting transfers between devices: 72.6 us -> 60.7 us
  waiting for transfers between devices: 101 us -> 105 us
  Pallas kernels: 25.7 us -> 22.8 us
    all_gather x1, waiting for transfers between devices: 37.9 us -> 0.01 us  [body(): here = lax.all_gather(piece, ('zh', 'zl'), axis=0, tiled=False)]
    all_to_all x1, starting transfers between devices: 31.4 us -> 10.8 us  [body(): spread = lax.all_to_all(attn, ('zh', 'zl', 'core', 'yl'), 0, 0, tiled=True)]
    all_to_all x1, waiting for transfers between devices: 0.01 us -> 18 us  [body(): query = lax.all_to_all(split, ('zh', 'zl'), 0, 0, tiled=True)]
    all_to_all x1, waiting for transfers between devices: 0.01 us -> 16.7 us  [body(): own = lax.all_to_all(packed, ('zh', 'zl'), 0, 0, tiled=True)]
    ppermute x6, starting transfers between devices: 7.49 us -> 14.5 us  [ring(): lax.ppermute(a, axis, [(i, (i + step) % size) for i in range(size)])]
    ppermute x6, waiting for transfers between devices: 35.6 us -> 42.4 us  [ring(): lax.ppermute(a, axis, [(i, (i + step) % size) for i in range(size)])]
    slice x4 -> x1, local copies, waits for them, and re-layouts: 4.84 us -> 1.82 us  [body(): low, high = (here[:Z // 2], here[Z // 2:])]
    pallas_call x1, Pallas kernels: 10.1 us -> 7.12 us  [body(): pl.pallas_call(projection_kernel, grid=(steps,), in_specs=[whole] + [pl.B...]
  transfers between devices with their start and end apart: 17 -> 17, of which waited for: 6 -> 8; matrix products, arithmetic and copies ran while one was open for 3% -> 2% of each run, Pallas kernels for 6% -> 7%
where the time goes in v7:
time: 214 us
  waiting for transfers between devices  105 us (49%)
  starting transfers between devices  60.7 us (28%)
  Pallas kernels  22.8 us (11%)
  between operations  13.5 us (6%)
  local copies, waits for them, and re-layouts  12.5 us (6%)
    ppermute x6, waiting for transfers between devices, ring(): lax.ppermute(a, axis, [(i, (i + step) % size) for i in range(size)])  42.4 us
    ppermute x1, waiting for transfers between devices, body(): lax.ppermute((send.astype(f32) + arrived[1].astype(f32)).astype(bf16), 'y...  23 us
    all_to_all x1, waiting for transfers between devices, body(): query = lax.all_to_all(split, ('zh', 'zl'), 0, 0, tiled=True)  18 us
    all_to_all x1, waiting for transfers between devices, body(): own = lax.all_to_all(packed, ('zh', 'zl'), 0, 0, tiled=True)  16.7 us
    ppermute x6, starting transfers between devices, ring(): lax.ppermute(a, axis, [(i, (i + step) % size) for i in range(size)])  14.5 us
    pallas_call x1, Pallas kernels, body(): pl.pallas_call(attention_kernel, out_shape=jax.ShapeDtypeStruct((4 * Z, R...  13.4 us
    all_to_all x1, starting transfers between devices, body(): spread = lax.all_to_all(attn, ('zh', 'zl', 'core', 'yl'), 0, 0, tiled=True)  10.8 us
    ppermute x1, starting transfers between devices, body(): other = lax.ppermute(own, 'yh', swap)  9.2 us
  transfers between devices with their start and end apart: 17, of which 8 were waited for; matrix products, arithmetic and copies ran while one was open for 2% of the time, Pallas kernels for 7%

profile of v7, /device:TPU:1, one launch (start us, length us, event | category | flops | bytes accessed | tf_op | source)
XLA Modules:
  0.0 214.4 jit_solution(11577591334384000450)
XLA Ops:
  6.5 0.0 all-gather.3.cloned.1.call-start
  6.5 1.0 dynamic_slice.3
  7.5 0.7 collective-permute-start
  8.2 0.0 copy-start
  8.2 0.9 copy-done
  9.1 0.0 copy-start.1
  9.1 0.9 copy-done.1
  10.1 0.0 copy-start.2
  10.1 0.7 copy-done.2
  10.8 0.0 copy-start.7
  10.8 0.9 pack_kv.1
  11.7 0.0 collective-permute-done
  11.7 0.0 copy-start.8
  11.7 0.7 copy-done.8
  12.4 0.0 all-gather.3.cloned.1.call-update
  12.4 9.0 %all-to-all-start.1 = ((bf16[8,144,256]{2,1,0:T(8,128)(2,1)}), bf16[8,144,256]{2,1,0:T(8,128)(2,1)}, u32[]{:S(2)}, u32[]{:S(2)}) async-start(bf16[8,144,256]{2,1,0:T(8,128)(2,1)} %pack_kv.1), calls=%async_computation.1 | async-start | bytes 1179648 | tf_op jit(solution)/shard_map/all_to_all | solution.py:190
  21.4 0.0 copy-done.7
  21.5 0.7 copy.6
  22.1 1.3 copy.7
  23.4 16.7 %all-to-all-done.1.own_ref = bf16[8,144,256]{2,1,0:T(8,128)(2,1)} async-done(((bf16[8,144,256]{2,1,0:T(8,128)(2,1)}), bf16[8,144,256]{2,1,0:T(8,128)(2,1)}, u32[]{:S(2)}, u32[]{:S(2)}) %all-to-all-start.1) | async-done | bytes 589856 | tf_op jit(solution)/shard_map/all_to_all | solution.py:190
  40.1 3.6 %all-to-all-start = ((bf16[8,128,512]{2,1,0:T(8,128)(2,1)}), bf16[8,128,512]{2,1,0:T(8,128)(2,1)S(1)}, u32[]{:S(2)}, u32[]{:S(2)}) async-start(bf16[8,128,512]{2,1,0:T(8,128)(2,1)} %bitcast.1), calls=%async_computation | async-start | bytes 2097152 | tf_op jit(solution)/shard_map/all_to_all | solution.py:202
  43.7 9.2 %collective-permute-start.1 = (bf16[8,144,256]{2,1,0:T(8,128)(2,1)}, bf16[8,144,256]{2,1,0:T(8,128)(2,1)}, u32[]{:S(2)}, u32[]{:S(2)}) collective-permute-start(bf16[8,144,256]{2,1,0:T(8,128)(2,1)} %all-to-all-done.1.own_ref), channel_id=1, source_target_pairs={{0,1},{1,0},{2,3},{3,2},{4,5},{5,4},{6,7},{7,6},{8,9},{9,8},{10,11... | collective-permute-start | bytes 1769480 | tf_op jit(solution)/shard_map/ppermute | solution.py:192
  52.9 7.4 %collective-permute-start.3 = (bf16[8,144,256]{2,1,0:T(8,128)(2,1)}, bf16[8,144,256]{2,1,0:T(8,128)(2,1)}, u32[]{:S(2)}, u32[]{:S(2)}) collective-permute-start(bf16[8,144,256]{2,1,0:T(8,128)(2,1)} %all-to-all-done.1.own_ref), channel_id=1, source_target_pairs={{16,33},{17,32},{48,65},{49,64},{80,97},{81,96},{112,129},{113,128... | collective-permute-start | bytes 1769480 | tf_op jit(solution)/shard_map/ppermute | solution.py:194
  60.3 1.9 collective-permute-start.2
  62.3 0.8 collective-permute-done.1.oth_ref
  63.1 1.3 collective-permute-start.4
  64.4 18.0 %all-to-all-done.q_ref = bf16[8,128,512]{2,1,0:T(8,128)(2,1)S(1)} async-done(((bf16[8,128,512]{2,1,0:T(8,128)(2,1)}), bf16[8,128,512]{2,1,0:T(8,128)(2,1)S(1)}, u32[]{:S(2)}, u32[]{:S(2)}) %all-to-all-start) | async-done | bytes 1048608 | tf_op jit(solution)/shard_map/all_to_all | solution.py:202
  82.3 0.0 all-gather.3.cloned.1.call-done
  82.3 1.8 fusion.1
  84.2 2.5 %collective-permute-start.8 = (bf16[4,128,1024]{2,1,0:T(8,128)(2,1)S(1)}, bf16[4,128,1024]{2,1,0:T(8,128)(2,1)}, u32[]{:S(2)}, u32[]{:S(2)}) collective-permute-start(bf16[4,128,1024]{2,1,0:T(8,128)(2,1)S(1)} %get-tuple-element.19.refs_1_), channel_id=1, source_target_pairs={{0,192},{64,0},{128,64},{192,128},{1,193},{65,1},{129,65},{193,129... | collective-permute-start | bytes 3145736 | tf_op jit(solution)/shard_map/ppermute | solution.py:181
  86.7 0.0 collective-permute-start.5
  86.7 0.0 collective-permute-done.3.poth0_ref
  86.7 0.0 collective-permute-done.2.pown_ref
  86.7 0.0 collective-permute-done.4.poth1_ref
  86.7 13.4 %attention.1 = bf16[32,128,128]{2,1,0:T(8,128)(2,1)} custom-call(bf16[8,128,512]{2,1,0:T(8,128)(2,1)S(1)} %all-to-all-done.q_ref, bf16[8,144,256]{2,1,0:T(8,128)(2,1)} %all-to-all-done.1.own_ref, bf16[8,144,256]{2,1,0:T(8,128)(2,1)} %collective-permute-done.1.oth_ref, bf16[8,144,256]{2,1,0:T(8,128)(2,1)} %collective-permute-done.2.pown_ref, ...), custom_call_target="tpu_custom_call" | custom-call | flops 16000000000 | bytes 6000000 | tf_op jit(solution)/shard_map/attention/pallas_call | solution.py:207
  100.2 10.8 %all-to-all-start.2 = ((bf16[32,128,128]{2,1,0:T(8,128)(2,1)}), bf16[32,128,128]{2,1,0:T(8,128)(2,1)S(1)}, u32[]{:S(2)}, u32[]{:S(2)}) async-start(bf16[32,128,128]{2,1,0:T(8,128)(2,1)} %attention.1), calls=%async_computation.2 | async-start | bytes 2097152 | tf_op jit(solution)/shard_map/all_to_all | solution.py:229
  110.9 0.8 collective-permute-start.6
  111.7 9.7 %collective-permute-start.7 = (bf16[4,128,1024]{2,1,0:T(8,128)(2,1)S(1)}, bf16[4,128,1024]{2,1,0:T(8,128)(2,1)S(1)}, u32[]{:S(2)}, u32[]{:S(2)}) collective-permute-start(bf16[4,128,1024]{2,1,0:T(8,128)(2,1)S(1)} %get-tuple-element.20.refs_0_), channel_id=1, source_target_pairs={{0,192},{64,0},{128,64},{192,128},{1,193},{65,1},{129,65},{193,129... | collective-permute-start | bytes 3145736 | tf_op jit(solution)/shard_map/ppermute | solution.py:181
  121.5 0.0 collective-permute-done.8.refs_5_
  121.5 1.4 collective-permute-start.10
  122.8 0.0 collective-permute-done.5.refs_2_
  122.8 0.1 collective-permute-start.9
  122.9 21.8 %collective-permute-done.6.refs_3_ = bf16[4,128,1024]{2,1,0:T(8,128)(2,1)S(1)} collective-permute-done((bf16[4,128,1024]{2,1,0:T(8,128)(2,1)S(1)}, bf16[4,128,1024]{2,1,0:T(8,128)(2,1)S(1)}, u32[]{:S(2)}, u32[]{:S(2)}) %collective-permute-start.6) | collective-permute-done | bytes 1048608 | tf_op jit(solution)/shard_map/ppermute | solution.py:181
  144.8 0.0 copy-start.3
  144.8 1.0 copy-done.3
  145.8 0.0 collective-permute-done.7.refs_4_
  145.8 0.0 copy-start.5
  145.8 1.0 copy-done.5
  146.8 0.0 all-to-all-done.2.spread_ref
  146.8 19.6 %collective-permute-done.10.refs_7_ = bf16[4,128,1024]{2,1,0:T(8,128)(2,1)} collective-permute-done((bf16[4,128,1024]{2,1,0:T(8,128)(2,1)}, bf16[4,128,1024]{2,1,0:T(8,128)(2,1)}, u32[]{:S(2)}, u32[]{:S(2)}) %collective-permute-start.10) | collective-permute-done | bytes 1048608 | tf_op jit(solution)/shard_map/ppermute | solution.py:181
  166.4 1.0 collective-permute-done.9.refs_6_
  167.3 0.0 copy-start.4
  167.3 1.2 copy-done.4
  168.6 0.0 copy-start.6
  168.6 1.2 copy-done.6
  169.8 7.1 %projection.1 = (bf16[128,4096]{1,0:T(8,128)(2,1)S(1)}, bf16[128,4096]{1,0:T(8,128)(2,1)S(1)}, bf16[2,128,4096]{2,1,0:T(8,128)(2,1)S(1)}) custom-call(bf16[32,128,128]{2,1,0:T(8,128)(2,1)S(1)} %all-to-all-done.2.spread_ref, bf16[4,128,1024]{2,1,0:T(8,128)(2,1)S(1)} %get-tuple-element.20.refs_0_, bf16[4,128,1024]{2,1,0:T(8,128)(2,1)S(1)} %get-tuple-element.19.refs_1_, ...), custom_call_target="tpu_custom_call" | custom-call | flops 4294967296 | bytes 12582912 | tf_op jit(solution)/shard_map/projection/pallas_call | solution.py:235
  176.9 0.8 collective-permute-start.11
  177.7 3.8 %collective-permute-done.11.arrived_ref = bf16[2,128,4096]{2,1,0:T(8,128)(2,1)S(1)} collective-permute-done((bf16[2,128,4096]{2,1,0:T(8,128)(2,1)S(1)}, bf16[2,128,4096]{2,1,0:T(8,128)(2,1)S(1)}, u32[]{:S(2)}, u32[]{:S(2)}) %collective-permute-start.11) | collective-permute-done | bytes 2097184 | tf_op jit(solution)/shard_map/ppermute | solution.py:251
  181.5 0.2 fusion
  181.8 1.5 collective-permute-start.12
  183.2 23.0 %collective-permute-done.12.last_ref = bf16[128,4096]{1,0:T(8,128)(2,1)S(1)} collective-permute-done((bf16[128,4096]{1,0:T(8,128)(2,1)S(1)}, bf16[128,4096]{1,0:T(8,128)(2,1)S(1)}, u32[]{:S(2)}, u32[]{:S(2)}) %collective-permute-start.12) | collective-permute-done | bytes 1048608 | tf_op jit(solution)/shard_map/ppermute | solution.py:252
  206.2 1.3 finish.1
Async XLA Ops:
  6.5 75.8 %all-gather.3.cloned.1.call-start = ((), (), s32[]{:S(2)}) async-start(), calls=%async_computation.3 | async-start | bytes 2359296 | tf_op jit(solution)/shard_map/all_gather | solution.py:191
  7.5 4.2 %collective-permute-start = (bf16[128,1024]{1,0:T(8,128)(2,1)S(1)}, bf16[128,1024]{1,0:T(8,128)(2,1)S(1)}, u32[]{:S(2)}, u32[]{:S(2)}) collective-permute-start(bf16[128,1024]{1,0:T(8,128)(2,1)S(1)} %dynamic_slice.3), channel_id=1, source_target_pairs={{0,0},{1,32},{32,1},{33,33},{2,2},{3,34},{34,3},{35,35},{4,4},{5,3... | collective-permute-start | bytes 786440 | tf_op jit(solution)/shard_map/ppermute | solution.py:188
  8.2 1.0 copy-start
  9.1 0.9 copy-start.1
  10.1 0.7 copy-start.2
  10.8 10.7 %copy-start.7 = (bf16[128,4096]{1,0:T(8,128)(2,1)S(1)}, bf16[128,4096]{1,0:T(8,128)(2,1)}, u32[]{:S(2)}) copy-start(bf16[128,4096]{1,0:T(8,128)(2,1)} %param.5) | copy-start | bytes 3145732
  11.7 0.7 copy-start.8
  12.4 27.7 %all-to-all-start.1 = ((bf16[8,144,256]{2,1,0:T(8,128)(2,1)}), bf16[8,144,256]{2,1,0:T(8,128)(2,1)}, u32[]{:S(2)}, u32[]{:S(2)}) async-start(bf16[8,144,256]{2,1,0:T(8,128)(2,1)} %pack_kv.1), calls=%async_computation.1 | async-start | bytes 1179648 | tf_op jit(solution)/shard_map/all_to_all | solution.py:190
  40.1 42.2 %all-to-all-start = ((bf16[8,128,512]{2,1,0:T(8,128)(2,1)}), bf16[8,128,512]{2,1,0:T(8,128)(2,1)S(1)}, u32[]{:S(2)}, u32[]{:S(2)}) async-start(bf16[8,128,512]{2,1,0:T(8,128)(2,1)} %bitcast.1), calls=%async_computation | async-start | bytes 2097152 | tf_op jit(solution)/shard_map/all_to_all | solution.py:202
  43.7 19.4 %collective-permute-start.1 = (bf16[8,144,256]{2,1,0:T(8,128)(2,1)}, bf16[8,144,256]{2,1,0:T(8,128)(2,1)}, u32[]{:S(2)}, u32[]{:S(2)}) collective-permute-start(bf16[8,144,256]{2,1,0:T(8,128)(2,1)} %all-to-all-done.1.own_ref), channel_id=1, source_target_pairs={{0,1},{1,0},{2,3},{3,2},{4,5},{5,4},{6,7},{7,6},{8,9},{9,8},{10,11... | collective-permute-start | bytes 1769480 | tf_op jit(solution)/shard_map/ppermute | solution.py:192
  52.9 33.8 %collective-permute-start.3 = (bf16[8,144,256]{2,1,0:T(8,128)(2,1)}, bf16[8,144,256]{2,1,0:T(8,128)(2,1)}, u32[]{:S(2)}, u32[]{:S(2)}) collective-permute-start(bf16[8,144,256]{2,1,0:T(8,128)(2,1)} %all-to-all-done.1.own_ref), channel_id=1, source_target_pairs={{16,33},{17,32},{48,65},{49,64},{80,97},{81,96},{112,129},{113,128... | collective-permute-start | bytes 1769480 | tf_op jit(solution)/shard_map/ppermute | solution.py:194
  60.3 26.4 %collective-permute-start.2 = (bf16[8,144,256]{2,1,0:T(8,128)(2,1)}, bf16[8,144,256]{2,1,0:T(8,128)(2,1)}, u32[]{:S(2)}, u32[]{:S(2)}) collective-permute-start(bf16[8,144,256]{2,1,0:T(8,128)(2,1)} %all-to-all-done.1.own_ref), channel_id=1, source_target_pairs={{0,16},{16,32},{32,48},{48,64},{64,80},{80,96},{96,112},{112,128},... | collective-permute-start | bytes 1769480 | tf_op jit(solution)/shard_map/ppermute | solution.py:193
  63.1 23.6 %collective-permute-start.4 = (bf16[8,144,256]{2,1,0:T(8,128)(2,1)}, bf16[8,144,256]{2,1,0:T(8,128)(2,1)}, u32[]{:S(2)}, u32[]{:S(2)}) collective-permute-start(bf16[8,144,256]{2,1,0:T(8,128)(2,1)} %collective-permute-done.1.oth_ref), channel_id=1, source_target_pairs={{0,16},{1,17},{2,18},{3,19},{4,20},{5,21},{6,22},{7,23},{8,24},{9,... | collective-permute-start | bytes 1769480 | tf_op jit(solution)/shard_map/ppermute | solution.py:199
  84.2 37.3 %collective-permute-start.8 = (bf16[4,128,1024]{2,1,0:T(8,128)(2,1)S(1)}, bf16[4,128,1024]{2,1,0:T(8,128)(2,1)}, u32[]{:S(2)}, u32[]{:S(2)}) collective-permute-start(bf16[4,128,1024]{2,1,0:T(8,128)(2,1)S(1)} %get-tuple-element.19.refs_1_), channel_id=1, source_target_pairs={{0,192},{64,0},{128,64},{192,128},{1,193},{65,1},{129,65},{193,129... | collective-permute-start | bytes 3145736 | tf_op jit(solution)/shard_map/ppermute | solution.py:181
  86.7 36.1 %collective-permute-start.5 = (bf16[4,128,1024]{2,1,0:T(8,128)(2,1)S(1)}, bf16[4,128,1024]{2,1,0:T(8,128)(2,1)}, u32[]{:S(2)}, u32[]{:S(2)}) collective-permute-start(bf16[4,128,1024]{2,1,0:T(8,128)(2,1)S(1)} %get-tuple-element.20.refs_0_), channel_id=1, source_target_pairs={{0,64},{64,128},{128,192},{192,0},{1,65},{65,129},{129,193},{193,1... | collective-permute-start | bytes 3145736 | tf_op jit(solution)/shard_map/ppermute | solution.py:181
  100.2 46.6 %all-to-all-start.2 = ((bf16[32,128,128]{2,1,0:T(8,128)(2,1)}), bf16[32,128,128]{2,1,0:T(8,128)(2,1)S(1)}, u32[]{:S(2)}, u32[]{:S(2)}) async-start(bf16[32,128,128]{2,1,0:T(8,128)(2,1)} %attention.1), calls=%async_computation.2 | async-start | bytes 2097152 | tf_op jit(solution)/shard_map/all_to_all | solution.py:229
  110.9 33.8 %collective-permute-start.6 = (bf16[4,128,1024]{2,1,0:T(8,128)(2,1)S(1)}, bf16[4,128,1024]{2,1,0:T(8,128)(2,1)S(1)}, u32[]{:S(2)}, u32[]{:S(2)}) collective-permute-start(bf16[4,128,1024]{2,1,0:T(8,128)(2,1)S(1)} %get-tuple-element.19.refs_1_), channel_id=1, source_target_pairs={{0,64},{64,128},{128,192},{192,0},{1,65},{65,129},{129,193},{193,1... | collective-permute-start | bytes 3145736 | tf_op jit(solution)/shard_map/ppermute | solution.py:181
  111.7 34.1 %collective-permute-start.7 = (bf16[4,128,1024]{2,1,0:T(8,128)(2,1)S(1)}, bf16[4,128,1024]{2,1,0:T(8,128)(2,1)S(1)}, u32[]{:S(2)}, u32[]{:S(2)}) collective-permute-start(bf16[4,128,1024]{2,1,0:T(8,128)(2,1)S(1)} %get-tuple-element.20.refs_0_), channel_id=1, source_target_pairs={{0,192},{64,0},{128,64},{192,128},{1,193},{65,1},{129,65},{193,129... | collective-permute-start | bytes 3145736 | tf_op jit(solution)/shard_map/ppermute | solution.py:181
  121.5 44.9 %collective-permute-start.10 = (bf16[4,128,1024]{2,1,0:T(8,128)(2,1)}, bf16[4,128,1024]{2,1,0:T(8,128)(2,1)}, u32[]{:S(2)}, u32[]{:S(2)}) collective-permute-start(bf16[4,128,1024]{2,1,0:T(8,128)(2,1)} %collective-permute-done.8.refs_5_), channel_id=1, source_target_pairs={{0,192},{64,0},{128,64},{192,128},{1,193},{65,1},{129,65},{193,129... | collective-permute-start | bytes 3145736 | tf_op jit(solution)/shard_map/ppermute | solution.py:181
  122.8 44.5 %collective-permute-start.9 = (bf16[4,128,1024]{2,1,0:T(8,128)(2,1)}, bf16[4,128,1024]{2,1,0:T(8,128)(2,1)}, u32[]{:S(2)}, u32[]{:S(2)}) collective-permute-start(bf16[4,128,1024]{2,1,0:T(8,128)(2,1)} %collective-permute-done.5.refs_2_), channel_id=1, source_target_pairs={{0,64},{64,128},{128,192},{192,0},{1,65},{65,129},{129,193},{193,1... | collective-permute-start | bytes 3145736 | tf_op jit(solution)/shard_map/ppermute | solution.py:181
  144.8 1.0 copy-start.3
  145.8 1.0 copy-start.5
  167.3 1.2 copy-start.4
  168.6 1.2 copy-start.6
  176.9 4.6 %collective-permute-start.11 = (bf16[2,128,4096]{2,1,0:T(8,128)(2,1)S(1)}, bf16[2,128,4096]{2,1,0:T(8,128)(2,1)S(1)}, u32[]{:S(2)}, u32[]{:S(2)}) collective-permute-start(bf16[2,128,4096]{2,1,0:T(8,128)(2,1)S(1)} %get-tuple-element.17), channel_id=1, source_target_pairs={{0,16},{16,0},{1,17},{17,1},{2,18},{18,2},{3,19},{19,3},{4,20},{20... | collective-permute-start | bytes 6291464 | tf_op jit(solution)/shard_map/ppermute | solution.py:251
  181.8 24.5 %collective-permute-start.12 = (bf16[128,4096]{1,0:T(8,128)(2,1)S(1)}, bf16[128,4096]{1,0:T(8,128)(2,1)S(1)}, u32[]{:S(2)}, u32[]{:S(2)}) collective-permute-start(bf16[128,4096]{1,0:T(8,128)(2,1)S(1)} %fusion), channel_id=1, source_target_pairs={{0,32},{32,0},{1,33},{33,1},{2,34},{34,2},{3,35},{35,3},{4,36},{36... | collective-permute-start | bytes 3145736 | tf_op jit(solution)/shard_map/ppermute | solution.py:252
Sparse Core Ops, SparseCore 0:
  12.5 69.2 all-gather.2

commit v8 on v5

--- a/solution.py
+++ b/solution.py
@@ -157,8 +157,8 @@
             other_ref[u, :, cols] = y[(2 + u) * ROWS : (3 + u) * ROWS]
 
 
-def far_kernel(spread_ref, low_ref, high_ref, *refs):
-    projection_kernel(spread_ref, (low_ref, high_ref), *refs)
+def far_kernel(spread_ref, *refs):
+    projection_kernel(spread_ref, refs[:4], *refs[4:])
 
 
 def finish_kernel(*refs):
@@ -236,17 +236,20 @@
     )(query, own, other, prev_own, prev_other_0, prev_other_1)
 
     spread = lax.all_to_all(attn, ("zh", "zl", "core", "yl"), 0, 0, tiled=True)
-    far_low, far_high = x_up(before[: Z // 2]), x_down(after[Z // 2 :])
+    far1 = x_up(before[:1]), x_down(after[4:5])
+    spread, far1 = lax.optimization_barrier((spread, far1))
+    far2 = x_up(before[1:4]), x_down(after[5:])
+    far = far1[0], far2[0], far1[1], far2[1]
     f32 = jnp.float32
     parts = []
     for kernel, weights, blocks in (
         (projection_kernel, (here, before, after), 3),
-        (far_kernel, (far_low, far_high), 1),
+        (far_kernel, far, 1),
     ):
         cols = blocks * out_cols // 4
         if parts:
+            parts[2] = lax.ppermute(parts[2], "yl", swap)
             spread, parts[2] = lax.optimization_barrier((spread, parts[2]))
-            parts[2] = lax.ppermute(parts[2], "yl", swap)
         one = jax.ShapeDtypeStruct((ROWS, cols), bf16)
         keep, send, theirs = pl.pallas_call(
             kernel,

time: 207 us -> 203 us (0.981)
  blocking collectives: 35 us -> 0 us
  starting transfers between devices: 42.7 us -> 65.4 us
  local copies, waits for them, and re-layouts: 6.36 us -> 11.9 us
  waiting for transfers between devices: 83.7 us -> 87.2 us
    all_to_all x1 -> x0, blocking collectives: 35 us -> none  [body(): spread = lax.all_to_all(attn, ('zh', 'zl', 'core', 'yl'), 0, 0, tiled=True)]
    ppermute x1, waiting for transfers between devices: 21.7 us -> 7.5 us  [body(): parts[5] = lax.ppermute(parts[5], 'yl', swap)]
    all_to_all x0 -> x1, starting transfers between devices: none -> 12.8 us  [body(): spread = lax.all_to_all(attn, ('zh', 'zl', 'core', 'yl'), 0, 0, tiled=True)]
    ppermute x1, waiting for transfers between devices: 0.01 us -> 11.5 us  [body(): parts[2] = lax.ppermute(parts[2], 'yl', swap)]
    slice x2 -> x4, local copies, waits for them, and re-layouts: 0.14 us -> 5.72 us  [the longest x2 3.35 us: body(): far1 = (x_up(before[:1]), x_down(after[4:5]))]
    pallas_call x1, Pallas kernels: 17.3 us -> 12.1 us  [body(): pl.pallas_call(attention_kernel, out_shape=jax.ShapeDtypeStruct((4 * Z, R...]
    ppermute x2, waiting for transfers between devices: 0.38 us -> 4.57 us  [body(): arrived = lax.ppermute(theirs, 'core', swap)]
    ppermute x1, starting transfers between devices: 1.36 us -> 5.17 us  [body(): parts[2] = lax.ppermute(parts[2], 'yl', swap)]
  transfers between devices with their start and end apart: 16 -> 19, of which waited for: 8 -> 12; matrix products, arithmetic and copies ran while one was open for 1% -> 4% of each run, Pallas kernels for 9% -> 6%
where the time goes in v8:
time: 203 us; the launch traced here: 201 us
  waiting for transfers between devices  87.2 us (43%)
  starting transfers between devices  65.4 us (32%)
  Pallas kernels  22.8 us (11%)
  between operations  13.5 us (7%)
  local copies, waits for them, and re-layouts  11.9 us (6%)
    ppermute x6, waiting for transfers between devices, ring(): lax.ppermute(a, axis, [(i, (i + step) % size) for i in range(size)])  23.7 us
    all_to_all x1, waiting for transfers between devices, body(): query = lax.all_to_all(split, ('zh', 'zl'), 0, 0, tiled=True)  18.5 us
    all_to_all x1, waiting for transfers between devices, body(): own = lax.all_to_all(packed, ('zh', 'zl'), 0, 0, tiled=True)  16.6 us
    all_to_all x1, starting transfers between devices, body(): spread = lax.all_to_all(attn, ('zh', 'zl', 'core', 'yl'), 0, 0, tiled=True)  12.8 us
    pallas_call x1, Pallas kernels, body(): pl.pallas_call(attention_kernel, out_shape=jax.ShapeDtypeStruct((4 * Z, R...  12.1 us
    ppermute x1, waiting for transfers between devices, body(): parts[2] = lax.ppermute(parts[2], 'yl', swap)  11.5 us
    ppermute x1, starting transfers between devices, body(): other = lax.ppermute(own, 'yh', swap)  9.21 us
    ppermute x6, starting transfers between devices, ring(): lax.ppermute(a, axis, [(i, (i + step) % size) for i in range(size)])  9.11 us
  transfers between devices with their start and end apart: 19, of which 12 were waited for; matrix products, arithmetic and copies ran while one was open for 4% of the time, Pallas kernels for 6%

profile of v8, /device:TPU:1, one launch (start us, length us, event | category | flops | bytes accessed | tf_op | source)
XLA Modules:
  0.0 201.2 jit_solution(534288622331954526)
XLA Ops:
  6.5 0.0 all-gather.3.cloned.1.call-start
  6.5 1.0 dynamic_slice.3
  7.5 0.7 collective-permute-start
  8.2 0.0 copy-start
  8.2 0.9 copy-done
  9.1 0.0 copy-start.1
  9.1 0.9 copy-done.1
  10.1 0.0 copy-start.2
  10.1 0.7 copy-done.2
  10.8 0.0 copy-start.4
  10.8 0.9 pack_kv.1
  11.7 0.0 collective-permute-done
  11.7 0.0 copy-start.5
  11.7 0.7 copy-done.5
  12.4 0.0 all-gather.3.cloned.1.call-update
  12.4 9.0 %all-to-all-start.1 = ((bf16[8,144,256]{2,1,0:T(8,128)(2,1)}), bf16[8,144,256]{2,1,0:T(8,128)(2,1)S(1)}, u32[]{:S(2)}, u32[]{:S(2)}) async-start(bf16[8,144,256]{2,1,0:T(8,128)(2,1)} %pack_kv.1), calls=%async_computation.1 | async-start | bytes 1179648 | tf_op jit(solution)/shard_map/all_to_all | solution.py:202
  21.4 0.0 copy-done.4
  21.4 0.7 copy.6
  22.1 1.3 copy.7
  23.4 16.6 %all-to-all-done.1.own_ref = bf16[8,144,256]{2,1,0:T(8,128)(2,1)S(1)} async-done(((bf16[8,144,256]{2,1,0:T(8,128)(2,1)}), bf16[8,144,256]{2,1,0:T(8,128)(2,1)S(1)}, u32[]{:S(2)}, u32[]{:S(2)}) %all-to-all-start.1) | async-done | bytes 589856 | tf_op jit(solution)/shard_map/all_to_all | solution.py:202
  40.0 3.6 %all-to-all-start = ((bf16[8,128,512]{2,1,0:T(8,128)(2,1)}), bf16[8,128,512]{2,1,0:T(8,128)(2,1)S(1)}, u32[]{:S(2)}, u32[]{:S(2)}) async-start(bf16[8,128,512]{2,1,0:T(8,128)(2,1)} %bitcast.1), calls=%async_computation | async-start | bytes 2097152 | tf_op jit(solution)/shard_map/all_to_all | solution.py:214
  43.6 9.2 %collective-permute-start.1 = (bf16[8,144,256]{2,1,0:T(8,128)(2,1)S(1)}, bf16[8,144,256]{2,1,0:T(8,128)(2,1)S(1)}, u32[]{:S(2)}, u32[]{:S(2)}) collective-permute-start(bf16[8,144,256]{2,1,0:T(8,128)(2,1)S(1)} %all-to-all-done.1.own_ref), channel_id=1, source_target_pairs={{0,1},{1,0},{2,3},{3,2},{4,5},{5,4},{6,7},{7,6},{8,9},{9,8},{10,11... | collective-permute-start | bytes 1769480 | tf_op jit(solution)/shard_map/ppermute | solution.py:204
  52.8 4.0 %collective-permute-start.2 = (bf16[8,144,256]{2,1,0:T(8,128)(2,1)S(1)}, bf16[8,144,256]{2,1,0:T(8,128)(2,1)S(1)}, u32[]{:S(2)}, u32[]{:S(2)}) collective-permute-start(bf16[8,144,256]{2,1,0:T(8,128)(2,1)S(1)} %all-to-all-done.1.own_ref), channel_id=1, source_target_pairs={{0,16},{16,32},{32,48},{48,64},{64,80},{80,96},{96,112},{112,128},... | collective-permute-start | bytes 1769480 | tf_op jit(solution)/shard_map/ppermute | solution.py:205
  56.7 4.6 %collective-permute-start.3 = (bf16[8,144,256]{2,1,0:T(8,128)(2,1)S(1)}, bf16[8,144,256]{2,1,0:T(8,128)(2,1)S(1)}, u32[]{:S(2)}, u32[]{:S(2)}) collective-permute-start(bf16[8,144,256]{2,1,0:T(8,128)(2,1)S(1)} %all-to-all-done.1.own_ref), channel_id=1, source_target_pairs={{16,33},{17,32},{48,65},{49,64},{80,97},{81,96},{112,129},{113,128... | collective-permute-start | bytes 1769480 | tf_op jit(solution)/shard_map/ppermute | solution.py:206
  61.4 1.3 collective-permute-done.1.oth_ref
  62.6 1.3 collective-permute-start.4
  63.9 18.5 %all-to-all-done.q_ref = bf16[8,128,512]{2,1,0:T(8,128)(2,1)S(1)} async-done(((bf16[8,128,512]{2,1,0:T(8,128)(2,1)}), bf16[8,128,512]{2,1,0:T(8,128)(2,1)S(1)}, u32[]{:S(2)}, u32[]{:S(2)}) %all-to-all-start) | async-done | bytes 1048608 | tf_op jit(solution)/shard_map/all_to_all | solution.py:214
  82.5 0.0 all-gather.3.cloned.1.call-done
  82.5 1.2 collective-permute-start.5
  83.6 1.5 collective-permute-start.7
  85.1 0.0 collective-permute-done.2.pown_ref
  85.1 0.0 collective-permute-done.3.poth0_ref
  85.2 0.0 collective-permute-done.4.poth1_ref
  85.2 12.1 %attention.1 = bf16[32,128,128]{2,1,0:T(8,128)(2,1)} custom-call(bf16[8,128,512]{2,1,0:T(8,128)(2,1)S(1)} %all-to-all-done.q_ref, bf16[8,144,256]{2,1,0:T(8,128)(2,1)S(1)} %all-to-all-done.1.own_ref, bf16[8,144,256]{2,1,0:T(8,128)(2,1)S(1)} %collective-permute-done.1.oth_ref, bf16[8,144,256]{2,1,0:T(8,128)(2,1)S(1)} %collective-permute-done.2.pown_ref, ...), custom_call_target="tpu_custom_call" | custom-call | flops 16000000000 | bytes 6000000 | tf_op jit(solution)/shard_map/attention/pallas_call | solution.py:217
  97.3 12.8 %all-to-all-start.2 = ((bf16[32,128,128]{2,1,0:T(8,128)(2,1)}), bf16[32,128,128]{2,1,0:T(8,128)(2,1)S(1)}, u32[]{:S(2)}, u32[]{:S(2)}) async-start(bf16[32,128,128]{2,1,0:T(8,128)(2,1)} %attention.1), calls=%async_computation.2 | async-start | bytes 2097152 | tf_op jit(solution)/shard_map/all_to_all | solution.py:238
  110.1 18.9 %collective-permute-done.5.refs_1_ = bf16[8,128,1024]{2,1,0:T(8,128)(2,1)} collective-permute-done((bf16[8,128,1024]{2,1,0:T(8,128)(2,1)}, bf16[8,128,1024]{2,1,0:T(8,128)(2,1)}, u32[]{:S(2)}, u32[]{:S(2)}) %collective-permute-start.5) | collective-permute-done | bytes 2097184 | tf_op jit(solution)/shard_map/ppermute | solution.py:193
  129.0 1.7 slice.24
  130.7 0.0 collective-permute-start.6
  130.7 0.0 collective-permute-done.7.refs_2_
  130.7 1.7 slice.25
  132.3 2.7 %collective-permute-start.8 = (bf16[1,128,1024]{2,1,0:T(8,128)(2,1)}, bf16[1,128,1024]{2,1,0:T(8,128)(2,1)}, u32[]{:S(2)}, u32[]{:S(2)}) collective-permute-start(bf16[1,128,1024]{2,1,0:T(8,128)(2,1)} %slice.25), channel_id=1, source_target_pairs={{0,192},{64,0},{128,64},{192,128},{1,193},{65,1},{129,65},{193,129... | collective-permute-start | bytes 786440 | tf_op jit(solution)/shard_map/ppermute | solution.py:193
  135.0 3.5 %all-to-all-done.2.spread_ref = bf16[32,128,128]{2,1,0:T(8,128)(2,1)S(1)} async-done(((bf16[32,128,128]{2,1,0:T(8,128)(2,1)}), bf16[32,128,128]{2,1,0:T(8,128)(2,1)S(1)}, u32[]{:S(2)}, u32[]{:S(2)}) %all-to-all-start.2) | async-done | bytes 1048608 | tf_op jit(solution)/shard_map/all_to_all | solution.py:238
  138.5 0.0 collective-permute-done.6.refs_0_
  138.5 0.1 collective-permute-done.8.refs_2_
  138.6 0.0 copy-done.3
  138.6 5.6 %projection.2 = (bf16[128,3072]{1,0:T(8,128)(2,1)S(1)}, bf16[128,3072]{1,0:T(8,128)(2,1)S(1)}, bf16[2,128,3072]{2,1,0:T(8,128)(2,1)S(1)}) custom-call(bf16[32,128,128]{2,1,0:T(8,128)(2,1)S(1)} %all-to-all-done.2.spread_ref, bf16[8,128,1024]{2,1,0:T(8,128)(2,1)S(1)} %bitcast.17, bf16[8,128,1024]{2,1,0:T(8,128)(2,1)} %collective-permute-done.5.refs_1_, ...), custom_call_target="tpu_custom_call" | custom-call | flops 3221225472 | bytes 9437184 | tf_op jit(solution)/shard_map/projection/pallas_call | solution.py:254
  144.3 4.3 %collective-permute-start.9 = (bf16[2,128,3072]{2,1,0:T(8,128)(2,1)S(1)}, bf16[2,128,3072]{2,1,0:T(8,128)(2,1)S(1)}, u32[]{:S(2)}, u32[]{:S(2)}) collective-permute-start(bf16[2,128,3072]{2,1,0:T(8,128)(2,1)S(1)} %get-tuple-element.26), channel_id=1, source_target_pairs={{0,16},{16,0},{1,17},{17,1},{2,18},{18,2},{3,19},{19,3},{4,20},{20... | collective-permute-start | bytes 4718600 | tf_op jit(solution)/shard_map/ppermute | solution.py:266
  148.6 3.0 %collective-permute-done.9.refs_1_ = bf16[2,128,3072]{2,1,0:T(8,128)(2,1)S(1)} collective-permute-done((bf16[2,128,3072]{2,1,0:T(8,128)(2,1)S(1)}, bf16[2,128,3072]{2,1,0:T(8,128)(2,1)S(1)}, u32[]{:S(2)}, u32[]{:S(2)}) %collective-permute-start.9) | collective-permute-done | bytes 1572896 | tf_op jit(solution)/shard_map/ppermute | solution.py:266
  151.6 0.2 fusion
  151.8 5.2 %collective-permute-start.10 = (bf16[128,3072]{1,0:T(8,128)(2,1)S(1)}, bf16[128,3072]{1,0:T(8,128)(2,1)S(1)}, u32[]{:S(2)}, u32[]{:S(2)}) collective-permute-start(bf16[128,3072]{1,0:T(8,128)(2,1)S(1)} %fusion), channel_id=1, source_target_pairs={{0,32},{32,0},{1,33},{33,1},{2,34},{34,2},{3,35},{35,3},{4,36},{36... | collective-permute-start | bytes 2359304 | tf_op jit(solution)/shard_map/ppermute | solution.py:251
  157.0 1.2 slice.27
  158.2 0.7 collective-permute-start.11
  158.9 1.2 slice.28
  160.1 3.0 %collective-permute-start.12 = (bf16[3,128,1024]{2,1,0:T(8,128)(2,1)S(1)}, bf16[3,128,1024]{2,1,0:T(8,128)(2,1)S(1)}, u32[]{:S(2)}, u32[]{:S(2)}) collective-permute-start(bf16[3,128,1024]{2,1,0:T(8,128)(2,1)S(1)} %slice.28), channel_id=1, source_target_pairs={{0,192},{64,0},{128,64},{192,128},{1,193},{65,1},{129,65},{193,129... | collective-permute-start | bytes 2359304 | tf_op jit(solution)/shard_map/ppermute | solution.py:193
  163.1 11.5 %collective-permute-done.10.refs_2_ = bf16[128,3072]{1,0:T(8,128)(2,1)S(1)} collective-permute-done((bf16[128,3072]{1,0:T(8,128)(2,1)S(1)}, bf16[128,3072]{1,0:T(8,128)(2,1)S(1)}, u32[]{:S(2)}, u32[]{:S(2)}) %collective-permute-start.10) | collective-permute-done | bytes 786464 | tf_op jit(solution)/shard_map/ppermute | solution.py:251
  174.6 4.4 %collective-permute-done.11.refs_1_ = bf16[3,128,1024]{2,1,0:T(8,128)(2,1)S(1)} collective-permute-done((bf16[3,128,1024]{2,1,0:T(8,128)(2,1)S(1)}, bf16[3,128,1024]{2,1,0:T(8,128)(2,1)S(1)}, u32[]{:S(2)}, u32[]{:S(2)}) %collective-permute-start.11) | collective-permute-done | bytes 786464 | tf_op jit(solution)/shard_map/ppermute | solution.py:193
  179.0 0.4 collective-permute-done.12.refs_3_
  179.4 2.8 %projection.3 = (bf16[128,1024]{1,0:T(8,128)(2,1)S(1)}, bf16[128,1024]{1,0:T(8,128)(2,1)S(1)}, bf16[2,128,1024]{2,1,0:T(8,128)(2,1)S(1)}) custom-call(bf16[32,128,128]{2,1,0:T(8,128)(2,1)S(1)} %all-to-all-done.2.spread_ref, bf16[1,128,1024]{2,1,0:T(8,128)(2,1)S(1)} %collective-permute-done.6.refs_0_, ...), custom_call_target="tpu_custom_call" | custom-call | flops 1073741824 | bytes 3145728 | tf_op jit(solution)/shard_map/projection/pallas_call | solution.py:254
  182.1 1.6 collective-permute-start.13
  183.7 1.5 collective-permute-done.13.refs_4_
  185.3 0.1 fusion.1
  185.4 0.1 collective-permute-start.14
  185.5 7.5 %collective-permute-done.14.refs_5_ = bf16[128,1024]{1,0:T(8,128)(2,1)S(1)} collective-permute-done((bf16[128,1024]{1,0:T(8,128)(2,1)S(1)}, bf16[128,1024]{1,0:T(8,128)(2,1)S(1)}, u32[]{:S(2)}, u32[]{:S(2)}) %collective-permute-start.14) | collective-permute-done | bytes 262176 | tf_op jit(solution)/shard_map/ppermute | solution.py:268
  193.0 1.3 finish.1
  (1 shorter events, 0.0 us)
Async XLA Ops:
  6.5 75.9 %all-gather.3.cloned.1.call-start = ((), (), s32[]{:S(2)}) async-start(), calls=%async_computation.3 | async-start | bytes 2359296 | tf_op jit(solution)/shard_map/all_gather | solution.py:203
  7.5 4.2 %collective-permute-start = (bf16[128,1024]{1,0:T(8,128)(2,1)S(1)}, bf16[128,1024]{1,0:T(8,128)(2,1)S(1)}, u32[]{:S(2)}, u32[]{:S(2)}) collective-permute-start(bf16[128,1024]{1,0:T(8,128)(2,1)S(1)} %dynamic_slice.3), channel_id=1, source_target_pairs={{0,0},{1,32},{32,1},{33,33},{2,2},{3,34},{34,3},{35,35},{4,4},{5,3... | collective-permute-start | bytes 786440 | tf_op jit(solution)/shard_map/ppermute | solution.py:200
  8.2 1.0 copy-start
  9.1 0.9 copy-start.1
  10.1 0.7 copy-start.2
  10.8 10.7 %copy-start.4 = (bf16[128,4096]{1,0:T(8,128)(2,1)S(1)}, bf16[128,4096]{1,0:T(8,128)(2,1)}, u32[]{:S(2)}) copy-start(bf16[128,4096]{1,0:T(8,128)(2,1)} %param.5) | copy-start | bytes 3145732
  11.7 0.7 copy-start.5
  12.4 27.6 %all-to-all-start.1 = ((bf16[8,144,256]{2,1,0:T(8,128)(2,1)}), bf16[8,144,256]{2,1,0:T(8,128)(2,1)S(1)}, u32[]{:S(2)}, u32[]{:S(2)}) async-start(bf16[8,144,256]{2,1,0:T(8,128)(2,1)} %pack_kv.1), calls=%async_computation.1 | async-start | bytes 1179648 | tf_op jit(solution)/shard_map/all_to_all | solution.py:202
  40.0 42.5 %all-to-all-start = ((bf16[8,128,512]{2,1,0:T(8,128)(2,1)}), bf16[8,128,512]{2,1,0:T(8,128)(2,1)S(1)}, u32[]{:S(2)}, u32[]{:S(2)}) async-start(bf16[8,128,512]{2,1,0:T(8,128)(2,1)} %bitcast.1), calls=%async_computation | async-start | bytes 2097152 | tf_op jit(solution)/shard_map/all_to_all | solution.py:214
  43.6 19.1 %collective-permute-start.1 = (bf16[8,144,256]{2,1,0:T(8,128)(2,1)S(1)}, bf16[8,144,256]{2,1,0:T(8,128)(2,1)S(1)}, u32[]{:S(2)}, u32[]{:S(2)}) collective-permute-start(bf16[8,144,256]{2,1,0:T(8,128)(2,1)S(1)} %all-to-all-done.1.own_ref), channel_id=1, source_target_pairs={{0,1},{1,0},{2,3},{3,2},{4,5},{5,4},{6,7},{7,6},{8,9},{9,8},{10,11... | collective-permute-start | bytes 1769480 | tf_op jit(solution)/shard_map/ppermute | solution.py:204
  52.8 32.4 %collective-permute-start.2 = (bf16[8,144,256]{2,1,0:T(8,128)(2,1)S(1)}, bf16[8,144,256]{2,1,0:T(8,128)(2,1)S(1)}, u32[]{:S(2)}, u32[]{:S(2)}) collective-permute-start(bf16[8,144,256]{2,1,0:T(8,128)(2,1)S(1)} %all-to-all-done.1.own_ref), channel_id=1, source_target_pairs={{0,16},{16,32},{32,48},{48,64},{64,80},{80,96},{96,112},{112,128},... | collective-permute-start | bytes 1769480 | tf_op jit(solution)/shard_map/ppermute | solution.py:205
  56.7 28.4 %collective-permute-start.3 = (bf16[8,144,256]{2,1,0:T(8,128)(2,1)S(1)}, bf16[8,144,256]{2,1,0:T(8,128)(2,1)S(1)}, u32[]{:S(2)}, u32[]{:S(2)}) collective-permute-start(bf16[8,144,256]{2,1,0:T(8,128)(2,1)S(1)} %all-to-all-done.1.own_ref), channel_id=1, source_target_pairs={{16,33},{17,32},{48,65},{49,64},{80,97},{81,96},{112,129},{113,128... | collective-permute-start | bytes 1769480 | tf_op jit(solution)/shard_map/ppermute | solution.py:206
  62.6 22.5 %collective-permute-start.4 = (bf16[8,144,256]{2,1,0:T(8,128)(2,1)S(1)}, bf16[8,144,256]{2,1,0:T(8,128)(2,1)}, u32[]{:S(2)}, u32[]{:S(2)}) collective-permute-start(bf16[8,144,256]{2,1,0:T(8,128)(2,1)S(1)} %collective-permute-done.1.oth_ref), channel_id=1, source_target_pairs={{0,16},{1,17},{2,18},{3,19},{4,20},{5,21},{6,22},{7,23},{8,24},{9,... | collective-permute-start | bytes 1769480 | tf_op jit(solution)/shard_map/ppermute | solution.py:211
  82.5 46.5 %collective-permute-start.5 = (bf16[8,128,1024]{2,1,0:T(8,128)(2,1)}, bf16[8,128,1024]{2,1,0:T(8,128)(2,1)}, u32[]{:S(2)}, u32[]{:S(2)}) collective-permute-start(bf16[8,128,1024]{2,1,0:T(8,128)(2,1)} %bitcast.15), channel_id=1, source_target_pairs={{0,64},{64,128},{128,192},{192,0},{1,65},{65,129},{129,193},{193,1... | collective-permute-start | bytes 6291464 | tf_op jit(solution)/shard_map/ppermute | solution.py:193
  83.6 47.0 %collective-permute-start.7 = (bf16[8,128,1024]{2,1,0:T(8,128)(2,1)}, bf16[8,128,1024]{2,1,0:T(8,128)(2,1)}, u32[]{:S(2)}, u32[]{:S(2)}) collective-permute-start(bf16[8,128,1024]{2,1,0:T(8,128)(2,1)} %bitcast.16), channel_id=1, source_target_pairs={{0,192},{64,0},{128,64},{192,128},{1,193},{65,1},{129,65},{193,129... | collective-permute-start | bytes 6291464 | tf_op jit(solution)/shard_map/ppermute | solution.py:193
  97.3 41.4 %copy-start.3 = (bf16[1024,1024]{1,0:T(8,128)(2,1)S(1)}, bf16[1024,1024]{1,0:T(8,128)(2,1)}, u32[]{:S(2)}) copy-start(bf16[1024,1024]{1,0:T(8,128)(2,1)} %all-gather.3.cloned.1.call-done) | copy-start | bytes 6291460
  97.3 41.3 %all-to-all-start.2 = ((bf16[32,128,128]{2,1,0:T(8,128)(2,1)}), bf16[32,128,128]{2,1,0:T(8,128)(2,1)S(1)}, u32[]{:S(2)}, u32[]{:S(2)}) async-start(bf16[32,128,128]{2,1,0:T(8,128)(2,1)} %attention.1), calls=%async_computation.2 | async-start | bytes 2097152 | tf_op jit(solution)/shard_map/all_to_all | solution.py:238
  130.7 7.9 %collective-permute-start.6 = (bf16[1,128,1024]{2,1,0:T(8,128)(2,1)}, bf16[1,128,1024]{2,1,0:T(8,128)(2,1)S(1)}, u32[]{:S(2)}, u32[]{:S(2)}) collective-permute-start(bf16[1,128,1024]{2,1,0:T(8,128)(2,1)} %slice.24), channel_id=1, source_target_pairs={{0,64},{64,128},{128,192},{192,0},{1,65},{65,129},{129,193},{193,1... | collective-permute-start | bytes 786440 | tf_op jit(solution)/shard_map/ppermute | solution.py:193
  132.3 6.3 %collective-permute-start.8 = (bf16[1,128,1024]{2,1,0:T(8,128)(2,1)}, bf16[1,128,1024]{2,1,0:T(8,128)(2,1)}, u32[]{:S(2)}, u32[]{:S(2)}) collective-permute-start(bf16[1,128,1024]{2,1,0:T(8,128)(2,1)} %slice.25), channel_id=1, source_target_pairs={{0,192},{64,0},{128,64},{192,128},{1,193},{65,1},{129,65},{193,129... | collective-permute-start | bytes 786440 | tf_op jit(solution)/shard_map/ppermute | solution.py:193
  144.3 7.3 %collective-permute-start.9 = (bf16[2,128,3072]{2,1,0:T(8,128)(2,1)S(1)}, bf16[2,128,3072]{2,1,0:T(8,128)(2,1)S(1)}, u32[]{:S(2)}, u32[]{:S(2)}) collective-permute-start(bf16[2,128,3072]{2,1,0:T(8,128)(2,1)S(1)} %get-tuple-element.26), channel_id=1, source_target_pairs={{0,16},{16,0},{1,17},{17,1},{2,18},{18,2},{3,19},{19,3},{4,20},{20... | collective-permute-start | bytes 4718600 | tf_op jit(solution)/shard_map/ppermute | solution.py:266
  151.8 22.8 %collective-permute-start.10 = (bf16[128,3072]{1,0:T(8,128)(2,1)S(1)}, bf16[128,3072]{1,0:T(8,128)(2,1)S(1)}, u32[]{:S(2)}, u32[]{:S(2)}) collective-permute-start(bf16[128,3072]{1,0:T(8,128)(2,1)S(1)} %fusion), channel_id=1, source_target_pairs={{0,32},{32,0},{1,33},{33,1},{2,34},{34,2},{3,35},{35,3},{4,36},{36... | collective-permute-start | bytes 2359304 | tf_op jit(solution)/shard_map/ppermute | solution.py:251
  158.2 20.8 %collective-permute-start.11 = (bf16[3,128,1024]{2,1,0:T(8,128)(2,1)S(1)}, bf16[3,128,1024]{2,1,0:T(8,128)(2,1)S(1)}, u32[]{:S(2)}, u32[]{:S(2)}) collective-permute-start(bf16[3,128,1024]{2,1,0:T(8,128)(2,1)S(1)} %slice.27), channel_id=1, source_target_pairs={{0,64},{64,128},{128,192},{192,0},{1,65},{65,129},{129,193},{193,1... | collective-permute-start | bytes 2359304 | tf_op jit(solution)/shard_map/ppermute | solution.py:193
  160.1 19.3 %collective-permute-start.12 = (bf16[3,128,1024]{2,1,0:T(8,128)(2,1)S(1)}, bf16[3,128,1024]{2,1,0:T(8,128)(2,1)S(1)}, u32[]{:S(2)}, u32[]{:S(2)}) collective-permute-start(bf16[3,128,1024]{2,1,0:T(8,128)(2,1)S(1)} %slice.28), channel_id=1, source_target_pairs={{0,192},{64,0},{128,64},{192,128},{1,193},{65,1},{129,65},{193,129... | collective-permute-start | bytes 2359304 | tf_op jit(solution)/shard_map/ppermute | solution.py:193
  182.1 3.1 %collective-permute-start.13 = (bf16[2,128,1024]{2,1,0:T(8,128)(2,1)S(1)}, bf16[2,128,1024]{2,1,0:T(8,128)(2,1)S(1)}, u32[]{:S(2)}, u32[]{:S(2)}) collective-permute-start(bf16[2,128,1024]{2,1,0:T(8,128)(2,1)S(1)} %get-tuple-element.33), channel_id=1, source_target_pairs={{0,16},{16,0},{1,17},{17,1},{2,18},{18,2},{3,19},{19,3},{4,20},{20... | collective-permute-start | bytes 1572872 | tf_op jit(solution)/shard_map/ppermute | solution.py:266
  185.4 7.6 %collective-permute-start.14 = (bf16[128,1024]{1,0:T(8,128)(2,1)S(1)}, bf16[128,1024]{1,0:T(8,128)(2,1)S(1)}, u32[]{:S(2)}, u32[]{:S(2)}) collective-permute-start(bf16[128,1024]{1,0:T(8,128)(2,1)S(1)} %fusion.1), channel_id=1, source_target_pairs={{0,32},{32,0},{1,33},{33,1},{2,34},{34,2},{3,35},{35,3},{4,36},{36... | collective-permute-start | bytes 786440 | tf_op jit(solution)/shard_map/ppermute | solution.py:268
Sparse Core Ops, SparseCore 0:
  12.5 69.1 all-gather.2

commit v9 on v7

--- a/solution.py
+++ b/solution.py
@@ -16,6 +16,7 @@
 PAIRS = 16
 EXP2_SCALE = math.log2(math.e) / math.sqrt(HEAD_DIM)
 MASKED = -1e30
+Z_ORDER = (0, 7, 1, 2, 3, 4, 5, 6)
 MIB = 1024 * 1024
 
 AXES = ("x", "yl", "core", "zh", "zl", "yh")
@@ -127,6 +128,13 @@
             o_ref[4 * z + 2 * (g % 2) + g // 2] = out.astype(jnp.bfloat16)
 
 
+def pick_kernel(w_ref, two_ref, three_ref):
+    z_here = 2 * lax.axis_index("zh") + lax.axis_index("zl")
+    for k in range(Z - 3):
+        ref, at = (two_ref, k) if k < 2 else (three_ref, k - 2)
+        ref[at] = w_ref[lax.rem(z_here + 2 + k, Z)]
+
+
 def projection_kernel(spread_ref, *refs):
     w_refs, (keep_ref, send_ref, other_ref, a_buf) = refs[:-4], refs[-4:]
     step, steps = pl.program_id(0), pl.num_programs(0)
@@ -136,18 +144,23 @@
     def _():
         core = lax.axis_index("core")
         yl = lax.axis_index("yl")
+        z_here = 2 * lax.axis_index("zh") + lax.axis_index("zl")
         for t in range(2):
             for u in range(2):
                 source = 2 * (core if t == 0 else 1 - core) + (yl if u == 0 else 1 - yl)
                 at = (2 * t + u) * ROWS
-                for z in range(Z):
-                    a_buf[at : at + ROWS, z * ROWS : (z + 1) * ROWS] = spread_ref[4 * z + source]
-
-    half, piece = Z * ROWS // 2, w_refs[0].shape[-1]
+                for k, shift in enumerate(Z_ORDER):
+                    z = lax.rem(z_here + shift, Z)
+                    a_buf[at : at + ROWS, k * ROWS : (k + 1) * ROWS] = spread_ref[4 * z + source]
+
+    piece = w_refs[0].shape[-1]
     for n, shift in enumerate((0, 3, 1, 2)):
-        low, high = (ref[...].reshape(half, piece) for ref in w_refs[2 * n : 2 * n + 2])
-        y = jnp.dot(a_buf[:, 0:half], low, preferred_element_type=jnp.float32)
-        y = y + jnp.dot(a_buf[:, half : 2 * half], high, preferred_element_type=jnp.float32)
+        y, at = None, 0
+        for part in w_refs[3 * n : 3 * n + 3]:
+            depth = part.shape[0] * ROWS
+            w = part[...].reshape(depth, piece)
+            term = jnp.dot(a_buf[:, at : at + depth], w, preferred_element_type=jnp.float32)
+            y, at = (term if y is None else y + term), at + depth
         y = y.astype(jnp.bfloat16)
         block = lax.rem(x + shift, 4) * steps + step
         cols = pl.ds(pl.multiple_of(block * piece, piece), piece)
@@ -189,6 +202,14 @@
     piece, packed = lax.optimization_barrier((piece, packed))
     own = lax.all_to_all(packed, ("zh", "zl"), 0, 0, tiled=True)
     here = lax.all_gather(piece, ("zh", "zl"), axis=0, tiled=False)
+    up1 = ring(("zh", "zl"), Z, 1)(piece)
+    down1 = ring(("zh", "zl"), Z, -1)(piece)
+
+    own = lax.all_to_all(packed, ("zh", "zl"), 0, 0, tiled=True)
+    own, up1, down1 = lax.optimization_barrier((own, up1, down1))
+    group1 = jnp.stack([piece, up1, down1])
+    before1, after1 = x_up(group1), x_down(group1)
+    far1 = x_up(before1)
     other = lax.ppermute(own, "yh", swap)
     prev_own = lax.ppermute(own, BLK, [(i, i + 1) for i in range(15)])
     prev_other_0 = lax.ppermute(
@@ -200,10 +221,15 @@
 
     split = queries.reshape(ROWS, Z, GROUP * HEAD_DIM).transpose(1, 0, 2)
     query = lax.all_to_all(split, ("zh", "zl"), 0, 0, tiled=True)
-    query, here = lax.optimization_barrier((query, here))
-    low, high = here[: Z // 2], here[Z // 2 :]
-    before_low, after_high = x_up(low), x_down(high)
-    before_high, after_low = x_up(high), x_down(low)
+    query, here, far1, after1 = lax.optimization_barrier((query, here, far1, after1))
+    group2, group3 = pl.pallas_call(
+        pick_kernel,
+        out_shape=[jax.ShapeDtypeStruct((n, ROWS, out_cols // 4), bf16) for n in (2, 3)],
+        compiler_params=params(16),
+        name="pick",
+    )(here)
+    before2, after2 = x_up(group2), x_down(group2)
+    before3, after3 = x_up(group3), x_down(group3)
     attn = pl.pallas_call(
         attention_kernel,
         out_shape=jax.ShapeDtypeStruct((4 * Z, ROWS, HEAD_DIM), bf16),
@@ -225,9 +251,12 @@
         name="attention",
     )(query, own, other, prev_own, prev_other_0, prev_other_1)
 
-    far_low, far_high = x_up(before_low), x_down(after_high)
+    attn, before2, after3 = lax.optimization_barrier((attn, before2, after3))
     spread = lax.all_to_all(attn, ("zh", "zl", "core", "yl"), 0, 0, tiled=True)
-    weights = (low, high, before_low, before_high, after_low, after_high, far_low, far_high)
+    far2, far3 = x_up(before2), x_down(after3)
+    weights = (
+        group1, group2, group3, before1, before2, before3, after1, after2, after3, far1, far2, far3
+    )
     f32 = jnp.float32
     one = jax.ShapeDtypeStruct((ROWS, out_cols), bf16)
     steps = 4
@@ -236,11 +265,14 @@
         projection_kernel,
         grid=(steps,),
         in_specs=[whole]
-        + [pl.BlockSpec((Z // 2, ROWS, out_cols // 4 // steps), lambda i: (0, 0, i))] * len(weights),
+        + [
+            pl.BlockSpec((w.shape[0], ROWS, out_cols // 4 // steps), lambda i: (0, 0, i))
+            for w in weights
+        ],
         out_specs=[whole] * 3,
         out_shape=[one, one, jax.ShapeDtypeStruct((2, ROWS, out_cols), bf16)],
         scratch_shapes=[pltpu.VMEM((4 * ROWS, Z * ROWS), bf16)],
-        compiler_params=params(40),
+        compiler_params=params(54),
         cost_estimate=pl.CostEstimate(
             flops=2 * 4 * ROWS * Z * ROWS * out_cols,
             bytes_accessed=2 * Z * ROWS * out_cols + 8 * ROWS * out_cols,

time: 214 us -> 216 us (level)
  waiting for transfers between devices: 105 us -> 75 us
  starting transfers between devices: 60.7 us -> 82.7 us
  Pallas kernels: 22.8 us -> 31.4 us
  other arithmetic: 0.25 us -> 2.46 us
    all_to_all x1, waiting for transfers between devices: 18 us -> 0.01 us  [body(): query = lax.all_to_all(split, ('zh', 'zl'), 0, 0, tiled=True)]
    ppermute x6 -> x11, waiting for transfers between devices: 42.4 us -> 32.3 us  [ring(): lax.ppermute(a, axis, [(i, (i + step) % size) for i in range(size)])]
    all_to_all x1, starting transfers between devices: 10.8 us -> 18.1 us  [body(): spread = lax.all_to_all(attn, ('zh', 'zl', 'core', 'yl'), 0, 0, tiled=True)]
    ppermute x1, starting transfers between devices: 7.43 us -> 13.8 us  [body(): lax.ppermute(own, BLK + ('yh',), [(2 * i + h, 2 * (i + 1) + 1 - h) for i...]
    ppermute x1, starting transfers between devices: 1.91 us -> 7.64 us  [body(): prev_own = lax.ppermute(own, BLK, [(i, i + 1) for i in range(15)])]
    pallas_call x1, Pallas kernels: 13.4 us -> 18 us  [body(): pl.pallas_call(attention_kernel, out_shape=jax.ShapeDtypeStruct((4 * Z, R...]
    pallas_call x1, Pallas kernels: 7.12 us -> 11 us  [body(): pl.pallas_call(projection_kernel, grid=(steps,), in_specs=[whole] + [pl.B...]
    ppermute x6 -> x11, starting transfers between devices: 14.5 us -> 15.5 us  [ring(): lax.ppermute(a, axis, [(i, (i + step) % size) for i in range(size)])]
  transfers between devices with their start and end apart: 17 -> 22, of which waited for: 8 -> 8; matrix products, arithmetic and copies ran while one was open for 2% -> 1% of each run, Pallas kernels for 7% -> 9%
where the time goes in v9:
time: 216 us
  starting transfers between devices  82.7 us (38%)
  waiting for transfers between devices  75 us (35%)
  Pallas kernels  31.4 us (15%)
  between operations  13.6 us (6%)
  local copies, waits for them, and re-layouts  11.3 us (5%)
  other arithmetic  2.46 us (1%)
    ppermute x11, waiting for transfers between devices, ring(): lax.ppermute(a, axis, [(i, (i + step) % size) for i in range(size)])  32.3 us
    ppermute x1, waiting for transfers between devices, body(): lax.ppermute((send.astype(f32) + arrived[1].astype(f32)).astype(bf16), 'y...  23 us
    all_to_all x1, starting transfers between devices, body(): spread = lax.all_to_all(attn, ('zh', 'zl', 'core', 'yl'), 0, 0, tiled=True)  18.1 us
    pallas_call x1, Pallas kernels, body(): pl.pallas_call(attention_kernel, out_shape=jax.ShapeDtypeStruct((4 * Z, R...  18 us
    ppermute x11, starting transfers between devices, ring(): lax.ppermute(a, axis, [(i, (i + step) % size) for i in range(size)])  15.5 us
    all_to_all x1, waiting for transfers between devices, body(): own = lax.all_to_all(packed, ('zh', 'zl'), 0, 0, tiled=True)  14.8 us
    ppermute x1, starting transfers between devices, body(): lax.ppermute(own, BLK + ('yh',), [(2 * i + h, 2 * (i + 1) + 1 - h) for i...  13.8 us
    pallas_call x1, Pallas kernels, body(): pl.pallas_call(projection_kernel, grid=(steps,), in_specs=[whole] + [pl.B...  11 us
  transfers between devices with their start and end apart: 22, of which 8 were waited for; matrix products, arithmetic and copies ran while one was open for 1% of the time, Pallas kernels for 9%

profile of v9, /device:TPU:1, one launch (start us, length us, event | category | flops | bytes accessed | tf_op | source)
XLA Modules:
  0.0 216.5 jit_solution(11790495024408383444)
XLA Ops:
  6.5 1.0 dynamic_slice.3
  7.5 0.7 collective-permute-start
  8.2 0.0 copy-start.2
  8.2 0.9 copy-done.2
  9.1 0.9 copy-done.3
  10.1 0.7 copy-done.4
  10.8 0.9 pack_kv.1
  11.7 0.0 collective-permute-done
  11.7 0.7 copy-done.9
  12.4 0.0 all-gather.3.cloned.1.call-update
  12.4 9.0 %all-to-all-start.1 = ((bf16[8,144,256]{2,1,0:T(8,128)(2,1)}), bf16[8,144,256]{2,1,0:T(8,128)(2,1)S(1)}, u32[]{:S(2)}, u32[]{:S(2)}) async-start(bf16[8,144,256]{2,1,0:T(8,128)(2,1)} %pack_kv.1), calls=%async_computation.1 | async-start | bytes 1179648 | tf_op jit(solution)/shard_map/all_to_all | solution.py:208
  21.5 2.7 %collective-permute-start.2 = (bf16[128,1024]{1,0:T(8,128)(2,1)}, bf16[128,1024]{1,0:T(8,128)(2,1)S(1)}, u32[]{:S(2)}, u32[]{:S(2)}) collective-permute-start(bf16[128,1024]{1,0:T(8,128)(2,1)} %copy-done.9), channel_id=1, source_target_pairs={{0,14},{2,0},{4,2},{6,4},{8,6},{10,8},{12,10},{14,12},{1,15},{3,1}... | collective-permute-start | bytes 786440 | tf_op jit(solution)/shard_map/ppermute | solution.py:194
  24.1 0.0 collective-permute-start.1
  24.1 0.7 copy.6
  24.8 1.3 copy.7
  26.1 14.8 %all-to-all-done.1.own_ref = bf16[8,144,256]{2,1,0:T(8,128)(2,1)S(1)} async-done(((bf16[8,144,256]{2,1,0:T(8,128)(2,1)}), bf16[8,144,256]{2,1,0:T(8,128)(2,1)S(1)}, u32[]{:S(2)}, u32[]{:S(2)}) %all-to-all-start.1) | async-done | bytes 589856 | tf_op jit(solution)/shard_map/all_to_all | solution.py:208
  40.9 3.6 %all-to-all-start = ((bf16[8,128,512]{2,1,0:T(8,128)(2,1)}), bf16[8,128,512]{2,1,0:T(8,128)(2,1)S(1)}, u32[]{:S(2)}, u32[]{:S(2)}) async-start(bf16[8,128,512]{2,1,0:T(8,128)(2,1)} %bitcast.1), calls=%async_computation | async-start | bytes 2097152 | tf_op jit(solution)/shard_map/all_to_all | solution.py:223
  44.5 1.0 collective-permute-done.2
  45.5 0.5 collective-permute-done.1
  46.0 1.0 pad_maximum_fusion.refs_0_
  47.0 1.2 collective-permute-start.3
  48.2 10.5 %collective-permute-start.6 = (bf16[8,144,256]{2,1,0:T(8,128)(2,1)S(1)}, bf16[8,144,256]{2,1,0:T(8,128)(2,1)S(1)}, u32[]{:S(2)}, u32[]{:S(2)}) collective-permute-start(bf16[8,144,256]{2,1,0:T(8,128)(2,1)S(1)} %all-to-all-done.1.own_ref), channel_id=1, source_target_pairs={{0,1},{1,0},{2,3},{3,2},{4,5},{5,4},{6,7},{7,6},{8,9},{9,8},{10,11... | collective-permute-start | bytes 1769480 | tf_op jit(solution)/shard_map/ppermute | solution.py:213
  58.7 1.5 collective-permute-start.5
  60.2 2.5 %collective-permute-done.3.refs_3_ = bf16[3,128,1024]{2,1,0:T(8,128)(2,1)S(1)} collective-permute-done((bf16[3,128,1024]{2,1,0:T(8,128)(2,1)}, bf16[3,128,1024]{2,1,0:T(8,128)(2,1)S(1)}, u32[]{:S(2)}, u32[]{:S(2)}) %collective-permute-start.3) | collective-permute-done | bytes 786464 | tf_op jit(solution)/shard_map/ppermute | solution.py:194
  62.7 0.4 collective-permute-start.4
  63.1 13.8 %collective-permute-start.8 = (bf16[8,144,256]{2,1,0:T(8,128)(2,1)S(1)}, bf16[8,144,256]{2,1,0:T(8,128)(2,1)}, u32[]{:S(2)}, u32[]{:S(2)}) collective-permute-start(bf16[8,144,256]{2,1,0:T(8,128)(2,1)S(1)} %all-to-all-done.1.own_ref), channel_id=1, source_target_pairs={{16,33},{17,32},{48,65},{49,64},{80,97},{81,96},{112,129},{113,128... | collective-permute-start | bytes 1769480 | tf_op jit(solution)/shard_map/ppermute | solution.py:215
  76.9 7.6 %collective-permute-start.7 = (bf16[8,144,256]{2,1,0:T(8,128)(2,1)S(1)}, bf16[8,144,256]{2,1,0:T(8,128)(2,1)}, u32[]{:S(2)}, u32[]{:S(2)}) collective-permute-start(bf16[8,144,256]{2,1,0:T(8,128)(2,1)S(1)} %all-to-all-done.1.own_ref), channel_id=1, source_target_pairs={{0,16},{16,32},{32,48},{48,64},{64,80},{80,96},{96,112},{112,128},... | collective-permute-start | bytes 1769480 | tf_op jit(solution)/shard_map/ppermute | solution.py:214
  84.6 0.0 collective-permute-done.6.oth_ref
  84.6 1.3 collective-permute-start.9
  85.9 0.0 all-to-all-done.q_ref
  85.9 0.0 collective-permute-done.5.refs_6_
  85.9 0.0 collective-permute-done.4.refs_9_
  85.9 0.0 all-gather.3.cloned.1.call-done
  86.0 1.6 copy-done
  87.6 0.1 pick.1
  87.7 1.3 collective-permute-start.10
  89.0 1.4 collective-permute-start.11
  90.4 0.0 collective-permute-done.8.poth0_ref
  90.4 1.0 collective-permute-done.7.pown_ref
  91.4 0.0 collective-permute-done.9.poth1_ref
  91.4 18.0 %attention.1 = bf16[32,128,128]{2,1,0:T(8,128)(2,1)} custom-call(bf16[8,128,512]{2,1,0:T(8,128)(2,1)S(1)} %all-to-all-done.q_ref, bf16[8,144,256]{2,1,0:T(8,128)(2,1)S(1)} %all-to-all-done.1.own_ref, bf16[8,144,256]{2,1,0:T(8,128)(2,1)S(1)} %collective-permute-done.6.oth_ref, bf16[8,144,256]{2,1,0:T(8,128)(2,1)} %collective-permute-done.7.pown_ref, ...), custom_call_target="tpu_custom_call" | custom-call | flops 16000000000 | bytes 6000000 | tf_op jit(solution)/shard_map/attention/pallas_call | solution.py:233
  109.4 0.0 collective-permute-done.10.refs_4_
  109.4 0.8 copy-done.13
  110.2 0.0 collective-permute-done.11.refs_8_
  110.2 18.1 %all-to-all-start.2 = ((bf16[32,128,128]{2,1,0:T(8,128)(2,1)}), bf16[32,128,128]{2,1,0:T(8,128)(2,1)S(1)}, u32[]{:S(2)}, u32[]{:S(2)}) async-start(bf16[32,128,128]{2,1,0:T(8,128)(2,1)} %attention.1), calls=%async_computation.2 | async-start | bytes 2097152 | tf_op jit(solution)/shard_map/all_to_all | solution.py:255
  128.3 0.8 collective-permute-start.12
  129.1 3.9 %collective-permute-start.15 = (bf16[3,128,1024]{2,1,0:T(8,128)(2,1)}, bf16[3,128,1024]{2,1,0:T(8,128)(2,1)}, u32[]{:S(2)}, u32[]{:S(2)}) collective-permute-start(bf16[3,128,1024]{2,1,0:T(8,128)(2,1)} %collective-permute-done.11.refs_8_), channel_id=1, source_target_pairs={{0,192},{64,0},{128,64},{192,128},{1,193},{65,1},{129,65},{193,129... | collective-permute-start | bytes 2359304 | tf_op jit(solution)/shard_map/ppermute | solution.py:194
  133.1 2.2 %collective-permute-start.13 = (bf16[2,128,1024]{2,1,0:T(8,128)(2,1)S(1)}, bf16[2,128,1024]{2,1,0:T(8,128)(2,1)S(1)}, u32[]{:S(2)}, u32[]{:S(2)}) collective-permute-start(bf16[2,128,1024]{2,1,0:T(8,128)(2,1)S(1)} %get-tuple-element.29.refs_1_), channel_id=1, source_target_pairs={{0,192},{64,0},{128,64},{192,128},{1,193},{65,1},{129,65},{193,129... | collective-permute-start | bytes 1572872 | tf_op jit(solution)/shard_map/ppermute | solution.py:194
  135.3 0.0 collective-permute-start.14
  135.3 28.2 %collective-permute-done.13.refs_7_ = bf16[2,128,1024]{2,1,0:T(8,128)(2,1)S(1)} collective-permute-done((bf16[2,128,1024]{2,1,0:T(8,128)(2,1)S(1)}, bf16[2,128,1024]{2,1,0:T(8,128)(2,1)S(1)}, u32[]{:S(2)}, u32[]{:S(2)}) %collective-permute-start.13) | collective-permute-done | bytes 524320 | tf_op jit(solution)/shard_map/ppermute | solution.py:194
  163.5 0.0 collective-permute-done.12.refs_5_
  163.5 0.0 collective-permute-done.14.refs_10_
  163.5 0.9 copy-done.12
  164.4 0.8 copy-done.16
  165.3 0.0 collective-permute-done.15.refs_11_
  165.3 0.0 copy-start.8
  165.3 1.0 copy-done.8
  166.3 11.0 %projection.1 = (bf16[128,4096]{1,0:T(8,128)(2,1)}, bf16[128,4096]{1,0:T(8,128)(2,1)}, bf16[2,128,4096]{2,1,0:T(8,128)(2,1)}) custom-call(bf16[32,128,128]{2,1,0:T(8,128)(2,1)} %copy-done.8, bf16[3,128,1024]{2,1,0:T(8,128)(2,1)} %pad_maximum_fusion.refs_0_, bf16[2,128,1024]{2,1,0:T(8,128)(2,1)} %copy-done.6, bf16[3,128,1024]{2,1,0:T(8,128)(2,1)} %copy-done.5, ...), custom_call_target="tpu_custom_call" | custom-call | flops 4294967296 | bytes 12582912 | tf_op jit(solution)/shard_map/projection/pallas_call | solution.py:264
  177.2 1.1 collective-permute-start.16
  178.4 4.0 %collective-permute-done.16.arrived_ref = bf16[2,128,4096]{2,1,0:T(8,128)(2,1)S(1)} collective-permute-done((bf16[2,128,4096]{2,1,0:T(8,128)(2,1)}, bf16[2,128,4096]{2,1,0:T(8,128)(2,1)S(1)}, u32[]{:S(2)}, u32[]{:S(2)}) %collective-permute-start.16) | collective-permute-done | bytes 2097184 | tf_op jit(solution)/shard_map/ppermute | solution.py:283
  182.4 1.5 fusion
  183.8 1.5 collective-permute-start.17
  185.3 23.0 %collective-permute-done.17.last_ref = bf16[128,4096]{1,0:T(8,128)(2,1)S(1)} collective-permute-done((bf16[128,4096]{1,0:T(8,128)(2,1)S(1)}, bf16[128,4096]{1,0:T(8,128)(2,1)S(1)}, u32[]{:S(2)}, u32[]{:S(2)}) %collective-permute-start.17) | collective-permute-done | bytes 1048608 | tf_op jit(solution)/shard_map/ppermute | solution.py:284
  208.3 1.3 finish.1
  (25 shorter events, 0.0 us)
Async XLA Ops:
  6.5 79.4 %all-gather.3.cloned.1.call-start = ((), (), s32[]{:S(2)}) async-start(), calls=%async_computation.3 | async-start | bytes 2359296 | tf_op jit(solution)/shard_map/all_gather | solution.py:204
  7.5 4.2 %collective-permute-start = (bf16[128,1024]{1,0:T(8,128)(2,1)S(1)}, bf16[128,1024]{1,0:T(8,128)(2,1)S(1)}, u32[]{:S(2)}, u32[]{:S(2)}) collective-permute-start(bf16[128,1024]{1,0:T(8,128)(2,1)S(1)} %dynamic_slice.3), channel_id=1, source_target_pairs={{0,0},{1,32},{32,1},{33,33},{2,2},{3,34},{34,3},{35,35},{4,4},{5,3... | collective-permute-start | bytes 786440 | tf_op jit(solution)/shard_map/ppermute | solution.py:201
  8.2 1.0 copy-start.2
  9.1 0.9 copy-start.3
  10.1 0.7 copy-start.4
  10.8 13.4 %copy-start.7 = (bf16[128,4096]{1,0:T(8,128)(2,1)S(1)}, bf16[128,4096]{1,0:T(8,128)(2,1)}, u32[]{:S(2)}) copy-start(bf16[128,4096]{1,0:T(8,128)(2,1)} %param.5) | copy-start | bytes 3145732
  11.7 0.7 copy-start.9
  12.4 28.5 %all-to-all-start.1 = ((bf16[8,144,256]{2,1,0:T(8,128)(2,1)}), bf16[8,144,256]{2,1,0:T(8,128)(2,1)S(1)}, u32[]{:S(2)}, u32[]{:S(2)}) async-start(bf16[8,144,256]{2,1,0:T(8,128)(2,1)} %pack_kv.1), calls=%async_computation.1 | async-start | bytes 1179648 | tf_op jit(solution)/shard_map/all_to_all | solution.py:208
  21.5 24.0 %collective-permute-start.2 = (bf16[128,1024]{1,0:T(8,128)(2,1)}, bf16[128,1024]{1,0:T(8,128)(2,1)S(1)}, u32[]{:S(2)}, u32[]{:S(2)}) collective-permute-start(bf16[128,1024]{1,0:T(8,128)(2,1)} %copy-done.9), channel_id=1, source_target_pairs={{0,14},{2,0},{4,2},{6,4},{8,6},{10,8},{12,10},{14,12},{1,15},{3,1}... | collective-permute-start | bytes 786440 | tf_op jit(solution)/shard_map/ppermute | solution.py:194
  24.1 21.9 %collective-permute-start.1 = (bf16[128,1024]{1,0:T(8,128)(2,1)}, bf16[128,1024]{1,0:T(8,128)(2,1)S(1)}, u32[]{:S(2)}, u32[]{:S(2)}) collective-permute-start(bf16[128,1024]{1,0:T(8,128)(2,1)} %copy-done.9), channel_id=1, source_target_pairs={{0,2},{2,4},{4,6},{6,8},{8,10},{10,12},{12,14},{14,0},{1,3},{3,5},... | collective-permute-start | bytes 786440 | tf_op jit(solution)/shard_map/ppermute | solution.py:194
  24.8 21.2 %copy-start.10 = (bf16[128,1024]{1,0:T(8,128)(2,1)S(1)}, bf16[128,1024]{1,0:T(8,128)(2,1)}, u32[]{:S(2)}) copy-start(bf16[128,1024]{1,0:T(8,128)(2,1)} %copy-done.9) | copy-start | bytes 786436
  40.9 45.0 %all-to-all-start = ((bf16[8,128,512]{2,1,0:T(8,128)(2,1)}), bf16[8,128,512]{2,1,0:T(8,128)(2,1)S(1)}, u32[]{:S(2)}, u32[]{:S(2)}) async-start(bf16[8,128,512]{2,1,0:T(8,128)(2,1)} %bitcast.1), calls=%async_computation | async-start | bytes 2097152 | tf_op jit(solution)/shard_map/all_to_all | solution.py:223
  47.0 15.7 %collective-permute-start.3 = (bf16[3,128,1024]{2,1,0:T(8,128)(2,1)}, bf16[3,128,1024]{2,1,0:T(8,128)(2,1)S(1)}, u32[]{:S(2)}, u32[]{:S(2)}) collective-permute-start(bf16[3,128,1024]{2,1,0:T(8,128)(2,1)} %pad_maximum_fusion.refs_0_), channel_id=1, source_target_pairs={{0,64},{64,128},{128,192},{192,0},{1,65},{65,129},{129,193},{193,1... | collective-permute-start | bytes 2359304 | tf_op jit(solution)/shard_map/ppermute | solution.py:194
  48.2 36.4 %collective-permute-start.6 = (bf16[8,144,256]{2,1,0:T(8,128)(2,1)S(1)}, bf16[8,144,256]{2,1,0:T(8,128)(2,1)S(1)}, u32[]{:S(2)}, u32[]{:S(2)}) collective-permute-start(bf16[8,144,256]{2,1,0:T(8,128)(2,1)S(1)} %all-to-all-done.1.own_ref), channel_id=1, source_target_pairs={{0,1},{1,0},{2,3},{3,2},{4,5},{5,4},{6,7},{7,6},{8,9},{9,8},{10,11... | collective-permute-start | bytes 1769480 | tf_op jit(solution)/shard_map/ppermute | solution.py:213
  58.7 27.2 %collective-permute-start.5 = (bf16[3,128,1024]{2,1,0:T(8,128)(2,1)}, bf16[3,128,1024]{2,1,0:T(8,128)(2,1)}, u32[]{:S(2)}, u32[]{:S(2)}) collective-permute-start(bf16[3,128,1024]{2,1,0:T(8,128)(2,1)} %pad_maximum_fusion.refs_0_), channel_id=1, source_target_pairs={{0,192},{64,0},{128,64},{192,128},{1,193},{65,1},{129,65},{193,129... | collective-permute-start | bytes 2359304 | tf_op jit(solution)/shard_map/ppermute | solution.py:194
  62.7 23.3 %copy-start.11 = (bf16[3,128,1024]{2,1,0:T(8,128)(2,1)}, bf16[3,128,1024]{2,1,0:T(8,128)(2,1)S(1)}, u32[]{:S(2)}) copy-start(bf16[3,128,1024]{2,1,0:T(8,128)(2,1)S(1)} %collective-permute-done.3.refs_3_) | copy-start | bytes 2359300
  62.7 23.2 %collective-permute-start.4 = (bf16[3,128,1024]{2,1,0:T(8,128)(2,1)S(1)}, bf16[3,128,1024]{2,1,0:T(8,128)(2,1)}, u32[]{:S(2)}, u32[]{:S(2)}) collective-permute-start(bf16[3,128,1024]{2,1,0:T(8,128)(2,1)S(1)} %collective-permute-done.3.refs_3_), channel_id=1, source_target_pairs={{0,64},{64,128},{128,192},{192,0},{1,65},{65,129},{129,193},{193,1... | collective-permute-start | bytes 2359304 | tf_op jit(solution)/shard_map/ppermute | solution.py:194
  63.1 27.3 %collective-permute-start.8 = (bf16[8,144,256]{2,1,0:T(8,128)(2,1)S(1)}, bf16[8,144,256]{2,1,0:T(8,128)(2,1)}, u32[]{:S(2)}, u32[]{:S(2)}) collective-permute-start(bf16[8,144,256]{2,1,0:T(8,128)(2,1)S(1)} %all-to-all-done.1.own_ref), channel_id=1, source_target_pairs={{16,33},{17,32},{48,65},{49,64},{80,97},{81,96},{112,129},{113,128... | collective-permute-start | bytes 1769480 | tf_op jit(solution)/shard_map/ppermute | solution.py:215
  76.9 14.5 %collective-permute-start.7 = (bf16[8,144,256]{2,1,0:T(8,128)(2,1)S(1)}, bf16[8,144,256]{2,1,0:T(8,128)(2,1)}, u32[]{:S(2)}, u32[]{:S(2)}) collective-permute-start(bf16[8,144,256]{2,1,0:T(8,128)(2,1)S(1)} %all-to-all-done.1.own_ref), channel_id=1, source_target_pairs={{0,16},{16,32},{32,48},{48,64},{64,80},{80,96},{96,112},{112,128},... | collective-permute-start | bytes 1769480 | tf_op jit(solution)/shard_map/ppermute | solution.py:214
  84.6 6.8 %collective-permute-start.9 = (bf16[8,144,256]{2,1,0:T(8,128)(2,1)S(1)}, bf16[8,144,256]{2,1,0:T(8,128)(2,1)}, u32[]{:S(2)}, u32[]{:S(2)}) collective-permute-start(bf16[8,144,256]{2,1,0:T(8,128)(2,1)S(1)} %collective-permute-done.6.oth_ref), channel_id=1, source_target_pairs={{0,16},{1,17},{2,18},{3,19},{4,20},{5,21},{6,22},{7,23},{8,24},{9,... | collective-permute-start | bytes 1769480 | tf_op jit(solution)/shard_map/ppermute | solution.py:220
  86.0 1.6 copy-start
  87.6 40.7 %copy-start.5 = (bf16[3,128,1024]{2,1,0:T(8,128)(2,1)}, bf16[3,128,1024]{2,1,0:T(8,128)(2,1)S(1)}, u32[]{:S(2)}) copy-start(bf16[3,128,1024]{2,1,0:T(8,128)(2,1)S(1)} %get-tuple-element.30.refs_2_) | copy-start | bytes 2359300
  87.7 45.4 %copy-start.6 = (bf16[2,128,1024]{2,1,0:T(8,128)(2,1)}, bf16[2,128,1024]{2,1,0:T(8,128)(2,1)S(1)}, u32[]{:S(2)}) copy-start(bf16[2,128,1024]{2,1,0:T(8,128)(2,1)S(1)} %get-tuple-element.29.refs_1_) | copy-start | bytes 1572868
  87.7 21.8 %collective-permute-start.10 = (bf16[2,128,1024]{2,1,0:T(8,128)(2,1)S(1)}, bf16[2,128,1024]{2,1,0:T(8,128)(2,1)S(1)}, u32[]{:S(2)}, u32[]{:S(2)}) collective-permute-start(bf16[2,128,1024]{2,1,0:T(8,128)(2,1)S(1)} %get-tuple-element.29.refs_1_), channel_id=1, source_target_pairs={{0,64},{64,128},{128,192},{192,0},{1,65},{65,129},{129,193},{193,1... | collective-permute-start | bytes 1572872 | tf_op jit(solution)/shard_map/ppermute | solution.py:194
  89.0 21.3 %collective-permute-start.11 = (bf16[3,128,1024]{2,1,0:T(8,128)(2,1)S(1)}, bf16[3,128,1024]{2,1,0:T(8,128)(2,1)}, u32[]{:S(2)}, u32[]{:S(2)}) collective-permute-start(bf16[3,128,1024]{2,1,0:T(8,128)(2,1)S(1)} %get-tuple-element.30.refs_2_), channel_id=1, source_target_pairs={{0,192},{64,0},{128,64},{192,128},{1,193},{65,1},{129,65},{193,129... | collective-permute-start | bytes 2359304 | tf_op jit(solution)/shard_map/ppermute | solution.py:194
  109.4 0.8 copy-start.13
  110.2 25.1 %copy-start.14 = (bf16[2,128,1024]{2,1,0:T(8,128)(2,1)S(1)}, bf16[2,128,1024]{2,1,0:T(8,128)(2,1)}, u32[]{:S(2)}) copy-start(bf16[2,128,1024]{2,1,0:T(8,128)(2,1)} %copy-done.13) | copy-start | bytes 1572868
  110.2 55.0 %all-to-all-start.2 = ((bf16[32,128,128]{2,1,0:T(8,128)(2,1)}), bf16[32,128,128]{2,1,0:T(8,128)(2,1)S(1)}, u32[]{:S(2)}, u32[]{:S(2)}) async-start(bf16[32,128,128]{2,1,0:T(8,128)(2,1)} %attention.1), calls=%async_computation.2 | async-start | bytes 2097152 | tf_op jit(solution)/shard_map/all_to_all | solution.py:255
  128.3 35.2 %collective-permute-start.12 = (bf16[3,128,1024]{2,1,0:T(8,128)(2,1)S(1)}, bf16[3,128,1024]{2,1,0:T(8,128)(2,1)S(1)}, u32[]{:S(2)}, u32[]{:S(2)}) collective-permute-start(bf16[3,128,1024]{2,1,0:T(8,128)(2,1)S(1)} %get-tuple-element.30.refs_2_), channel_id=1, source_target_pairs={{0,64},{64,128},{128,192},{192,0},{1,65},{65,129},{129,193},{193,1... | collective-permute-start | bytes 2359304 | tf_op jit(solution)/shard_map/ppermute | solution.py:194
  129.1 36.1 %collective-permute-start.15 = (bf16[3,128,1024]{2,1,0:T(8,128)(2,1)}, bf16[3,128,1024]{2,1,0:T(8,128)(2,1)}, u32[]{:S(2)}, u32[]{:S(2)}) collective-permute-start(bf16[3,128,1024]{2,1,0:T(8,128)(2,1)} %collective-permute-done.11.refs_8_), channel_id=1, source_target_pairs={{0,192},{64,0},{128,64},{192,128},{1,193},{65,1},{129,65},{193,129... | collective-permute-start | bytes 2359304 | tf_op jit(solution)/shard_map/ppermute | solution.py:194
  133.1 30.4 %collective-permute-start.13 = (bf16[2,128,1024]{2,1,0:T(8,128)(2,1)S(1)}, bf16[2,128,1024]{2,1,0:T(8,128)(2,1)S(1)}, u32[]{:S(2)}, u32[]{:S(2)}) collective-permute-start(bf16[2,128,1024]{2,1,0:T(8,128)(2,1)S(1)} %get-tuple-element.29.refs_1_), channel_id=1, source_target_pairs={{0,192},{64,0},{128,64},{192,128},{1,193},{65,1},{129,65},{193,129... | collective-permute-start | bytes 1572872 | tf_op jit(solution)/shard_map/ppermute | solution.py:194
  135.3 28.2 %collective-permute-start.14 = (bf16[2,128,1024]{2,1,0:T(8,128)(2,1)S(1)}, bf16[2,128,1024]{2,1,0:T(8,128)(2,1)S(1)}, u32[]{:S(2)}, u32[]{:S(2)}) collective-permute-start(bf16[2,128,1024]{2,1,0:T(8,128)(2,1)S(1)} %copy-done.14), channel_id=1, source_target_pairs={{0,64},{64,128},{128,192},{192,0},{1,65},{65,129},{129,193},{193,1... | collective-permute-start | bytes 1572872 | tf_op jit(solution)/shard_map/ppermute | solution.py:194
  163.5 1.8 copy-start.15
  163.5 0.9 copy-start.12
  164.4 0.8 copy-start.16
  165.3 1.0 copy-start.8
  177.2 31.1 %copy-start.1 = (bf16[128,4096]{1,0:T(8,128)(2,1)S(1)}, bf16[128,4096]{1,0:T(8,128)(2,1)}, u32[]{:S(2)}) copy-start(bf16[128,4096]{1,0:T(8,128)(2,1)} %get-tuple-element.36.keep_ref) | copy-start | bytes 3145732
  177.2 5.1 %collective-permute-start.16 = (bf16[2,128,4096]{2,1,0:T(8,128)(2,1)}, bf16[2,128,4096]{2,1,0:T(8,128)(2,1)S(1)}, u32[]{:S(2)}, u32[]{:S(2)}) collective-permute-start(bf16[2,128,4096]{2,1,0:T(8,128)(2,1)} %get-tuple-element.37), channel_id=1, source_target_pairs={{0,16},{16,0},{1,17},{17,1},{2,18},{18,2},{3,19},{19,3},{4,20},{20... | collective-permute-start | bytes 6291464 | tf_op jit(solution)/shard_map/ppermute | solution.py:283
  183.8 24.5 %collective-permute-start.17 = (bf16[128,4096]{1,0:T(8,128)(2,1)S(1)}, bf16[128,4096]{1,0:T(8,128)(2,1)S(1)}, u32[]{:S(2)}, u32[]{:S(2)}) collective-permute-start(bf16[128,4096]{1,0:T(8,128)(2,1)S(1)} %fusion), channel_id=1, source_target_pairs={{0,32},{32,0},{1,33},{33,1},{2,34},{34,2},{3,35},{35,3},{4,36},{36... | collective-permute-start | bytes 3145736 | tf_op jit(solution)/shard_map/ppermute | solution.py:284
Sparse Core Ops, SparseCore 0:
  12.5 73.2 all-gather.2

commit v10 on v8

--- a/solution.py
+++ b/solution.py
@@ -158,7 +158,7 @@
 
 
 def far_kernel(spread_ref, *refs):
-    projection_kernel(spread_ref, refs[:4], *refs[4:])
+    projection_kernel(spread_ref, refs[:2], *refs[2:])
 
 
 def finish_kernel(*refs):
@@ -236,10 +236,7 @@
     )(query, own, other, prev_own, prev_other_0, prev_other_1)
 
     spread = lax.all_to_all(attn, ("zh", "zl", "core", "yl"), 0, 0, tiled=True)
-    far1 = x_up(before[:1]), x_down(after[4:5])
-    spread, far1 = lax.optimization_barrier((spread, far1))
-    far2 = x_up(before[1:4]), x_down(after[5:])
-    far = far1[0], far2[0], far1[1], far2[1]
+    far = x_up(before[: Z // 2]), x_down(after[Z // 2 :])
     f32 = jnp.float32
     parts = []
     for kernel, weights, blocks in (

time: 203 us -> 192 us (0.946)
  blocking collectives: 0 us -> 38 us
  waiting for transfers between devices: 87.2 us -> 65.7 us
  starting transfers between devices: 65.4 us -> 46.7 us
  local copies, waits for them, and re-layouts: 11.9 us -> 6.36 us
  Pallas kernels: 22.8 us -> 20 us
    all_to_all x0 -> x1, blocking collectives: none -> 38 us  [body(): spread = lax.all_to_all(attn, ('zh', 'zl', 'core', 'yl'), 0, 0, tiled=True)]
    ppermute x6 -> x4, waiting for transfers between devices: 23.7 us -> 4.05 us  [ring(): lax.ppermute(a, axis, [(i, (i + step) % size) for i in range(size)])]
    all_to_all x1 -> x0, starting transfers between devices: 12.8 us -> none  [body(): spread = lax.all_to_all(attn, ('zh', 'zl', 'core', 'yl'), 0, 0, tiled=True)]
    ppermute x1, waiting for transfers between devices: 11.5 us -> 17.5 us  [body(): parts[2] = lax.ppermute(parts[2], 'yl', swap)]
    slice x4 -> x2, local copies, waits for them, and re-layouts: 5.72 us -> 0.14 us  [body(): far = (x_up(before[:Z // 2]), x_down(after[Z // 2:]))]
    ppermute x2, starting transfers between devices: 5.89 us -> 1.69 us  [body(): arrived = lax.ppermute(theirs, 'core', swap)]
    pallas_call x2, Pallas kernels: 8.42 us -> 4.69 us  [body(): pl.pallas_call(kernel, out_shape=[one, one, jax.ShapeDtypeStruct((2, ROWS...]
    ppermute x1, starting transfers between devices: 5.17 us -> 1.61 us  [body(): parts[2] = lax.ppermute(parts[2], 'yl', swap)]
  transfers between devices with their start and end apart: 19 -> 16, of which waited for: 12 -> 7; matrix products, arithmetic and copies ran while one was open for 4% -> 1% of each run, Pallas kernels for 6% -> 7%
where the time goes in v10:
time: 192 us; the launch traced here: 190 us
  waiting for transfers between devices  65.7 us (34%)
  starting transfers between devices  46.7 us (24%)
  blocking collectives  38 us (20%)
  Pallas kernels  20 us (10%)
  between operations  13.5 us (7%)
  local copies, waits for them, and re-layouts  6.36 us (3%)
    all_to_all x1, blocking collectives, body(): spread = lax.all_to_all(attn, ('zh', 'zl', 'core', 'yl'), 0, 0, tiled=True)  38 us
    all_to_all x1, waiting for transfers between devices, body(): query = lax.all_to_all(split, ('zh', 'zl'), 0, 0, tiled=True)  18.5 us
    ppermute x1, waiting for transfers between devices, body(): parts[2] = lax.ppermute(parts[2], 'yl', swap)  17.5 us
    all_to_all x1, waiting for transfers between devices, body(): own = lax.all_to_all(packed, ('zh', 'zl'), 0, 0, tiled=True)  16.6 us
    pallas_call x1, Pallas kernels, body(): pl.pallas_call(attention_kernel, out_shape=jax.ShapeDtypeStruct((4 * Z, R...  13 us
    ppermute x4, starting transfers between devices, ring(): lax.ppermute(a, axis, [(i, (i + step) % size) for i in range(size)])  9.65 us
    ppermute x1, starting transfers between devices, body(): other = lax.ppermute(own, 'yh', swap)  9.2 us
    all_to_all x1, starting transfers between devices, body(): own = lax.all_to_all(packed, ('zh', 'zl'), 0, 0, tiled=True)  9.04 us
  transfers between devices with their start and end apart: 16, of which 7 were waited for; matrix products, arithmetic and copies ran while one was open for 1% of the time, Pallas kernels for 7%

profile of v10, /device:TPU:1, one launch (start us, length us, event | category | flops | bytes accessed | tf_op | source)
XLA Modules:
  0.0 190.5 jit_solution(15272824826497869259)
XLA Ops:
  6.5 0.0 all-gather.3.cloned.1.call-start
  6.5 1.0 dynamic_slice.3
  7.5 0.7 collective-permute-start
  8.2 0.0 copy-start
  8.2 0.9 copy-done
  9.1 0.0 copy-start.1
  9.1 0.9 copy-done.1
  10.1 0.0 copy-start.2
  10.1 0.7 copy-done.2
  10.8 0.0 copy-start.4
  10.8 0.9 pack_kv.1
  11.7 0.0 collective-permute-done
  11.7 0.0 copy-start.5
  11.7 0.7 copy-done.5
  12.4 0.0 all-gather.3.cloned.1.call-update
  12.4 9.0 %all-to-all-start.1 = ((bf16[8,144,256]{2,1,0:T(8,128)(2,1)}), bf16[8,144,256]{2,1,0:T(8,128)(2,1)S(1)}, u32[]{:S(2)}, u32[]{:S(2)}) async-start(bf16[8,144,256]{2,1,0:T(8,128)(2,1)} %pack_kv.1), calls=%async_computation.1 | async-start | bytes 1179648 | tf_op jit(solution)/shard_map/all_to_all | solution.py:202
  21.5 0.0 copy-done.4
  21.5 0.7 copy.6
  22.2 1.3 copy.7
  23.5 16.6 %all-to-all-done.1.own_ref = bf16[8,144,256]{2,1,0:T(8,128)(2,1)S(1)} async-done(((bf16[8,144,256]{2,1,0:T(8,128)(2,1)}), bf16[8,144,256]{2,1,0:T(8,128)(2,1)S(1)}, u32[]{:S(2)}, u32[]{:S(2)}) %all-to-all-start.1) | async-done | bytes 589856 | tf_op jit(solution)/shard_map/all_to_all | solution.py:202
  40.0 3.6 %all-to-all-start = ((bf16[8,128,512]{2,1,0:T(8,128)(2,1)}), bf16[8,128,512]{2,1,0:T(8,128)(2,1)S(1)}, u32[]{:S(2)}, u32[]{:S(2)}) async-start(bf16[8,128,512]{2,1,0:T(8,128)(2,1)} %bitcast.1), calls=%async_computation | async-start | bytes 2097152 | tf_op jit(solution)/shard_map/all_to_all | solution.py:214
  43.6 9.2 %collective-permute-start.1 = (bf16[8,144,256]{2,1,0:T(8,128)(2,1)S(1)}, bf16[8,144,256]{2,1,0:T(8,128)(2,1)S(1)}, u32[]{:S(2)}, u32[]{:S(2)}) collective-permute-start(bf16[8,144,256]{2,1,0:T(8,128)(2,1)S(1)} %all-to-all-done.1.own_ref), channel_id=1, source_target_pairs={{0,1},{1,0},{2,3},{3,2},{4,5},{5,4},{6,7},{7,6},{8,9},{9,8},{10,11... | collective-permute-start | bytes 1769480 | tf_op jit(solution)/shard_map/ppermute | solution.py:204
  52.8 4.0 %collective-permute-start.2 = (bf16[8,144,256]{2,1,0:T(8,128)(2,1)S(1)}, bf16[8,144,256]{2,1,0:T(8,128)(2,1)S(1)}, u32[]{:S(2)}, u32[]{:S(2)}) collective-permute-start(bf16[8,144,256]{2,1,0:T(8,128)(2,1)S(1)} %all-to-all-done.1.own_ref), channel_id=1, source_target_pairs={{0,16},{16,32},{32,48},{48,64},{64,80},{80,96},{96,112},{112,128},... | collective-permute-start | bytes 1769480 | tf_op jit(solution)/shard_map/ppermute | solution.py:205
  56.8 4.6 %collective-permute-start.3 = (bf16[8,144,256]{2,1,0:T(8,128)(2,1)S(1)}, bf16[8,144,256]{2,1,0:T(8,128)(2,1)S(1)}, u32[]{:S(2)}, u32[]{:S(2)}) collective-permute-start(bf16[8,144,256]{2,1,0:T(8,128)(2,1)S(1)} %all-to-all-done.1.own_ref), channel_id=1, source_target_pairs={{16,33},{17,32},{48,65},{49,64},{80,97},{81,96},{112,129},{113,128... | collective-permute-start | bytes 1769480 | tf_op jit(solution)/shard_map/ppermute | solution.py:206
  61.4 1.3 collective-permute-done.1.oth_ref
  62.7 1.3 collective-permute-start.4
  64.0 18.5 %all-to-all-done.q_ref = bf16[8,128,512]{2,1,0:T(8,128)(2,1)S(1)} async-done(((bf16[8,128,512]{2,1,0:T(8,128)(2,1)}), bf16[8,128,512]{2,1,0:T(8,128)(2,1)S(1)}, u32[]{:S(2)}, u32[]{:S(2)}) %all-to-all-start) | async-done | bytes 1048608 | tf_op jit(solution)/shard_map/all_to_all | solution.py:214
  82.5 0.0 all-gather.3.cloned.1.call-done
  82.5 1.2 collective-permute-start.5
  83.7 1.4 collective-permute-start.6
  85.1 0.0 collective-permute-done.2.pown_ref
  85.1 0.0 collective-permute-done.3.poth0_ref
  85.1 0.0 collective-permute-done.4.poth1_ref
  85.2 13.0 %attention.1 = bf16[32,128,128]{2,1,0:T(8,128)(2,1)S(1)} custom-call(bf16[8,128,512]{2,1,0:T(8,128)(2,1)S(1)} %all-to-all-done.q_ref, bf16[8,144,256]{2,1,0:T(8,128)(2,1)S(1)} %all-to-all-done.1.own_ref, bf16[8,144,256]{2,1,0:T(8,128)(2,1)S(1)} %collective-permute-done.1.oth_ref, bf16[8,144,256]{2,1,0:T(8,128)(2,1)S(1)} %collective-permute-done.2.pown_ref, ...), custom_call_target="tpu_custom_call" | custom-call | flops 16000000000 | bytes 6000000 | tf_op jit(solution)/shard_map/attention/pallas_call | solution.py:217
  98.2 0.0 copy-start.3
  98.2 38.0 %all_to_all.15.spread_ref = bf16[32,128,128]{2,1,0:T(8,128)(2,1)S(1)} all-to-all(bf16[32,128,128]{2,1,0:T(8,128)(2,1)S(1)} %attention.1), channel_id=1, replica_groups=mesh['x'=4,'yl'=2,'core'=2,'zh'=4,'zl'=2,'yh'=2] {'zh','zl','core','yl'}, dimensions={0} | all-to-all | bytes 2097152 | tf_op jit(solution)/shard_map/all_to_all | solution.py:238
  136.2 0.0 collective-permute-done.5.refs_1_
  136.2 0.0 collective-permute-done.6.refs_2_
  136.2 0.0 copy-done.3
  136.2 3.4 %projection.2 = (bf16[128,3072]{1,0:T(8,128)(2,1)S(1)}, bf16[128,3072]{1,0:T(8,128)(2,1)S(1)}, bf16[2,128,3072]{2,1,0:T(8,128)(2,1)S(1)}) custom-call(bf16[32,128,128]{2,1,0:T(8,128)(2,1)S(1)} %all_to_all.15.spread_ref, bf16[8,128,1024]{2,1,0:T(8,128)(2,1)S(1)} %bitcast.17, bf16[8,128,1024]{2,1,0:T(8,128)(2,1)S(1)} %collective-permute-done.5.refs_1_, ...), custom_call_target="tpu_custom_call" | custom-call | flops 3221225472 | bytes 9437184 | tf_op jit(solution)/shard_map/projection/pallas_call | solution.py:251
  139.6 1.0 collective-permute-start.7
  140.6 0.1 slice.18
  140.7 2.6 %collective-permute-start.10 = (bf16[4,128,1024]{2,1,0:T(8,128)(2,1)S(1)}, bf16[4,128,1024]{2,1,0:T(8,128)(2,1)S(1)}, u32[]{:S(2)}, u32[]{:S(2)}) collective-permute-start(bf16[4,128,1024]{2,1,0:T(8,128)(2,1)S(1)} %slice.18), channel_id=1, source_target_pairs={{0,192},{64,0},{128,64},{192,128},{1,193},{65,1},{129,65},{193,129... | collective-permute-start | bytes 3145736 | tf_op jit(solution)/shard_map/ppermute | solution.py:193
  143.3 0.1 slice.17
  143.4 4.3 %collective-permute-start.9 = (bf16[4,128,1024]{2,1,0:T(8,128)(2,1)S(1)}, bf16[4,128,1024]{2,1,0:T(8,128)(2,1)S(1)}, u32[]{:S(2)}, u32[]{:S(2)}) collective-permute-start(bf16[4,128,1024]{2,1,0:T(8,128)(2,1)S(1)} %slice.17), channel_id=1, source_target_pairs={{0,64},{64,128},{128,192},{192,0},{1,65},{65,129},{129,193},{193,1... | collective-permute-start | bytes 3145736 | tf_op jit(solution)/shard_map/ppermute | solution.py:193
  147.7 0.0 collective-permute-done.7.refs_1_
  147.8 0.2 fusion
  147.9 1.6 collective-permute-start.8
  149.6 17.5 %collective-permute-done.8.refs_2_ = bf16[128,3072]{1,0:T(8,128)(2,1)S(1)} collective-permute-done((bf16[128,3072]{1,0:T(8,128)(2,1)S(1)}, bf16[128,3072]{1,0:T(8,128)(2,1)S(1)}, u32[]{:S(2)}, u32[]{:S(2)}) %collective-permute-start.8) | collective-permute-done | bytes 786464 | tf_op jit(solution)/shard_map/ppermute | solution.py:248
  167.1 4.0 %collective-permute-done.10.refs_1_ = bf16[4,128,1024]{2,1,0:T(8,128)(2,1)S(1)} collective-permute-done((bf16[4,128,1024]{2,1,0:T(8,128)(2,1)S(1)}, bf16[4,128,1024]{2,1,0:T(8,128)(2,1)S(1)}, u32[]{:S(2)}, u32[]{:S(2)}) %collective-permute-start.10) | collective-permute-done | bytes 1048608 | tf_op jit(solution)/shard_map/ppermute | solution.py:193
  171.1 0.0 collective-permute-done.9.refs_0_
  171.1 1.3 projection.3
  172.4 0.7 collective-permute-start.11
  173.1 1.5 collective-permute-done.11.refs_4_
  174.6 0.1 fusion.1
  174.7 1.4 collective-permute-start.12
  176.1 6.2 %collective-permute-done.12.refs_5_ = bf16[128,1024]{1,0:T(8,128)(2,1)S(1)} collective-permute-done((bf16[128,1024]{1,0:T(8,128)(2,1)S(1)}, bf16[128,1024]{1,0:T(8,128)(2,1)S(1)}, u32[]{:S(2)}, u32[]{:S(2)}) %collective-permute-start.12) | collective-permute-done | bytes 262176 | tf_op jit(solution)/shard_map/ppermute | solution.py:265
  182.3 1.3 finish.1
Async XLA Ops:
  6.5 75.9 %all-gather.3.cloned.1.call-start = ((), (), s32[]{:S(2)}) async-start(), calls=%async_computation.3 | async-start | bytes 2359296 | tf_op jit(solution)/shard_map/all_gather | solution.py:203
  7.5 4.2 %collective-permute-start = (bf16[128,1024]{1,0:T(8,128)(2,1)S(1)}, bf16[128,1024]{1,0:T(8,128)(2,1)S(1)}, u32[]{:S(2)}, u32[]{:S(2)}) collective-permute-start(bf16[128,1024]{1,0:T(8,128)(2,1)S(1)} %dynamic_slice.3), channel_id=1, source_target_pairs={{0,0},{1,32},{32,1},{33,33},{2,2},{3,34},{34,3},{35,35},{4,4},{5,3... | collective-permute-start | bytes 786440 | tf_op jit(solution)/shard_map/ppermute | solution.py:200
  8.2 1.0 copy-start
  9.1 0.9 copy-start.1
  10.1 0.7 copy-start.2
  10.8 10.7 %copy-start.4 = (bf16[128,4096]{1,0:T(8,128)(2,1)S(1)}, bf16[128,4096]{1,0:T(8,128)(2,1)}, u32[]{:S(2)}) copy-start(bf16[128,4096]{1,0:T(8,128)(2,1)} %param.5) | copy-start | bytes 3145732
  11.7 0.7 copy-start.5
  12.4 27.6 %all-to-all-start.1 = ((bf16[8,144,256]{2,1,0:T(8,128)(2,1)}), bf16[8,144,256]{2,1,0:T(8,128)(2,1)S(1)}, u32[]{:S(2)}, u32[]{:S(2)}) async-start(bf16[8,144,256]{2,1,0:T(8,128)(2,1)} %pack_kv.1), calls=%async_computation.1 | async-start | bytes 1179648 | tf_op jit(solution)/shard_map/all_to_all | solution.py:202
  40.0 42.4 %all-to-all-start = ((bf16[8,128,512]{2,1,0:T(8,128)(2,1)}), bf16[8,128,512]{2,1,0:T(8,128)(2,1)S(1)}, u32[]{:S(2)}, u32[]{:S(2)}) async-start(bf16[8,128,512]{2,1,0:T(8,128)(2,1)} %bitcast.1), calls=%async_computation | async-start | bytes 2097152 | tf_op jit(solution)/shard_map/all_to_all | solution.py:214
  43.6 19.0 %collective-permute-start.1 = (bf16[8,144,256]{2,1,0:T(8,128)(2,1)S(1)}, bf16[8,144,256]{2,1,0:T(8,128)(2,1)S(1)}, u32[]{:S(2)}, u32[]{:S(2)}) collective-permute-start(bf16[8,144,256]{2,1,0:T(8,128)(2,1)S(1)} %all-to-all-done.1.own_ref), channel_id=1, source_target_pairs={{0,1},{1,0},{2,3},{3,2},{4,5},{5,4},{6,7},{7,6},{8,9},{9,8},{10,11... | collective-permute-start | bytes 1769480 | tf_op jit(solution)/shard_map/ppermute | solution.py:204
  52.8 32.3 %collective-permute-start.2 = (bf16[8,144,256]{2,1,0:T(8,128)(2,1)S(1)}, bf16[8,144,256]{2,1,0:T(8,128)(2,1)S(1)}, u32[]{:S(2)}, u32[]{:S(2)}) collective-permute-start(bf16[8,144,256]{2,1,0:T(8,128)(2,1)S(1)} %all-to-all-done.1.own_ref), channel_id=1, source_target_pairs={{0,16},{16,32},{32,48},{48,64},{64,80},{80,96},{96,112},{112,128},... | collective-permute-start | bytes 1769480 | tf_op jit(solution)/shard_map/ppermute | solution.py:205
  56.8 28.4 %collective-permute-start.3 = (bf16[8,144,256]{2,1,0:T(8,128)(2,1)S(1)}, bf16[8,144,256]{2,1,0:T(8,128)(2,1)S(1)}, u32[]{:S(2)}, u32[]{:S(2)}) collective-permute-start(bf16[8,144,256]{2,1,0:T(8,128)(2,1)S(1)} %all-to-all-done.1.own_ref), channel_id=1, source_target_pairs={{16,33},{17,32},{48,65},{49,64},{80,97},{81,96},{112,129},{113,128... | collective-permute-start | bytes 1769480 | tf_op jit(solution)/shard_map/ppermute | solution.py:206
  62.7 22.5 %collective-permute-start.4 = (bf16[8,144,256]{2,1,0:T(8,128)(2,1)S(1)}, bf16[8,144,256]{2,1,0:T(8,128)(2,1)}, u32[]{:S(2)}, u32[]{:S(2)}) collective-permute-start(bf16[8,144,256]{2,1,0:T(8,128)(2,1)S(1)} %collective-permute-done.1.oth_ref), channel_id=1, source_target_pairs={{0,16},{1,17},{2,18},{3,19},{4,20},{5,21},{6,22},{7,23},{8,24},{9,... | collective-permute-start | bytes 1769480 | tf_op jit(solution)/shard_map/ppermute | solution.py:211
  82.5 53.7 %collective-permute-start.5 = (bf16[8,128,1024]{2,1,0:T(8,128)(2,1)}, bf16[8,128,1024]{2,1,0:T(8,128)(2,1)S(1)}, u32[]{:S(2)}, u32[]{:S(2)}) collective-permute-start(bf16[8,128,1024]{2,1,0:T(8,128)(2,1)} %bitcast.15), channel_id=1, source_target_pairs={{0,64},{64,128},{128,192},{192,0},{1,65},{65,129},{129,193},{193,1... | collective-permute-start | bytes 6291464 | tf_op jit(solution)/shard_map/ppermute | solution.py:193
  83.7 52.5 %collective-permute-start.6 = (bf16[8,128,1024]{2,1,0:T(8,128)(2,1)}, bf16[8,128,1024]{2,1,0:T(8,128)(2,1)S(1)}, u32[]{:S(2)}, u32[]{:S(2)}) collective-permute-start(bf16[8,128,1024]{2,1,0:T(8,128)(2,1)} %bitcast.16), channel_id=1, source_target_pairs={{0,192},{64,0},{128,64},{192,128},{1,193},{65,1},{129,65},{193,129... | collective-permute-start | bytes 6291464 | tf_op jit(solution)/shard_map/ppermute | solution.py:193
  98.2 38.0 %copy-start.3 = (bf16[1024,1024]{1,0:T(8,128)(2,1)S(1)}, bf16[1024,1024]{1,0:T(8,128)(2,1)}, u32[]{:S(2)}) copy-start(bf16[1024,1024]{1,0:T(8,128)(2,1)} %all-gather.3.cloned.1.call-done) | copy-start | bytes 6291460
  139.6 8.1 %collective-permute-start.7 = (bf16[2,128,3072]{2,1,0:T(8,128)(2,1)S(1)}, bf16[2,128,3072]{2,1,0:T(8,128)(2,1)S(1)}, u32[]{:S(2)}, u32[]{:S(2)}) collective-permute-start(bf16[2,128,3072]{2,1,0:T(8,128)(2,1)S(1)} %get-tuple-element.22), channel_id=1, source_target_pairs={{0,16},{16,0},{1,17},{17,1},{2,18},{18,2},{3,19},{19,3},{4,20},{20... | collective-permute-start | bytes 4718600 | tf_op jit(solution)/shard_map/ppermute | solution.py:263
  140.7 30.4 %collective-permute-start.10 = (bf16[4,128,1024]{2,1,0:T(8,128)(2,1)S(1)}, bf16[4,128,1024]{2,1,0:T(8,128)(2,1)S(1)}, u32[]{:S(2)}, u32[]{:S(2)}) collective-permute-start(bf16[4,128,1024]{2,1,0:T(8,128)(2,1)S(1)} %slice.18), channel_id=1, source_target_pairs={{0,192},{64,0},{128,64},{192,128},{1,193},{65,1},{129,65},{193,129... | collective-permute-start | bytes 3145736 | tf_op jit(solution)/shard_map/ppermute | solution.py:193
  143.4 27.7 %collective-permute-start.9 = (bf16[4,128,1024]{2,1,0:T(8,128)(2,1)S(1)}, bf16[4,128,1024]{2,1,0:T(8,128)(2,1)S(1)}, u32[]{:S(2)}, u32[]{:S(2)}) collective-permute-start(bf16[4,128,1024]{2,1,0:T(8,128)(2,1)S(1)} %slice.17), channel_id=1, source_target_pairs={{0,64},{64,128},{128,192},{192,0},{1,65},{65,129},{129,193},{193,1... | collective-permute-start | bytes 3145736 | tf_op jit(solution)/shard_map/ppermute | solution.py:193
  147.9 19.1 %collective-permute-start.8 = (bf16[128,3072]{1,0:T(8,128)(2,1)S(1)}, bf16[128,3072]{1,0:T(8,128)(2,1)S(1)}, u32[]{:S(2)}, u32[]{:S(2)}) collective-permute-start(bf16[128,3072]{1,0:T(8,128)(2,1)S(1)} %fusion), channel_id=1, source_target_pairs={{0,32},{32,0},{1,33},{33,1},{2,34},{34,2},{3,35},{35,3},{4,36},{36... | collective-permute-start | bytes 2359304 | tf_op jit(solution)/shard_map/ppermute | solution.py:248
  172.4 2.2 %collective-permute-start.11 = (bf16[2,128,1024]{2,1,0:T(8,128)(2,1)S(1)}, bf16[2,128,1024]{2,1,0:T(8,128)(2,1)S(1)}, u32[]{:S(2)}, u32[]{:S(2)}) collective-permute-start(bf16[2,128,1024]{2,1,0:T(8,128)(2,1)S(1)} %get-tuple-element.27), channel_id=1, source_target_pairs={{0,16},{16,0},{1,17},{17,1},{2,18},{18,2},{3,19},{19,3},{4,20},{20... | collective-permute-start | bytes 1572872 | tf_op jit(solution)/shard_map/ppermute | solution.py:263
  174.7 7.6 %collective-permute-start.12 = (bf16[128,1024]{1,0:T(8,128)(2,1)S(1)}, bf16[128,1024]{1,0:T(8,128)(2,1)S(1)}, u32[]{:S(2)}, u32[]{:S(2)}) collective-permute-start(bf16[128,1024]{1,0:T(8,128)(2,1)S(1)} %fusion.1), channel_id=1, source_target_pairs={{0,32},{32,0},{1,33},{33,1},{2,34},{34,2},{3,35},{35,3},{4,36},{36... | collective-permute-start | bytes 786440 | tf_op jit(solution)/shard_map/ppermute | solution.py:265
Sparse Core Ops, SparseCore 0:
  12.6 68.9 all-gather.2

commit v11 on v10

--- a/solution.py
+++ b/solution.py
@@ -186,7 +186,7 @@
     packed = pl.pallas_call(
         pack_kernel,
         out_shape=jax.ShapeDtypeStruct((Z, ROWS + 16, 2 * HEAD_DIM), bf16),
-        compiler_params=params(8),
+        compiler_params=params(56),
         name="pack_kv",
     )(keys, values, doc_ids.reshape(1, ROWS))
     def ring(axis, size, step):

time: 192 us -> 194 us (1.010)
  waiting for transfers between devices: 65.7 us -> 68.6 us
  local copies, waits for them, and re-layouts: 6.36 us -> 3.91 us
  blocking collectives: 38 us -> 40.1 us
    unnamed x13 -> x7, local copies, waits for them, and re-layouts: 3.94 us -> 1.41 us
    ppermute x4, waiting for transfers between devices: 4.05 us -> 6.35 us  [ring(): lax.ppermute(a, axis, [(i, (i + step) % size) for i in range(size)])]
    all_to_all x1, blocking collectives: 38 us -> 40.1 us  [body(): spread = lax.all_to_all(attn, ('zh', 'zl', 'core', 'yl'), 0, 0, tiled=True)]
  transfers between devices with their start and end apart: 16 -> 16, of which waited for: 7 -> 8; matrix products, arithmetic and copies ran while one was open for 1% -> 1% of each run, Pallas kernels for 7% -> 7%
where the time goes in v11:
time: 194 us
  waiting for transfers between devices  68.6 us (35%)
  starting transfers between devices  48 us (25%)
  blocking collectives  40.1 us (21%)
  Pallas kernels  19.7 us (10%)
  between operations  13.5 us (7%)
  local copies, waits for them, and re-layouts  3.91 us (2%)
    all_to_all x1, blocking collectives, body(): spread = lax.all_to_all(attn, ('zh', 'zl', 'core', 'yl'), 0, 0, tiled=True)  40.1 us
    all_to_all x1, waiting for transfers between devices, body(): query = lax.all_to_all(split, ('zh', 'zl'), 0, 0, tiled=True)  18.3 us
    ppermute x1, waiting for transfers between devices, body(): parts[2] = lax.ppermute(parts[2], 'yl', swap)  17.5 us
    all_to_all x1, waiting for transfers between devices, body(): own = lax.all_to_all(packed, ('zh', 'zl'), 0, 0, tiled=True)  17.4 us
    pallas_call x1, Pallas kernels, body(): pl.pallas_call(attention_kernel, out_shape=jax.ShapeDtypeStruct((4 * Z, R...  11.8 us
    ppermute x1, starting transfers between devices, body(): other = lax.ppermute(own, 'yh', swap)  9.95 us
    ppermute x4, starting transfers between devices, ring(): lax.ppermute(a, axis, [(i, (i + step) % size) for i in range(size)])  9.68 us
    all_to_all x1, starting transfers between devices, body(): own = lax.all_to_all(packed, ('zh', 'zl'), 0, 0, tiled=True)  9.04 us
  transfers between devices with their start and end apart: 16, of which 8 were waited for; matrix products, arithmetic and copies ran while one was open for 1% of the time, Pallas kernels for 7%

profile of v11, /device:TPU:1, one launch (start us, length us, event | category | flops | bytes accessed | tf_op | source)
XLA Modules:
  0.0 194.0 jit_solution(518786850932311966)
XLA Ops:
  6.5 0.0 copy-start.1
  6.5 0.0 all-gather.3.cloned.1.call-start
  6.5 1.1 dynamic_slice.3
  7.6 0.7 collective-permute-start
  8.3 2.0 %pack_kv.1 = bf16[8,144,256]{2,1,0:T(8,128)(2,1)} custom-call(bf16[128,1024]{1,0:T(8,128)(2,1)} %k_ref.1, bf16[128,1024]{1,0:T(8,128)(2,1)} %v_ref.1, s32[1,128]{1,0:T(1,128)} %bitcast.18), custom_call_target="tpu_custom_call" | custom-call | tf_op jit(solution)/shard_map/pack_kv/pallas_call | solution.py:186
  10.2 0.0 collective-permute-done
  10.2 0.0 copy-start.2
  10.2 0.7 copy-done.2
  11.0 0.0 all-gather.3.cloned.1.call-update
  11.0 9.0 %all-to-all-start.1 = ((bf16[8,144,256]{2,1,0:T(8,128)(2,1)}), bf16[8,144,256]{2,1,0:T(8,128)(2,1)S(1)}, u32[]{:S(2)}, u32[]{:S(2)}) async-start(bf16[8,144,256]{2,1,0:T(8,128)(2,1)} %pack_kv.1), calls=%async_computation.1 | async-start | bytes 1179648 | tf_op jit(solution)/shard_map/all_to_all | solution.py:202
  20.0 0.0 copy-done.1
  20.1 0.7 copy.6
  20.7 1.3 copy.7
  22.0 17.4 %all-to-all-done.1.own_ref = bf16[8,144,256]{2,1,0:T(8,128)(2,1)S(1)} async-done(((bf16[8,144,256]{2,1,0:T(8,128)(2,1)}), bf16[8,144,256]{2,1,0:T(8,128)(2,1)S(1)}, u32[]{:S(2)}, u32[]{:S(2)}) %all-to-all-start.1) | async-done | bytes 589856 | tf_op jit(solution)/shard_map/all_to_all | solution.py:202
  39.4 3.6 %all-to-all-start = ((bf16[8,128,512]{2,1,0:T(8,128)(2,1)}), bf16[8,128,512]{2,1,0:T(8,128)(2,1)S(1)}, u32[]{:S(2)}, u32[]{:S(2)}) async-start(bf16[8,128,512]{2,1,0:T(8,128)(2,1)} %bitcast.1), calls=%async_computation | async-start | bytes 2097152 | tf_op jit(solution)/shard_map/all_to_all | solution.py:214
  43.0 9.9 %collective-permute-start.1 = (bf16[8,144,256]{2,1,0:T(8,128)(2,1)S(1)}, bf16[8,144,256]{2,1,0:T(8,128)(2,1)S(1)}, u32[]{:S(2)}, u32[]{:S(2)}) collective-permute-start(bf16[8,144,256]{2,1,0:T(8,128)(2,1)S(1)} %all-to-all-done.1.own_ref), channel_id=1, source_target_pairs={{0,1},{1,0},{2,3},{3,2},{4,5},{5,4},{6,7},{7,6},{8,9},{9,8},{10,11... | collective-permute-start | bytes 1769480 | tf_op jit(solution)/shard_map/ppermute | solution.py:204
  52.9 4.0 %collective-permute-start.2 = (bf16[8,144,256]{2,1,0:T(8,128)(2,1)S(1)}, bf16[8,144,256]{2,1,0:T(8,128)(2,1)S(1)}, u32[]{:S(2)}, u32[]{:S(2)}) collective-permute-start(bf16[8,144,256]{2,1,0:T(8,128)(2,1)S(1)} %all-to-all-done.1.own_ref), channel_id=1, source_target_pairs={{0,16},{16,32},{32,48},{48,64},{64,80},{80,96},{96,112},{112,128},... | collective-permute-start | bytes 1769480 | tf_op jit(solution)/shard_map/ppermute | solution.py:205
  56.9 4.6 %collective-permute-start.3 = (bf16[8,144,256]{2,1,0:T(8,128)(2,1)S(1)}, bf16[8,144,256]{2,1,0:T(8,128)(2,1)S(1)}, u32[]{:S(2)}, u32[]{:S(2)}) collective-permute-start(bf16[8,144,256]{2,1,0:T(8,128)(2,1)S(1)} %all-to-all-done.1.own_ref), channel_id=1, source_target_pairs={{16,33},{17,32},{48,65},{49,64},{80,97},{81,96},{112,129},{113,128... | collective-permute-start | bytes 1769480 | tf_op jit(solution)/shard_map/ppermute | solution.py:206
  61.5 1.3 collective-permute-done.1.oth_ref
  62.8 1.3 collective-permute-start.4
  64.1 18.3 %all-to-all-done.q_ref = bf16[8,128,512]{2,1,0:T(8,128)(2,1)S(1)} async-done(((bf16[8,128,512]{2,1,0:T(8,128)(2,1)}), bf16[8,128,512]{2,1,0:T(8,128)(2,1)S(1)}, u32[]{:S(2)}, u32[]{:S(2)}) %all-to-all-start) | async-done | bytes 1048608 | tf_op jit(solution)/shard_map/all_to_all | solution.py:214
  82.4 0.0 all-gather.3.cloned.1.call-done
  82.4 1.2 collective-permute-start.5
  83.5 1.5 collective-permute-start.6
  85.1 0.0 collective-permute-done.2.pown_ref
  85.1 0.0 collective-permute-done.3.poth0_ref
  85.1 0.0 collective-permute-done.4.poth1_ref
  85.1 11.8 %attention.1 = bf16[32,128,128]{2,1,0:T(8,128)(2,1)S(1)} custom-call(bf16[8,128,512]{2,1,0:T(8,128)(2,1)S(1)} %all-to-all-done.q_ref, bf16[8,144,256]{2,1,0:T(8,128)(2,1)S(1)} %all-to-all-done.1.own_ref, bf16[8,144,256]{2,1,0:T(8,128)(2,1)S(1)} %collective-permute-done.1.oth_ref, bf16[8,144,256]{2,1,0:T(8,128)(2,1)S(1)} %collective-permute-done.2.pown_ref, ...), custom_call_target="tpu_custom_call" | custom-call | flops 16000000000 | bytes 6000000 | tf_op jit(solution)/shard_map/attention/pallas_call | solution.py:217
  96.8 0.0 copy-start
  96.9 40.1 %all_to_all.15.spread_ref = bf16[32,128,128]{2,1,0:T(8,128)(2,1)S(1)} all-to-all(bf16[32,128,128]{2,1,0:T(8,128)(2,1)S(1)} %attention.1), channel_id=1, replica_groups=mesh['x'=4,'yl'=2,'core'=2,'zh'=4,'zl'=2,'yh'=2] {'zh','zl','core','yl'}, dimensions={0} | all-to-all | bytes 2097152 | tf_op jit(solution)/shard_map/all_to_all | solution.py:238
  136.9 0.0 collective-permute-done.5.refs_1_
  136.9 0.0 collective-permute-done.6.refs_2_
  136.9 0.0 copy-done
  136.9 3.4 %projection.2 = (bf16[128,3072]{1,0:T(8,128)(2,1)S(1)}, bf16[128,3072]{1,0:T(8,128)(2,1)S(1)}, bf16[2,128,3072]{2,1,0:T(8,128)(2,1)S(1)}) custom-call(bf16[32,128,128]{2,1,0:T(8,128)(2,1)S(1)} %all_to_all.15.spread_ref, bf16[8,128,1024]{2,1,0:T(8,128)(2,1)S(1)} %bitcast.16, bf16[8,128,1024]{2,1,0:T(8,128)(2,1)S(1)} %collective-permute-done.5.refs_1_, ...), custom_call_target="tpu_custom_call" | custom-call | flops 3221225472 | bytes 9437184 | tf_op jit(solution)/shard_map/projection/pallas_call | solution.py:251
  140.4 1.0 collective-permute-start.7
  141.4 0.1 slice.18
  141.4 6.9 %collective-permute-start.10 = (bf16[4,128,1024]{2,1,0:T(8,128)(2,1)S(1)}, bf16[4,128,1024]{2,1,0:T(8,128)(2,1)S(1)}, u32[]{:S(2)}, u32[]{:S(2)}) collective-permute-start(bf16[4,128,1024]{2,1,0:T(8,128)(2,1)S(1)} %slice.18), channel_id=1, source_target_pairs={{0,192},{64,0},{128,64},{192,128},{1,193},{65,1},{129,65},{193,129... | collective-permute-start | bytes 3145736 | tf_op jit(solution)/shard_map/ppermute | solution.py:193
  148.4 0.1 slice.17
  148.4 0.1 collective-permute-start.9
  148.5 0.0 collective-permute-done.7.refs_1_
  148.5 0.2 fusion
  148.7 1.6 collective-permute-start.8
  150.3 17.5 %collective-permute-done.8.refs_2_ = bf16[128,3072]{1,0:T(8,128)(2,1)S(1)} collective-permute-done((bf16[128,3072]{1,0:T(8,128)(2,1)S(1)}, bf16[128,3072]{1,0:T(8,128)(2,1)S(1)}, u32[]{:S(2)}, u32[]{:S(2)}) %collective-permute-start.8) | collective-permute-done | bytes 786464 | tf_op jit(solution)/shard_map/ppermute | solution.py:248
  167.8 3.1 %collective-permute-done.10.refs_1_ = bf16[4,128,1024]{2,1,0:T(8,128)(2,1)S(1)} collective-permute-done((bf16[4,128,1024]{2,1,0:T(8,128)(2,1)S(1)}, bf16[4,128,1024]{2,1,0:T(8,128)(2,1)S(1)}, u32[]{:S(2)}, u32[]{:S(2)}) %collective-permute-start.10) | collective-permute-done | bytes 1048608 | tf_op jit(solution)/shard_map/ppermute | solution.py:193
  170.9 3.2 %collective-permute-done.9.refs_0_ = bf16[4,128,1024]{2,1,0:T(8,128)(2,1)S(1)} collective-permute-done((bf16[4,128,1024]{2,1,0:T(8,128)(2,1)S(1)}, bf16[4,128,1024]{2,1,0:T(8,128)(2,1)S(1)}, u32[]{:S(2)}, u32[]{:S(2)}) %collective-permute-start.9) | collective-permute-done | bytes 1048608 | tf_op jit(solution)/shard_map/ppermute | solution.py:193
  174.2 1.3 projection.3
  175.4 1.2 collective-permute-start.11
  176.6 1.5 collective-permute-done.11.refs_4_
  178.2 0.1 fusion.1
  178.2 1.4 collective-permute-start.12
  179.7 6.2 %collective-permute-done.12.refs_5_ = bf16[128,1024]{1,0:T(8,128)(2,1)S(1)} collective-permute-done((bf16[128,1024]{1,0:T(8,128)(2,1)S(1)}, bf16[128,1024]{1,0:T(8,128)(2,1)S(1)}, u32[]{:S(2)}, u32[]{:S(2)}) %collective-permute-start.12) | collective-permute-done | bytes 262176 | tf_op jit(solution)/shard_map/ppermute | solution.py:265
  185.9 1.3 finish.1
Async XLA Ops:
  6.5 13.5 %copy-start.1 = (bf16[128,4096]{1,0:T(8,128)(2,1)S(1)}, bf16[128,4096]{1,0:T(8,128)(2,1)}, u32[]{:S(2)}) copy-start(bf16[128,4096]{1,0:T(8,128)(2,1)} %param.5) | copy-start | bytes 3145732
  6.5 75.8 %all-gather.3.cloned.1.call-start = ((), (), s32[]{:S(2)}) async-start(), calls=%async_computation.3 | async-start | bytes 2359296 | tf_op jit(solution)/shard_map/all_gather | solution.py:203
  7.6 2.6 %collective-permute-start = (bf16[128,1024]{1,0:T(8,128)(2,1)S(1)}, bf16[128,1024]{1,0:T(8,128)(2,1)S(1)}, u32[]{:S(2)}, u32[]{:S(2)}) collective-permute-start(bf16[128,1024]{1,0:T(8,128)(2,1)S(1)} %dynamic_slice.3), channel_id=1, source_target_pairs={{0,0},{1,32},{32,1},{33,33},{2,2},{3,34},{34,3},{35,35},{4,4},{5,3... | collective-permute-start | bytes 786440 | tf_op jit(solution)/shard_map/ppermute | solution.py:200
  10.2 0.7 copy-start.2
  11.0 28.4 %all-to-all-start.1 = ((bf16[8,144,256]{2,1,0:T(8,128)(2,1)}), bf16[8,144,256]{2,1,0:T(8,128)(2,1)S(1)}, u32[]{:S(2)}, u32[]{:S(2)}) async-start(bf16[8,144,256]{2,1,0:T(8,128)(2,1)} %pack_kv.1), calls=%async_computation.1 | async-start | bytes 1179648 | tf_op jit(solution)/shard_map/all_to_all | solution.py:202
  39.4 43.0 %all-to-all-start = ((bf16[8,128,512]{2,1,0:T(8,128)(2,1)}), bf16[8,128,512]{2,1,0:T(8,128)(2,1)S(1)}, u32[]{:S(2)}, u32[]{:S(2)}) async-start(bf16[8,128,512]{2,1,0:T(8,128)(2,1)} %bitcast.1), calls=%async_computation | async-start | bytes 2097152 | tf_op jit(solution)/shard_map/all_to_all | solution.py:214
  43.0 19.8 %collective-permute-start.1 = (bf16[8,144,256]{2,1,0:T(8,128)(2,1)S(1)}, bf16[8,144,256]{2,1,0:T(8,128)(2,1)S(1)}, u32[]{:S(2)}, u32[]{:S(2)}) collective-permute-start(bf16[8,144,256]{2,1,0:T(8,128)(2,1)S(1)} %all-to-all-done.1.own_ref), channel_id=1, source_target_pairs={{0,1},{1,0},{2,3},{3,2},{4,5},{5,4},{6,7},{7,6},{8,9},{9,8},{10,11... | collective-permute-start | bytes 1769480 | tf_op jit(solution)/shard_map/ppermute | solution.py:204
  52.9 32.1 %collective-permute-start.2 = (bf16[8,144,256]{2,1,0:T(8,128)(2,1)S(1)}, bf16[8,144,256]{2,1,0:T(8,128)(2,1)S(1)}, u32[]{:S(2)}, u32[]{:S(2)}) collective-permute-start(bf16[8,144,256]{2,1,0:T(8,128)(2,1)S(1)} %all-to-all-done.1.own_ref), channel_id=1, source_target_pairs={{0,16},{16,32},{32,48},{48,64},{64,80},{80,96},{96,112},{112,128},... | collective-permute-start | bytes 1769480 | tf_op jit(solution)/shard_map/ppermute | solution.py:205
  56.9 28.2 %collective-permute-start.3 = (bf16[8,144,256]{2,1,0:T(8,128)(2,1)S(1)}, bf16[8,144,256]{2,1,0:T(8,128)(2,1)S(1)}, u32[]{:S(2)}, u32[]{:S(2)}) collective-permute-start(bf16[8,144,256]{2,1,0:T(8,128)(2,1)S(1)} %all-to-all-done.1.own_ref), channel_id=1, source_target_pairs={{16,33},{17,32},{48,65},{49,64},{80,97},{81,96},{112,129},{113,128... | collective-permute-start | bytes 1769480 | tf_op jit(solution)/shard_map/ppermute | solution.py:206
  62.8 22.3 %collective-permute-start.4 = (bf16[8,144,256]{2,1,0:T(8,128)(2,1)S(1)}, bf16[8,144,256]{2,1,0:T(8,128)(2,1)}, u32[]{:S(2)}, u32[]{:S(2)}) collective-permute-start(bf16[8,144,256]{2,1,0:T(8,128)(2,1)S(1)} %collective-permute-done.1.oth_ref), channel_id=1, source_target_pairs={{0,16},{1,17},{2,18},{3,19},{4,20},{5,21},{6,22},{7,23},{8,24},{9,... | collective-permute-start | bytes 1769480 | tf_op jit(solution)/shard_map/ppermute | solution.py:211
  82.4 54.5 %collective-permute-start.5 = (bf16[8,128,1024]{2,1,0:T(8,128)(2,1)}, bf16[8,128,1024]{2,1,0:T(8,128)(2,1)S(1)}, u32[]{:S(2)}, u32[]{:S(2)}) collective-permute-start(bf16[8,128,1024]{2,1,0:T(8,128)(2,1)} %bitcast.14), channel_id=1, source_target_pairs={{0,64},{64,128},{128,192},{192,0},{1,65},{65,129},{129,193},{193,1... | collective-permute-start | bytes 6291464 | tf_op jit(solution)/shard_map/ppermute | solution.py:193
  83.5 53.4 %collective-permute-start.6 = (bf16[8,128,1024]{2,1,0:T(8,128)(2,1)}, bf16[8,128,1024]{2,1,0:T(8,128)(2,1)S(1)}, u32[]{:S(2)}, u32[]{:S(2)}) collective-permute-start(bf16[8,128,1024]{2,1,0:T(8,128)(2,1)} %bitcast.15), channel_id=1, source_target_pairs={{0,192},{64,0},{128,64},{192,128},{1,193},{65,1},{129,65},{193,129... | collective-permute-start | bytes 6291464 | tf_op jit(solution)/shard_map/ppermute | solution.py:193
  96.8 40.1 %copy-start = (bf16[1024,1024]{1,0:T(8,128)(2,1)S(1)}, bf16[1024,1024]{1,0:T(8,128)(2,1)}, u32[]{:S(2)}) copy-start(bf16[1024,1024]{1,0:T(8,128)(2,1)} %all-gather.3.cloned.1.call-done) | copy-start | bytes 6291460
  140.4 8.2 %collective-permute-start.7 = (bf16[2,128,3072]{2,1,0:T(8,128)(2,1)S(1)}, bf16[2,128,3072]{2,1,0:T(8,128)(2,1)S(1)}, u32[]{:S(2)}, u32[]{:S(2)}) collective-permute-start(bf16[2,128,3072]{2,1,0:T(8,128)(2,1)S(1)} %get-tuple-element.22), channel_id=1, source_target_pairs={{0,16},{16,0},{1,17},{17,1},{2,18},{18,2},{3,19},{19,3},{4,20},{20... | collective-permute-start | bytes 4718600 | tf_op jit(solution)/shard_map/ppermute | solution.py:263
  141.4 29.5 %collective-permute-start.10 = (bf16[4,128,1024]{2,1,0:T(8,128)(2,1)S(1)}, bf16[4,128,1024]{2,1,0:T(8,128)(2,1)S(1)}, u32[]{:S(2)}, u32[]{:S(2)}) collective-permute-start(bf16[4,128,1024]{2,1,0:T(8,128)(2,1)S(1)} %slice.18), channel_id=1, source_target_pairs={{0,192},{64,0},{128,64},{192,128},{1,193},{65,1},{129,65},{193,129... | collective-permute-start | bytes 3145736 | tf_op jit(solution)/shard_map/ppermute | solution.py:193
  148.4 25.7 %collective-permute-start.9 = (bf16[4,128,1024]{2,1,0:T(8,128)(2,1)S(1)}, bf16[4,128,1024]{2,1,0:T(8,128)(2,1)S(1)}, u32[]{:S(2)}, u32[]{:S(2)}) collective-permute-start(bf16[4,128,1024]{2,1,0:T(8,128)(2,1)S(1)} %slice.17), channel_id=1, source_target_pairs={{0,64},{64,128},{128,192},{192,0},{1,65},{65,129},{129,193},{193,1... | collective-permute-start | bytes 3145736 | tf_op jit(solution)/shard_map/ppermute | solution.py:193
  148.7 19.1 %collective-permute-start.8 = (bf16[128,3072]{1,0:T(8,128)(2,1)S(1)}, bf16[128,3072]{1,0:T(8,128)(2,1)S(1)}, u32[]{:S(2)}, u32[]{:S(2)}) collective-permute-start(bf16[128,3072]{1,0:T(8,128)(2,1)S(1)} %fusion), channel_id=1, source_target_pairs={{0,32},{32,0},{1,33},{33,1},{2,34},{34,2},{3,35},{35,3},{4,36},{36... | collective-permute-start | bytes 2359304 | tf_op jit(solution)/shard_map/ppermute | solution.py:248
  175.4 2.7 %collective-permute-start.11 = (bf16[2,128,1024]{2,1,0:T(8,128)(2,1)S(1)}, bf16[2,128,1024]{2,1,0:T(8,128)(2,1)S(1)}, u32[]{:S(2)}, u32[]{:S(2)}) collective-permute-start(bf16[2,128,1024]{2,1,0:T(8,128)(2,1)S(1)} %get-tuple-element.27), channel_id=1, source_target_pairs={{0,16},{16,0},{1,17},{17,1},{2,18},{18,2},{3,19},{19,3},{4,20},{20... | collective-permute-start | bytes 1572872 | tf_op jit(solution)/shard_map/ppermute | solution.py:263
  178.2 7.6 %collective-permute-start.12 = (bf16[128,1024]{1,0:T(8,128)(2,1)S(1)}, bf16[128,1024]{1,0:T(8,128)(2,1)S(1)}, u32[]{:S(2)}, u32[]{:S(2)}) collective-permute-start(bf16[128,1024]{1,0:T(8,128)(2,1)S(1)} %fusion.1), channel_id=1, source_target_pairs={{0,32},{32,0},{1,33},{33,1},{2,34},{34,2},{3,35},{35,3},{4,36},{36... | collective-permute-start | bytes 786440 | tf_op jit(solution)/shard_map/ppermute | solution.py:265
Sparse Core Ops, SparseCore 0:
  11.1 69.7 all-gather.2
